TPU v7x, 32 devices: a whole 2x2x4 slice. The times are simulated.
32 devices in a mesh: groups: 2 (over y), gx: 4 (over x, core), gy: 4 (over z).
Axes of the slice: x: 2, y: 2, z: 4, core: 2. Of those that a mesh axis runs over, the one named last changes fastest.
Arguments:
- layer_input: bfloat16 [256, 16384], P(('groups', 'gx'), 'gy'), parts along dimension 0, may hold values from -32 to 32, as said below
- attn_context: bfloat16 [256, 8192], P(('groups', 'gx'), 'gy'), parts along dimension 0, may hold values from -6 to 6
- ffn_hidden: bfloat16 [256, 26624], P(('groups', 'gx'), 'gy'), parts along dimension 0, may hold values from -6 to 6
- norm_gain: float32 [16384], replicated, may hold values from 0.1 to 1.9
- w_query: bfloat16 [16384, 8192], P('gx', 'gy'), may hold values from -0.046875 to 0.046875
- w_keyval: bfloat16 [16384, 1024], P('gx', 'gy'), may hold values from -0.046875 to 0.046875
- w_out: bfloat16 [8192, 16384], P('gx', 'gy'), may hold values from -0.0625 to 0.0625
- w_down: bfloat16 [26624, 16384], P('gx', 'gy'), may hold values from -0.0390625 to 0.0390625
Outputs:
- queries: bfloat16 [256, 8192], P(('groups', 'gx'), 'gy'), parts along dimension 0
- keys_values: bfloat16 [256, 1024], P(('groups', 'gx'), 'gy'), parts along dimension 0
- block_output: bfloat16 [256, 16384], P(('groups', 'gx'), 'gy'), parts along dimension 0
There are 2 independent parts, one for each index of `groups`. A program takes and returns all parts, laid end to end along the dimension named above; an argument that names none is the same for every part. Nothing has to cross between parts.
Inputs may be any that keep to these rules, and one draw needn't show every extreme that they name: `layer_input`: the layer's input.
All inputs are finite; a program needn't handle non-finite values.
Results may differ from a plain program's by a relative error of at most 0.005.
Values may be sent and summed in bfloat16 or wider, within the bound.
No kernel may reach another device: no remote copies, remote signals or barrier semaphores. Data moves between devices by JAX's collectives and lax.ppermute only.
A program may use at most 192 MiB of HBM per device.

v0:
```python
import jax
import jax.numpy as jnp
from jax import lax
from jax.sharding import PartitionSpec as P

norm_epsilon = 1e-05


def local(layer_input, attn_context, ffn_hidden, norm_gain, w_query, w_keyval, w_out, w_down):
    feat_width = layer_input.shape[1]
    model_width = norm_gain.shape[0]
    input_float = layer_input.astype(jnp.float32)
    row_sums = jnp.sum(input_float * input_float, axis=1)
    summed = lax.psum(row_sums, "gy")
    scale_rows = lax.rsqrt(summed / model_width + norm_epsilon)
    gain_slice = lax.dynamic_slice_in_dim(norm_gain, lax.axis_index("gy") * feat_width, feat_width)
    normed = (input_float * scale_rows[:, None] * gain_slice).astype(jnp.bfloat16)
    wide_input, wide_context, wide_hidden = (
        lax.all_gather(normed, "gy", axis=1, tiled=True),
        lax.all_gather(attn_context, "gy", axis=1, tiled=True),
        lax.all_gather(ffn_hidden, "gy", axis=1, tiled=True),
    )
    column_input, column_context, column_hidden = (
        lax.all_to_all(wide_input, "gx", split_axis=1, concat_axis=0, tiled=True),
        lax.all_to_all(wide_context, "gx", split_axis=1, concat_axis=0, tiled=True),
        lax.all_to_all(wide_hidden, "gx", split_axis=1, concat_axis=0, tiled=True),
    )
    row_block = column_input
    query_part = jnp.dot(row_block, w_query, preferred_element_type=jnp.float32)
    keyval_part = jnp.dot(row_block, w_keyval, preferred_element_type=jnp.float32)
    heads_summed = lax.psum_scatter(
        jnp.concatenate([query_part, keyval_part], axis=1), "gx", scatter_dimension=0, tiled=True
    )
    query_cols = w_query.shape[1]
    queries = heads_summed[:, :query_cols].astype(jnp.bfloat16)
    keys_values = heads_summed[:, query_cols:].astype(jnp.bfloat16)
    row_block = column_context
    attn_sum = lax.psum_scatter(
        jnp.dot(row_block, w_out, preferred_element_type=jnp.float32),
        "gx",
        scatter_dimension=0,
        tiled=True,
    )
    row_block = column_hidden
    ffn_sum = lax.psum_scatter(
        jnp.dot(row_block, w_down, preferred_element_type=jnp.float32),
        "gx",
        scatter_dimension=0,
        tiled=True,
    )
    block_float = input_float + attn_sum + ffn_sum
    return (queries, keys_values, block_float.astype(jnp.bfloat16))


def solution(mesh):
    return jax.shard_map(
        local,
        mesh=mesh,
        in_specs=(
            P(("groups", "gx"), "gy"),
            P(("groups", "gx"), "gy"),
            P(("groups", "gx"), "gy"),
            P(),
            P("gx", "gy"),
            P("gx", "gy"),
            P("gx", "gy"),
            P("gx", "gy"),
        ),
        out_specs=(P(("groups", "gx"), "gy"), P(("groups", "gx"), "gy"), P(("groups", "gx"), "gy")),
        check_vma=False,
    )
```

profile of v0, /device:TPU:0, one launch (start us, length us, event | category | flops | bytes accessed | tf_op | source)
XLA Modules:
  0.0 232.6 jit_solution(13742974537355467096)
XLA Ops:
  8.0 0.0 copy-start
  8.0 0.0 all-gather.5.cloned.1.call-start
  8.1 0.7 all-gather.5.cloned.1.call-update
  8.7 0.0 reduce-scatter.6.cloned.1.call-start
  8.8 19.4 %all_gather.10 = bf16[32,8192]{1,0:T(8,128)(2,1)S(1)} all-gather(bf16[32,2048]{1,0:T(8,128)(2,1)} %param.9), channel_id=1, replica_groups=mesh['groups'=2,'gx'=4,'gy'=4] {'gy'}, dimensions={1}, use_global_device_ids=true | all-gather | bytes 655360 | tf_op jit(solution)/shard_map/all_gather | solution.py:20
  28.2 11.3 %all_to_all.57 = bf16[32,4,2048]{2,0,1:T(8,128)(2,1)S(1)} all-to-all(bf16[32,4,2048]{2,0,1:T(8,128)(2,1)S(1)} %bitcast.36), channel_id=1, replica_groups=mesh['groups'=2,'gx'=4,'gy'=4] {'gx'}, dimensions={1} | all-to-all | bytes 1048576 | tf_op jit(solution)/shard_map/all_to_all | solution.py:25
  39.5 9.5 %fusion.7 = f32[128,4096]{1,0:T(8,128)} fusion(bf16[128,2048]{1,0:T(8,128)(2,1)S(1)} %bitcast.34, bf16[2048,4096]{1,0:T(8,128)(2,1)} %param.14), kind=kOutput, calls=%fused_computation.15 | convolution fusion | flops 2147483648 | bytes 19398656 | tf_op jit(solution)/shard_map/dot_general | solution.py:39
  49.1 0.0 reduce-scatter.6.cloned.1.call-update
  49.1 0.0 reduce-scatter.8.cloned.1.call-start
  49.2 5.1 %all-gather.5.cloned.1.call-done = bf16[32,26624]{1,0:T(8,128)(2,1)} async-done(((bf16[32,6656]{1,0:T(8,128)(2,1)}), bf16[32,26624]{1,0:T(8,128)(2,1)}) %all-gather.5.cloned.1.call-update) | async-done | bytes 1703952 | tf_op jit(solution)/shard_map/all_gather | solution.py:21
  54.3 1.8 copy.24
  56.1 35.1 %all_to_all.58 = bf16[32,4,6656]{2,0,1:T(8,128)(2,1)S(1)} all-to-all(bf16[32,4,6656]{2,0,1:T(8,128)(2,1)S(1)} %bitcast.32), channel_id=1, replica_groups=mesh['groups'=2,'gx'=4,'gy'=4] {'gx'}, dimensions={1} | all-to-all | bytes 3407872 | tf_op jit(solution)/shard_map/all_to_all | solution.py:26
  91.3 20.5 %fusion.8 = f32[128,4096]{1,0:T(8,128)} fusion(bf16[128,6656]{1,0:T(8,128)(2,1)S(1)} %bitcast.31, bf16[6656,4096]{1,0:T(8,128)(2,1)} %param.15), kind=kOutput, calls=%fused_computation.16 | convolution fusion | flops 6979321856 | bytes 58327040 | tf_op jit(solution)/shard_map/dot_general | solution.py:46
  111.7 0.0 copy-start.1
  111.7 0.0 reduce-scatter.8.cloned.1.call-update
  111.8 0.0 all-gather.3.cloned.1.call-start
  111.8 0.7 dynamic_slice.3
  112.5 0.1 copy-done.1
  112.7 0.2 fusion
  112.9 8.4 %psum.7 = f32[32]{0:T(128)S(1)} all-reduce(f32[32]{0:T(128)S(1)} %fusion), channel_id=1, replica_groups=mesh['groups'=2,'gx'=4,'gy'=4] {'gy'}, use_global_device_ids=true, to_apply=%region_1.0 | all-reduce | flops 32 | bytes 256 | tf_op jit(solution)/shard_map/psum | solution.py:14
  121.2 0.0 reduce-scatter.6.cloned.1.call-done
  121.2 18.9 %reduce-scatter.8.cloned.1.call-done = f32[32,4096]{1,0:T(8,128)} async-done(((f32[128,4096]{1,0:T(8,128)}), f32[32,4096]{1,0:T(8,128)}) %reduce-scatter.8.cloned.1.call-update) | async-done | bytes 524304 | tf_op jit(solution)/shard_map/reduce_scatter | solution.py:45
  140.2 2.1 fusion.4
  142.3 0.0 all-gather.3.cloned.1.call-update
  142.3 0.0 reduce-scatter.4.cloned.1.call-start
  142.3 28.0 %all-gather.3.cloned.1.call-done = bf16[32,16384]{1,0:T(8,128)(2,1)} async-done(((bf16[32,4096]{1,0:T(8,128)(2,1)}), bf16[32,16384]{1,0:T(8,128)(2,1)}) %all-gather.3.cloned.1.call-update) | async-done | bytes 1048592 | tf_op jit(solution)/shard_map/all_gather | solution.py:19
  170.4 1.3 copy.25
  171.7 17.0 %all_to_all.59 = bf16[32,4,4096]{2,0,1:T(8,128)(2,1)S(1)} all-to-all(bf16[32,4,4096]{2,0,1:T(8,128)(2,1)S(1)} %bitcast.33), channel_id=1, replica_groups=mesh['groups'=2,'gx'=4,'gy'=4] {'gx'}, dimensions={1} | all-to-all | bytes 2097152 | tf_op jit(solution)/shard_map/all_to_all | solution.py:24
  188.7 0.0 copy-done
  188.7 0.5 fusion.6
  189.2 8.2 %fusion.5 = f32[128,2048]{1,0:T(8,128)S(1)} fusion(bf16[128,4096]{1,0:T(8,128)(2,1)S(1)} %bitcast.30, bf16[4096,2048]{1,0:T(8,128)(2,1)} %param.12), kind=kOutput, calls=%fused_computation.13 | convolution fusion | flops 2147483648 | bytes 18874368 | tf_op jit(solution)/shard_map/dot_general | solution.py:29
  197.4 1.1 pad_maximum_fusion
  198.5 0.0 reduce-scatter.4.cloned.1.call-update
  198.5 24.3 %reduce-scatter.4.cloned.1.call-done = f32[32,2304]{1,0:T(8,128)} async-done(((f32[128,2304]{1,0:T(8,128)}), f32[32,2304]{1,0:T(8,128)}) %reduce-scatter.4.cloned.1.call-update) | async-done | bytes 294928 | tf_op jit(solution)/shard_map/reduce_scatter | solution.py:31
  222.8 1.0 convert.4
  223.8 0.7 slice.10
  224.4 0.6 slice.11
  (2 shorter events, 0.1 us)
Async XLA Ops:
  8.0 180.7 %copy-start = (bf16[4096,256]{1,0:T(8,128)(2,1)S(1)}, bf16[4096,256]{1,0:T(8,128)(2,1)}, u32[]{:S(2)}) copy-start(bf16[4096,256]{1,0:T(8,128)(2,1)} %param.13) | copy-start | bytes 6291460
  8.0 46.3 %all-gather.5.cloned.1.call-start = ((), (), s32[]{:S(2)}) async-start(), calls=%async_computation.9 | async-start | bytes 2129920 | tf_op jit(solution)/shard_map/all_gather | solution.py:21
  8.7 112.5 %reduce-scatter.6.cloned.1.call-start = ((), (), s32[]{:S(2)}) async-start(), calls=%async_computation.8 | async-start | bytes 2621440 | tf_op jit(solution)/shard_map/reduce_scatter | solution.py:38
  49.1 91.1 %reduce-scatter.8.cloned.1.call-start = ((), (), s32[]{:S(2)}) async-start(), calls=%async_computation.10 | async-start | bytes 2621440 | tf_op jit(solution)/shard_map/reduce_scatter | solution.py:45
  111.7 0.9 copy-start.1
  111.8 58.6 %all-gather.3.cloned.1.call-start = ((), (), s32[]{:S(2)}) async-start(), calls=%async_computation.6 | async-start | bytes 1310720 | tf_op jit(solution)/shard_map/all_gather | solution.py:19
  142.3 80.5 %reduce-scatter.4.cloned.1.call-start = ((), (), s32[]{:S(2)}) async-start(), calls=%async_computation.7 | async-start | bytes 1474560 | tf_op jit(solution)/shard_map/reduce_scatter | solution.py:31
Sparse Core Ops, SparseCore 0:
  10.5 43.7 all-gather.4
  142.4 27.9 all-gather.2
Sparse Core Ops, SparseCore 1:
  49.2 43.1 reduce-scatter.5
  111.8 28.3 reduce-scatter.7
  198.6 24.2 reduce-scatter.3
where the time goes:
time: 233 us
  blocking collectives  91.2 us (39%)
  waiting for transfers between devices  77.2 us (33%)
  matrix products  38.7 us (17%)
  between operations  15.7 us (7%)
  local copies, waits for them, and re-layouts  5.32 us (2%)
  other arithmetic  4.32 us (2%)
    all_to_all x1, blocking collectives, local(): lax.all_to_all(wide_hidden, 'gx', split_axis=1, concat_axis=0, tiled=True)  35.1 us
    all_gather x1, waiting for transfers between devices, local(): lax.all_gather(normed, 'gy', axis=1, tiled=True)  28 us
    reduce_scatter x1, waiting for transfers between devices, local(): lax.psum_scatter(jnp.concatenate([query_part, keyval_part], axis=1), 'gx'...  24.3 us
    dot_general x1, matrix products, local(): jnp.dot(row_block, w_down, preferred_element_type=jnp.float32)  20.5 us
    all_gather x1, blocking collectives, local(): lax.all_gather(attn_context, 'gy', axis=1, tiled=True)  19.4 us
    reduce_scatter x1, waiting for transfers between devices, local(): lax.psum_scatter(jnp.dot(row_block, w_down, preferred_element_type=jnp.fl...  18.9 us
    all_to_all x1, blocking collectives, local(): lax.all_to_all(wide_input, 'gx', split_axis=1, concat_axis=0, tiled=True)  17 us
    all_to_all x1, blocking collectives, local(): lax.all_to_all(wide_context, 'gx', split_axis=1, concat_axis=0, tiled=True)  11.3 us
  transfers between devices with their start and end apart: 5, of which 4 were waited for; matrix products, arithmetic and copies ran while one was open for 14% of the time, Pallas kernels for 0%

commit v1 on v0

v1 whole, which is shorter than its diff:
```python
import jax
import jax.numpy as jnp
from jax import lax
from jax.sharding import PartitionSpec as P

norm_epsilon = 1e-05


def solution(mesh):
    nx, ny = mesh.shape["gx"], mesh.shape["gy"]
    ratio = nx // ny
    assert nx == ratio * ny

    def routes(shift, turn):
        pairs = []
        for gx in range(nx):
            for gy in range(ny):
                piece = (turn + gx) % ratio
                target = (gy * ratio + piece, (gx // ratio + shift) % ny)
                pairs.append((gx * ny + gy, target[0] * ny + target[1]))
        return pairs

    steps = [(shift, turn, routes(shift, turn)) for shift in range(ny) for turn in range(ratio)]

    def spread(block):
        gx = lax.axis_index("gx")
        width = block.shape[1] // ratio
        parts = []
        for shift, turn, pairs in steps:
            piece = block
            if ratio > 1:
                piece = lax.dynamic_slice_in_dim(block, (turn + gx) % ratio * width, width, axis=1)
            parts.append(lax.ppermute(piece, ("gx", "gy"), pairs))
        return jnp.concatenate(parts, axis=0)

    def row_block_of(step):
        shift, turn, _ = steps[step]
        gx, gy = lax.axis_index("gx"), lax.axis_index("gy")
        return (gy - shift) % ny * ratio + (gx % ratio - turn) % ratio

    def step_of(owner):
        gx, gy = lax.axis_index("gx"), lax.axis_index("gy")
        return (gy - owner // ratio) % ny * ratio + (gx % ratio - owner % ratio) % ratio

    def sum_over_gx(partial, rows):
        gx = lax.axis_index("gx")

        def rows_of(owner):
            return lax.dynamic_slice_in_dim(partial, step_of(owner) * rows, rows, axis=0)

        total = rows_of(gx)
        for hop in range(1, nx):
            pairs = [(i, (i + hop) % nx) for i in range(nx)]
            sent = rows_of((gx + hop) % nx).astype(jnp.bfloat16)
            total = total + lax.ppermute(sent, "gx", pairs).astype(jnp.float32)
        return total

    def local(layer_input, attn_context, ffn_hidden, norm_gain, w_query, w_keyval, w_out, w_down):
        rows = layer_input.shape[0]
        model_width = norm_gain.shape[0]
        depth = w_query.shape[0]
        gx = lax.axis_index("gx")

        input_float = layer_input.astype(jnp.float32)
        row_sums = jnp.sum(input_float * input_float, axis=1)
        all_sums = lax.all_gather(row_sums, ("gx", "gy"), axis=0, tiled=False)
        all_sums = jnp.sum(all_sums.reshape(nx, ny, rows), axis=1)

        column_context = spread(attn_context)
        column_hidden = spread(ffn_hidden)
        column_input = spread(layer_input)

        block_part = jnp.dot(column_context, w_out, preferred_element_type=jnp.float32)
        block_part = block_part + jnp.dot(column_hidden, w_down, preferred_element_type=jnp.float32)
        block_sum = sum_over_gx(block_part, rows)

        order = jnp.stack([row_block_of(step) for step in range(len(steps))])
        mean_square = jnp.take(all_sums, order, axis=0).reshape(nx * rows, 1) / model_width
        gain = lax.dynamic_slice_in_dim(norm_gain, gx * depth, depth)
        normed = (column_input.astype(jnp.float32) * lax.rsqrt(mean_square + norm_epsilon) * gain).astype(jnp.bfloat16)
        query_part = jnp.dot(normed, w_query, preferred_element_type=jnp.float32)
        keyval_part = jnp.dot(normed, w_keyval, preferred_element_type=jnp.float32)
        queries = sum_over_gx(query_part, rows).astype(jnp.bfloat16)
        keys_values = sum_over_gx(keyval_part, rows).astype(jnp.bfloat16)
        return (queries, keys_values, (input_float + block_sum).astype(jnp.bfloat16))

    return jax.shard_map(
        local,
        mesh=mesh,
        in_specs=(
            P(("groups", "gx"), "gy"),
            P(("groups", "gx"), "gy"),
            P(("groups", "gx"), "gy"),
            P(),
            P("gx", "gy"),
            P("gx", "gy"),
            P("gx", "gy"),
            P("gx", "gy"),
        ),
        out_specs=(P(("groups", "gx"), "gy"), P(("groups", "gx"), "gy"), P(("groups", "gx"), "gy")),
        check_vma=False,
    )
```

time: 233 us -> 162 us (0.70)
  waiting for transfers between devices: 77.2 us -> 8.74 us
  starting transfers between devices: 0.21 us -> 67.4 us
  blocking collectives: 91.2 us -> 36.8 us
  between operations: 15.7 us -> 1.46 us
    ppermute x0 -> x21, starting transfers between devices: none -> 67.4 us  [the longest x12 57.1 us: spread(): parts.append(lax.ppermute(piece, ('gx', 'gy'), pairs))]
    all_to_all x3 -> x0, blocking collectives: 63.4 us -> none  [the longest x1 35.1 us: local(): lax.all_to_all(wide_hidden, 'gx', split_axis=1, concat_axis=0, tiled=True)]
    reduce_scatter x3 -> x0, waiting for transfers between devices: 43.3 us -> none  [the longest x1 24.3 us: local(): lax.psum_scatter(jnp.concatenate([query_part, keyval_part], axis=1), 'gx'...]
    unnamed x0 -> x1, blocking collectives: none -> 36.8 us
    all_gather x2 -> x0, waiting for transfers between devices: 33.2 us -> none  [the longest x1 28 us: local(): lax.all_gather(normed, 'gy', axis=1, tiled=True)]
    all_gather x1 -> x0, blocking collectives: 19.4 us -> none  [local(): lax.all_gather(attn_context, 'gy', axis=1, tiled=True)]
    ppermute x0 -> x21, waiting for transfers between devices: none -> 8.74 us  [the longest x9 5.18 us: sum_over_gx(): total = total + lax.ppermute(sent, 'gx', pairs).astype(jnp.float32)]
    psum x1 -> x0, blocking collectives: 8.36 us -> none  [local(): summed = lax.psum(row_sums, 'gy')]
  transfers between devices with their start and end apart: 5 -> 21, of which waited for: 4 -> 5; matrix products, arithmetic and copies ran while one was open for 14% -> 26% of each run, Pallas kernels for 0% -> 0%
where the time goes in v1:
time: 162 us; the launch traced here: 161 us
  starting transfers between devices  67.4 us (42%)
  matrix products  38.2 us (24%)
  blocking collectives  36.8 us (23%)
  waiting for transfers between devices  8.74 us (5%)
  local copies, waits for them, and re-layouts  4.5 us (3%)
  other arithmetic  3.72 us (2%)
    ppermute x12, starting transfers between devices, spread(): parts.append(lax.ppermute(piece, ('gx', 'gy'), pairs))  57.1 us
    unnamed x1, blocking collectives  36.8 us
    dot_general x1, matrix products, local(): jnp.dot(column_hidden, w_down, preferred_element_type=jnp.float32)  19.7 us
    ppermute x9, starting transfers between devices, sum_over_gx(): total = total + lax.ppermute(sent, 'gx', pairs).astype(jnp.float32)  10.3 us
    dot_general x1, matrix products, local(): query_part = jnp.dot(normed, w_query, preferred_element_type=jnp.float32)  8.49 us
    dot_general x1, matrix products, local(): jnp.dot(column_context, w_out, preferred_element_type=jnp.float32)  8.28 us
    ppermute x9, waiting for transfers between devices, sum_over_gx(): total = total + lax.ppermute(sent, 'gx', pairs).astype(jnp.float32)  5.18 us
    ppermute x12, waiting for transfers between devices, spread(): parts.append(lax.ppermute(piece, ('gx', 'gy'), pairs))  3.55 us
  transfers between devices with their start and end apart: 21, of which 5 were waited for; matrix products, arithmetic and copies ran while one was open for 26% of the time, Pallas kernels for 0%

profile of v1, /device:TPU:0, one launch (start us, length us, event | category | flops | bytes accessed | tf_op | source)
XLA Modules:
  0.0 160.9 jit_solution(7726494628073961537)
XLA Ops:
  0.6 0.0 copy-start
  0.6 1.8 %collective-permute-start.14 = (bf16[32,6656]{1,0:T(8,128)(2,1)}, bf16[32,6656]{1,0:T(8,128)(2,1)S(1)}, u32[]{:S(2)}, u32[]{:S(2)}) collective-permute-start(bf16[32,6656]{1,0:T(8,128)(2,1)} %param.10), channel_id=1, source_target_pairs={{0,0},{1,4},{2,8},{3,12},{4,1},{5,5},{6,9},{7,13},{8,2},{9,6},{10,... | collective-permute-start | bytes 1277960 | tf_op jit(solution)/shard_map/ppermute | solution.py:33
  2.4 3.3 %collective-permute-start.15 = (bf16[32,6656]{1,0:T(8,128)(2,1)}, bf16[32,6656]{1,0:T(8,128)(2,1)S(1)}, u32[]{:S(2)}, u32[]{:S(2)}) collective-permute-start(bf16[32,6656]{1,0:T(8,128)(2,1)} %param.10), channel_id=1, source_target_pairs={{0,1},{1,5},{2,9},{3,13},{4,2},{5,6},{6,10},{7,14},{8,3},{9,7},{10... | collective-permute-start | bytes 1277960 | tf_op jit(solution)/shard_map/ppermute | solution.py:33
  5.8 3.4 %collective-permute-start.16 = (bf16[32,6656]{1,0:T(8,128)(2,1)}, bf16[32,6656]{1,0:T(8,128)(2,1)S(1)}, u32[]{:S(2)}, u32[]{:S(2)}) collective-permute-start(bf16[32,6656]{1,0:T(8,128)(2,1)} %param.10), channel_id=1, source_target_pairs={{0,2},{1,6},{2,10},{3,14},{4,3},{5,7},{6,11},{7,15},{8,0},{9,4},{1... | collective-permute-start | bytes 1277960 | tf_op jit(solution)/shard_map/ppermute | solution.py:33
  9.2 2.6 %collective-permute-start.17 = (bf16[32,6656]{1,0:T(8,128)(2,1)}, bf16[32,6656]{1,0:T(8,128)(2,1)}, u32[]{:S(2)}, u32[]{:S(2)}) collective-permute-start(bf16[32,6656]{1,0:T(8,128)(2,1)} %param.10), channel_id=1, source_target_pairs={{0,3},{1,7},{2,11},{3,15},{4,0},{5,4},{6,8},{7,12},{8,1},{9,5},{10... | collective-permute-start | bytes 1277960 | tf_op jit(solution)/shard_map/ppermute | solution.py:33
  11.8 1.6 collective-permute-start.10
  13.3 0.0 collective-permute-done.14
  13.4 4.0 %collective-permute-start.11 = (bf16[32,2048]{1,0:T(8,128)(2,1)}, bf16[32,2048]{1,0:T(8,128)(2,1)S(1)}, u32[]{:S(2)}, u32[]{:S(2)}) collective-permute-start(bf16[32,2048]{1,0:T(8,128)(2,1)} %param.9), channel_id=1, source_target_pairs={{0,1},{1,5},{2,9},{3,13},{4,2},{5,6},{6,10},{7,14},{8,3},{9,7},{10... | collective-permute-start | bytes 393224 | tf_op jit(solution)/shard_map/ppermute | solution.py:33
  17.4 3.5 %collective-permute-done.15 = bf16[32,6656]{1,0:T(8,128)(2,1)S(1)} collective-permute-done((bf16[32,6656]{1,0:T(8,128)(2,1)}, bf16[32,6656]{1,0:T(8,128)(2,1)S(1)}, u32[]{:S(2)}, u32[]{:S(2)}) %collective-permute-start.15) | collective-permute-done | bytes 426016 | tf_op jit(solution)/shard_map/ppermute | solution.py:33
  20.9 29.1 %collective-permute-start.12 = (bf16[32,2048]{1,0:T(8,128)(2,1)}, bf16[32,2048]{1,0:T(8,128)(2,1)S(1)}, u32[]{:S(2)}, u32[]{:S(2)}) collective-permute-start(bf16[32,2048]{1,0:T(8,128)(2,1)} %param.9), channel_id=1, source_target_pairs={{0,2},{1,6},{2,10},{3,14},{4,3},{5,7},{6,11},{7,15},{8,0},{9,4},{1... | collective-permute-start | bytes 393224 | tf_op jit(solution)/shard_map/ppermute | solution.py:33
  50.0 3.6 %collective-permute-start = (bf16[32,4096]{1,0:T(8,128)(2,1)}, bf16[32,4096]{1,0:T(8,128)(2,1)}, u32[]{:S(2)}, u32[]{:S(2)}) collective-permute-start(bf16[32,4096]{1,0:T(8,128)(2,1)} %param.8), channel_id=1, source_target_pairs={{0,0},{1,4},{2,8},{3,12},{4,1},{5,5},{6,9},{7,13},{8,2},{9,6},{10,... | collective-permute-start | bytes 786440 | tf_op jit(solution)/shard_map/ppermute | solution.py:33
  53.6 19.7 %fusion = f32[128,4096]{1,0:T(8,128)S(1)} fusion(bf16[6656,4096]{1,0:T(8,128)(2,1)} %param.15, bf16[32,6656]{1,0:T(8,128)(2,1)} %collective-permute-done.17, bf16[32,6656]{1,0:T(8,128)(2,1)S(1)} %collective-permute-done.16, bf16[32,6656]{1,0:T(8,128)(2,1)S(1)} %collective-permute-done.15, bf16[32,6656]{1,0:T(8,128)(2,1)S(1)} %collective-permute-done.14), kind=kOutput, calls=%fused_computation.3 | convolution fusion | flops 6986137600 | bytes 58327040 | tf_op jit(solution)/shard_map/dot_general | solution.py:74
  73.4 0.0 copy-start.3
  73.4 0.5 collective-permute-start.1
  73.9 8.3 %convolution_add_fusion = f32[128,4096]{1,0:T(8,128)S(1)} fusion(f32[128,4096]{1,0:T(8,128)S(1)} %fusion, bf16[2048,4096]{1,0:T(8,128)(2,1)} %param.14, bf16[32,2048]{1,0:T(8,128)(2,1)S(1)} %collective-permute-done.13, bf16[32,2048]{1,0:T(8,128)(2,1)S(1)} %collective-permute-done.12, bf16[32,2048]{1,0:T(8,128)(2,1)S(1)} %collective-permute-done.11, ...), kind=kOutput, calls=%fused_computation.1 | convolution fusion | flops 2150105088 | bytes 21495808 | tf_op jit(solution)/shard_map/dot_general | solution.py:73
  82.2 1.3 copy-done.1
  83.5 0.8 dynamic-slice_convert_fusion.2
  84.3 1.5 collective-permute-start.18
  85.9 2.3 %collective-permute-start.19 = (bf16[32,4096]{1,0:T(8,128)(2,1)S(1)}, bf16[32,4096]{1,0:T(8,128)(2,1)S(1)}, u32[]{:S(2)}, u32[]{:S(2)}) collective-permute-start(bf16[32,4096]{1,0:T(8,128)(2,1)S(1)} %get-tuple-element.5), channel_id=1, source_target_pairs={{0,8},{4,12},{8,0},{12,4},{1,9},{5,13},{9,1},{13,5},{2,10},{6,14},... | collective-permute-start | bytes 786440 | tf_op jit(solution)/shard_map/ppermute | solution.py:55
  88.1 1.4 collective-permute-start.20
  89.6 0.1 fusion.17
  89.7 0.6 dynamic-slice
  90.9 0.7 dynamic_slice.39
  91.6 0.1 compare_and_fusion
  91.7 6.9 %collective-permute-start.2 = (bf16[32,4096]{1,0:T(8,128)(2,1)}, bf16[32,4096]{1,0:T(8,128)(2,1)}, u32[]{:S(2)}, u32[]{:S(2)}) collective-permute-start(bf16[32,4096]{1,0:T(8,128)(2,1)} %param.8), channel_id=1, source_target_pairs={{0,2},{1,6},{2,10},{3,14},{4,3},{5,7},{6,11},{7,15},{8,0},{9,4},{1... | collective-permute-start | bytes 786440 | tf_op jit(solution)/shard_map/ppermute | solution.py:33
  98.7 0.3 collective-permute-start.3
  98.9 1.1 collective-permute-done.20
  100.1 2.1 %fusion.9 = (bf16[32,4096]{1,0:T(8,128)(2,1)}, f32[32]{0:T(128)S(1)}) fusion(bf16[32,4096]{1,0:T(8,128)(2,1)} %param.8, bf16[32,4096]{1,0:T(8,128)(2,1)S(1)} %collective-permute-done.20, bf16[32,4096]{1,0:T(8,128)(2,1)S(1)} %collective-permute-done.19, bf16[32,4096]{1,0:T(8,128)(2,1)S(1)} %collective-permute-done.18, f32[128,4096]{1,0:T(8,128)} %copy-done.1, ...), kind=kLoop, calls=%fused_computation.14 | loop fusion | flops 1441760 | bytes 1835140 | tf_op jit(solution)/shard_map/convert_element_type | solution.py:85
  102.2 0.2 dynamic-update-slice
  102.4 36.8 %all-reduce = f32[512]{0:T(512)S(1)} all-reduce(f32[512]{0:T(512)S(1)} %dynamic-update-slice), channel_id=2, replica_groups=mesh['groups'=2,'gx'=4,'gy'=4] {'gx','gy'}, use_global_device_ids=true, to_apply=%add | all-reduce | flops 512 | bytes 4096
  139.2 0.1 reshape.217
  139.4 0.6 gather_fusion
  139.9 0.1 add_rsqrt_fusion
  140.0 0.1 rsqrt.12
  140.1 1.7 %fusion.20 = f32[128,256]{1,0:T(8,128)S(1)} fusion(bf16[4096,256]{1,0:T(8,128)(2,1)S(1)} %copy-done, bf16[32,4096]{1,0:T(8,128)(2,1)S(1)} %collective-permute-done.3, bf16[32,4096]{1,0:T(8,128)(2,1)} %collective-permute-done.2, bf16[32,4096]{1,0:T(8,128)(2,1)} %collective-permute-done.1, bf16[32,4096]{1,0:T(8,128)(2,1)} %collective-permute-done, ...), kind=kOutput, calls=%fused_computation.41 | convolution fusion | flops 274202624 | bytes 3293696 | tf_op jit(solution)/shard_map/dot_general | solution.py:82
  141.9 0.1 collective-permute-start.7
  141.9 0.1 collective-permute-start.8
  142.0 1.7 %collective-permute-start.9 = (bf16[32,256]{1,0:T(8,128)(2,1)S(1)}, bf16[32,256]{1,0:T(8,128)(2,1)S(1)}, u32[]{:S(2)}, u32[]{:S(2)}) collective-permute-start(bf16[32,256]{1,0:T(8,128)(2,1)S(1)} %get-tuple-element.12), channel_id=1, source_target_pairs={{0,12},{4,0},{8,4},{12,8},{1,13},{5,1},{9,5},{13,9},{2,14},{6,2},{... | collective-permute-start | bytes 49160 | tf_op jit(solution)/shard_map/ppermute | solution.py:55
  143.7 8.5 %fusion.21 = f32[128,2048]{1,0:T(8,128)S(1)} fusion(bf16[4096,2048]{1,0:T(8,128)(2,1)} %param.12, bf16[32,4096]{1,0:T(8,128)(2,1)} %copy-done.2, bf16[32,4096]{1,0:T(8,128)(2,1)} %collective-permute-done.2, bf16[32,4096]{1,0:T(8,128)(2,1)} %collective-permute-done.1, bf16[32,4096]{1,0:T(8,128)(2,1)} %collective-permute-done, f32[4096]{0:T(1024)S(1)} %dynamic_slice.39, ...), kind=kOutput, calls=%fused_computation.42 | convolution fusion | flops 2153250816 | bytes 18891264 | tf_op jit(solution)/shard_map/dot_general | solution.py:81
  152.2 0.1 dynamic-slice_convert_fusion.5
  152.3 0.1 collective-permute-start.4
  152.4 1.7 %collective-permute-start.5 = (bf16[32,2048]{1,0:T(8,128)(2,1)S(1)}, bf16[32,2048]{1,0:T(8,128)(2,1)S(1)}, u32[]{:S(2)}, u32[]{:S(2)}) collective-permute-start(bf16[32,2048]{1,0:T(8,128)(2,1)S(1)} %get-tuple-element.8), channel_id=1, source_target_pairs={{0,8},{4,12},{8,0},{12,4},{1,9},{5,13},{9,1},{13,5},{2,10},{6,14},... | collective-permute-start | bytes 393224 | tf_op jit(solution)/shard_map/ppermute | solution.py:55
  154.1 1.4 collective-permute-start.6
  155.5 0.6 add_convert_fusion.1
  156.1 1.4 collective-permute-done.4
  157.5 1.2 collective-permute-done.5
  158.7 1.4 collective-permute-done.6
  160.1 0.7 add_convert_fusion
  (25 shorter events, 0.1 us)
Async XLA Ops:
  0.6 139.5 %copy-start = (bf16[4096,256]{1,0:T(8,128)(2,1)S(1)}, bf16[4096,256]{1,0:T(8,128)(2,1)}, u32[]{:S(2)}) copy-start(bf16[4096,256]{1,0:T(8,128)(2,1)} %param.13) | copy-start | bytes 6291460
  0.6 12.7 %collective-permute-start.14 = (bf16[32,6656]{1,0:T(8,128)(2,1)}, bf16[32,6656]{1,0:T(8,128)(2,1)S(1)}, u32[]{:S(2)}, u32[]{:S(2)}) collective-permute-start(bf16[32,6656]{1,0:T(8,128)(2,1)} %param.10), channel_id=1, source_target_pairs={{0,0},{1,4},{2,8},{3,12},{4,1},{5,5},{6,9},{7,13},{8,2},{9,6},{10,... | collective-permute-start | bytes 1277960 | tf_op jit(solution)/shard_map/ppermute | solution.py:33
  2.4 18.5 %collective-permute-start.15 = (bf16[32,6656]{1,0:T(8,128)(2,1)}, bf16[32,6656]{1,0:T(8,128)(2,1)S(1)}, u32[]{:S(2)}, u32[]{:S(2)}) collective-permute-start(bf16[32,6656]{1,0:T(8,128)(2,1)} %param.10), channel_id=1, source_target_pairs={{0,1},{1,5},{2,9},{3,13},{4,2},{5,6},{6,10},{7,14},{8,3},{9,7},{10... | collective-permute-start | bytes 1277960 | tf_op jit(solution)/shard_map/ppermute | solution.py:33
  5.8 44.2 %collective-permute-start.16 = (bf16[32,6656]{1,0:T(8,128)(2,1)}, bf16[32,6656]{1,0:T(8,128)(2,1)S(1)}, u32[]{:S(2)}, u32[]{:S(2)}) collective-permute-start(bf16[32,6656]{1,0:T(8,128)(2,1)} %param.10), channel_id=1, source_target_pairs={{0,2},{1,6},{2,10},{3,14},{4,3},{5,7},{6,11},{7,15},{8,0},{9,4},{1... | collective-permute-start | bytes 1277960 | tf_op jit(solution)/shard_map/ppermute | solution.py:33
  9.2 40.8 %collective-permute-start.17 = (bf16[32,6656]{1,0:T(8,128)(2,1)}, bf16[32,6656]{1,0:T(8,128)(2,1)}, u32[]{:S(2)}, u32[]{:S(2)}) collective-permute-start(bf16[32,6656]{1,0:T(8,128)(2,1)} %param.10), channel_id=1, source_target_pairs={{0,3},{1,7},{2,11},{3,15},{4,0},{5,4},{6,8},{7,12},{8,1},{9,5},{10... | collective-permute-start | bytes 1277960 | tf_op jit(solution)/shard_map/ppermute | solution.py:33
  11.8 61.6 %collective-permute-start.10 = (bf16[32,2048]{1,0:T(8,128)(2,1)}, bf16[32,2048]{1,0:T(8,128)(2,1)S(1)}, u32[]{:S(2)}, u32[]{:S(2)}) collective-permute-start(bf16[32,2048]{1,0:T(8,128)(2,1)} %param.9), channel_id=1, source_target_pairs={{0,0},{1,4},{2,8},{3,12},{4,1},{5,5},{6,9},{7,13},{8,2},{9,6},{10,... | collective-permute-start | bytes 393224 | tf_op jit(solution)/shard_map/ppermute | solution.py:33
  13.4 60.6 %collective-permute-start.11 = (bf16[32,2048]{1,0:T(8,128)(2,1)}, bf16[32,2048]{1,0:T(8,128)(2,1)S(1)}, u32[]{:S(2)}, u32[]{:S(2)}) collective-permute-start(bf16[32,2048]{1,0:T(8,128)(2,1)} %param.9), channel_id=1, source_target_pairs={{0,1},{1,5},{2,9},{3,13},{4,2},{5,6},{6,10},{7,14},{8,3},{9,7},{10... | collective-permute-start | bytes 393224 | tf_op jit(solution)/shard_map/ppermute | solution.py:33
  20.9 53.0 %collective-permute-start.12 = (bf16[32,2048]{1,0:T(8,128)(2,1)}, bf16[32,2048]{1,0:T(8,128)(2,1)S(1)}, u32[]{:S(2)}, u32[]{:S(2)}) collective-permute-start(bf16[32,2048]{1,0:T(8,128)(2,1)} %param.9), channel_id=1, source_target_pairs={{0,2},{1,6},{2,10},{3,14},{4,3},{5,7},{6,11},{7,15},{8,0},{9,4},{1... | collective-permute-start | bytes 393224 | tf_op jit(solution)/shard_map/ppermute | solution.py:33
  50.0 23.9 %collective-permute-start.13 = (bf16[32,2048]{1,0:T(8,128)(2,1)}, bf16[32,2048]{1,0:T(8,128)(2,1)S(1)}, u32[]{:S(2)}, u32[]{:S(2)}) collective-permute-start(bf16[32,2048]{1,0:T(8,128)(2,1)} %param.9), channel_id=1, source_target_pairs={{0,3},{1,7},{2,11},{3,15},{4,0},{5,4},{6,8},{7,12},{8,1},{9,5},{10... | collective-permute-start | bytes 393224 | tf_op jit(solution)/shard_map/ppermute | solution.py:33
  50.0 90.1 %collective-permute-start = (bf16[32,4096]{1,0:T(8,128)(2,1)}, bf16[32,4096]{1,0:T(8,128)(2,1)}, u32[]{:S(2)}, u32[]{:S(2)}) collective-permute-start(bf16[32,4096]{1,0:T(8,128)(2,1)} %param.8), channel_id=1, source_target_pairs={{0,0},{1,4},{2,8},{3,12},{4,1},{5,5},{6,9},{7,13},{8,2},{9,6},{10,... | collective-permute-start | bytes 786440 | tf_op jit(solution)/shard_map/ppermute | solution.py:33
  73.4 16.3 %copy-start.3 = (u32[32]{0:T(128)S(1)}, u32[32]{0:T(128)}, u32[]{:S(2)}) copy-start(u32[32]{0:T(128)} %constant.314) | copy-start | bytes 388
  73.4 66.7 %collective-permute-start.1 = (bf16[32,4096]{1,0:T(8,128)(2,1)}, bf16[32,4096]{1,0:T(8,128)(2,1)}, u32[]{:S(2)}, u32[]{:S(2)}) collective-permute-start(bf16[32,4096]{1,0:T(8,128)(2,1)} %param.8), channel_id=1, source_target_pairs={{0,1},{1,5},{2,9},{3,13},{4,2},{5,6},{6,10},{7,14},{8,3},{9,7},{10... | collective-permute-start | bytes 786440 | tf_op jit(solution)/shard_map/ppermute | solution.py:33
  82.2 1.3 copy-start.1
  84.3 7.4 %collective-permute-start.18 = (bf16[32,4096]{1,0:T(8,128)(2,1)}, bf16[32,4096]{1,0:T(8,128)(2,1)S(1)}, u32[]{:S(2)}, u32[]{:S(2)}) collective-permute-start(bf16[32,4096]{1,0:T(8,128)(2,1)} %get-tuple-element.3), channel_id=1, source_target_pairs={{0,4},{4,8},{8,12},{12,0},{1,5},{5,9},{9,13},{13,1},{2,6},{6,10},{... | collective-permute-start | bytes 786440 | tf_op jit(solution)/shard_map/ppermute | solution.py:55
  85.9 12.8 %collective-permute-start.19 = (bf16[32,4096]{1,0:T(8,128)(2,1)S(1)}, bf16[32,4096]{1,0:T(8,128)(2,1)S(1)}, u32[]{:S(2)}, u32[]{:S(2)}) collective-permute-start(bf16[32,4096]{1,0:T(8,128)(2,1)S(1)} %get-tuple-element.5), channel_id=1, source_target_pairs={{0,8},{4,12},{8,0},{12,4},{1,9},{5,13},{9,1},{13,5},{2,10},{6,14},... | collective-permute-start | bytes 786440 | tf_op jit(solution)/shard_map/ppermute | solution.py:55
  88.1 11.9 %collective-permute-start.20 = (bf16[32,4096]{1,0:T(8,128)(2,1)S(1)}, bf16[32,4096]{1,0:T(8,128)(2,1)S(1)}, u32[]{:S(2)}, u32[]{:S(2)}) collective-permute-start(bf16[32,4096]{1,0:T(8,128)(2,1)S(1)} %get-tuple-element.4), channel_id=1, source_target_pairs={{0,12},{4,0},{8,4},{12,8},{1,13},{5,1},{9,5},{13,9},{2,14},{6,2},{... | collective-permute-start | bytes 786440 | tf_op jit(solution)/shard_map/ppermute | solution.py:55
  91.7 48.4 %collective-permute-start.2 = (bf16[32,4096]{1,0:T(8,128)(2,1)}, bf16[32,4096]{1,0:T(8,128)(2,1)}, u32[]{:S(2)}, u32[]{:S(2)}) collective-permute-start(bf16[32,4096]{1,0:T(8,128)(2,1)} %param.8), channel_id=1, source_target_pairs={{0,2},{1,6},{2,10},{3,14},{4,3},{5,7},{6,11},{7,15},{8,0},{9,4},{1... | collective-permute-start | bytes 786440 | tf_op jit(solution)/shard_map/ppermute | solution.py:33
  98.7 41.4 %collective-permute-start.3 = (bf16[32,4096]{1,0:T(8,128)(2,1)}, bf16[32,4096]{1,0:T(8,128)(2,1)S(1)}, u32[]{:S(2)}, u32[]{:S(2)}) collective-permute-start(bf16[32,4096]{1,0:T(8,128)(2,1)} %param.8), channel_id=1, source_target_pairs={{0,3},{1,7},{2,11},{3,15},{4,0},{5,4},{6,8},{7,12},{8,1},{9,5},{10... | collective-permute-start | bytes 786440 | tf_op jit(solution)/shard_map/ppermute | solution.py:33
  140.1 1.7 %copy-start.2 = (bf16[32,4096]{1,0:T(8,128)(2,1)}, bf16[32,4096]{1,0:T(8,128)(2,1)S(1)}, u32[]{:S(2)}) copy-start(bf16[32,4096]{1,0:T(8,128)(2,1)S(1)} %collective-permute-done.3) | copy-start | bytes 786436
  141.9 12.2 %collective-permute-start.7 = (bf16[32,256]{1,0:T(8,128)(2,1)S(1)}, bf16[32,256]{1,0:T(8,128)(2,1)S(1)}, u32[]{:S(2)}, u32[]{:S(2)}) collective-permute-start(bf16[32,256]{1,0:T(8,128)(2,1)S(1)} %get-tuple-element.11), channel_id=1, source_target_pairs={{0,4},{4,8},{8,12},{12,0},{1,5},{5,9},{9,13},{13,1},{2,6},{6,10},{... | collective-permute-start | bytes 49160 | tf_op jit(solution)/shard_map/ppermute | solution.py:55
  141.9 13.6 %collective-permute-start.8 = (bf16[32,256]{1,0:T(8,128)(2,1)S(1)}, bf16[32,256]{1,0:T(8,128)(2,1)S(1)}, u32[]{:S(2)}, u32[]{:S(2)}) collective-permute-start(bf16[32,256]{1,0:T(8,128)(2,1)S(1)} %get-tuple-element.13), channel_id=1, source_target_pairs={{0,8},{4,12},{8,0},{12,4},{1,9},{5,13},{9,1},{13,5},{2,10},{6,14},... | collective-permute-start | bytes 49160 | tf_op jit(solution)/shard_map/ppermute | solution.py:55
  142.0 13.5 %collective-permute-start.9 = (bf16[32,256]{1,0:T(8,128)(2,1)S(1)}, bf16[32,256]{1,0:T(8,128)(2,1)S(1)}, u32[]{:S(2)}, u32[]{:S(2)}) collective-permute-start(bf16[32,256]{1,0:T(8,128)(2,1)S(1)} %get-tuple-element.12), channel_id=1, source_target_pairs={{0,12},{4,0},{8,4},{12,8},{1,13},{5,1},{9,5},{13,9},{2,14},{6,2},{... | collective-permute-start | bytes 49160 | tf_op jit(solution)/shard_map/ppermute | solution.py:55
  152.3 5.2 %collective-permute-start.4 = (bf16[32,2048]{1,0:T(8,128)(2,1)S(1)}, bf16[32,2048]{1,0:T(8,128)(2,1)S(1)}, u32[]{:S(2)}, u32[]{:S(2)}) collective-permute-start(bf16[32,2048]{1,0:T(8,128)(2,1)S(1)} %get-tuple-element.6), channel_id=1, source_target_pairs={{0,4},{4,8},{8,12},{12,0},{1,5},{5,9},{9,13},{13,1},{2,6},{6,10},{... | collective-permute-start | bytes 393224 | tf_op jit(solution)/shard_map/ppermute | solution.py:55
  152.4 6.3 %collective-permute-start.5 = (bf16[32,2048]{1,0:T(8,128)(2,1)S(1)}, bf16[32,2048]{1,0:T(8,128)(2,1)S(1)}, u32[]{:S(2)}, u32[]{:S(2)}) collective-permute-start(bf16[32,2048]{1,0:T(8,128)(2,1)S(1)} %get-tuple-element.8), channel_id=1, source_target_pairs={{0,8},{4,12},{8,0},{12,4},{1,9},{5,13},{9,1},{13,5},{2,10},{6,14},... | collective-permute-start | bytes 393224 | tf_op jit(solution)/shard_map/ppermute | solution.py:55
  154.1 6.0 %collective-permute-start.6 = (bf16[32,2048]{1,0:T(8,128)(2,1)S(1)}, bf16[32,2048]{1,0:T(8,128)(2,1)S(1)}, u32[]{:S(2)}, u32[]{:S(2)}) collective-permute-start(bf16[32,2048]{1,0:T(8,128)(2,1)S(1)} %get-tuple-element.7), channel_id=1, source_target_pairs={{0,12},{4,0},{8,4},{12,8},{1,13},{5,1},{9,5},{13,9},{2,14},{6,2},{... | collective-permute-start | bytes 393224 | tf_op jit(solution)/shard_map/ppermute | solution.py:55

commit v2 on v0

v2 whole, which is shorter than its diff:
```python
import jax
import jax.numpy as jnp
from jax import lax
from jax.sharding import PartitionSpec as P

norm_epsilon = 1e-05


def after(value, *others):
    return lax.optimization_barrier((value, others))[0]


def dot(left, right):
    return jnp.dot(left, right, preferred_element_type=jnp.float32)


def flip(value, axis, bit):
    return lax.ppermute(value, axis, [(i, i ^ bit) for i in range(lax.axis_size(axis))])


slots = (0, 2, 1, 3)


def solution(mesh):
    nx, ny = mesh.shape["gx"], mesh.shape["gy"]
    square = nx == 4 and ny == 4

    def over_z(block):
        return block, flip(block, "gy", 2)

    def over_x(pair):
        block, far = pair
        mine = lax.axis_index("gx") // 2 == lax.axis_index("gy") // 2
        keep, give = jnp.where(mine, block, far), jnp.where(mine, far, block)
        return keep, flip(give, "gx", 2)

    def over_near_z(pair):
        keep = jnp.concatenate(pair)
        return keep, flip(keep, "gy", 1)

    def over_cores(pair):
        keep, near = pair
        mine = lax.axis_index("gx") % 2 == lax.axis_index("gy") % 2
        keep, give = jnp.where(mine, keep, near), jnp.where(mine, near, keep)
        return keep, flip(give, "gx", 1)

    def gather_plain(block):
        wide = lax.all_gather(block, "gy", axis=1, tiled=True)
        return lax.all_to_all(wide, "gx", split_axis=1, concat_axis=0, tiled=True)

    def sum_over_gx(partial, rows):
        if not square:
            return partial, lax.psum_scatter(partial, "gx", scatter_dimension=0, tiled=True)
        give = partial[2 * rows :]
        pair = partial[: 2 * rows] + flip(give.astype(jnp.bfloat16), "gx", 1).astype(jnp.float32)
        return pair, pair[:rows] + flip(pair[rows:].astype(jnp.bfloat16), "gx", 2).astype(jnp.float32)

    def sum_over_gy(value):
        if not square:
            return lax.psum(value, "gy")
        value = value + flip(value, "gy", 1)
        return value + flip(value, "gy", 2)

    def local(layer_input, attn_context, ffn_hidden, norm_gain, w_query, w_keyval, w_out, w_down):
        rows, feat_width = layer_input.shape
        model_width = norm_gain.shape[0]

        input_float = layer_input.astype(jnp.float32)
        row_sums = sum_over_gy(jnp.sum(input_float * input_float, axis=1))
        scale = lax.rsqrt(row_sums / model_width + norm_epsilon)
        gain = lax.dynamic_slice_in_dim(norm_gain, lax.axis_index("gy") * feat_width, feat_width)
        normed = (input_float * scale[:, None] * gain).astype(jnp.bfloat16)

        if square:
            half = ffn_hidden.shape[1] // 2
            first, second = ffn_hidden[:, :half], ffn_hidden[:, half:]
            context, first = over_z(attn_context), over_z(first)
            second = over_z(after(second, context[1]))
            context = over_x(context)
            normed = over_z(normed)
            first = over_x(first)
            context = over_near_z(context)
            context = over_cores(context)
            first = over_near_z(first)
            second = over_x(second)
            ready = jnp.concatenate(after(context, normed[1]))
            block_part = dot(ready, w_out)
            first = over_cores(first)
            normed = over_x(normed)
            second = over_near_z(second)
            ready = jnp.concatenate(after(first, block_part))
            block_part += dot(ready, w_down[:half])
            second = over_cores(after(second, block_part))
            normed = over_near_z(normed)
            ready = jnp.concatenate(after(second, block_part))
            block_part += dot(ready, w_down[half:])
            normed = jnp.concatenate(over_cores(normed))
            normed = after(normed, block_part)
        else:
            context, hidden, normed = gather_plain(attn_context), gather_plain(ffn_hidden), gather_plain(normed)
            block_part = dot(context, w_out) + dot(hidden, w_down)
        paired, block_sum = sum_over_gx(block_part, rows)
        normed = after(normed, paired)

        query_part, keyval_part = dot(normed, w_query), dot(normed, w_keyval)
        heads = sum_over_gx(jnp.concatenate([query_part, keyval_part], axis=1), rows)[1].astype(jnp.bfloat16)
        split = w_query.shape[1]
        return (heads[:, :split], heads[:, split:], (input_float + block_sum).astype(jnp.bfloat16))

    return jax.shard_map(
        local,
        mesh=mesh,
        in_specs=(
            P(("groups", "gx"), "gy"),
            P(("groups", "gx"), "gy"),
            P(("groups", "gx"), "gy"),
            P(),
            P("gx", "gy"),
            P("gx", "gy"),
            P("gx", "gy"),
            P("gx", "gy"),
        ),
        out_specs=(P(("groups", "gx"), "gy"), P(("groups", "gx"), "gy"), P(("groups", "gx"), "gy")),
        check_vma=False,
    )
```

time: 233 us -> 117 us (0.50)
  blocking collectives: 91.2 us -> 0 us
  waiting for transfers between devices: 77.2 us -> 42.6 us
  starting transfers between devices: 0.21 us -> 24.7 us
  between operations: 15.7 us -> 0.89 us
    all_to_all x3 -> x0, blocking collectives: 63.4 us -> none  [the longest x1 35.1 us: local(): lax.all_to_all(wide_hidden, 'gx', split_axis=1, concat_axis=0, tiled=True)]
    reduce_scatter x3 -> x0, waiting for transfers between devices: 43.3 us -> none  [the longest x1 24.3 us: local(): lax.psum_scatter(jnp.concatenate([query_part, keyval_part], axis=1), 'gx'...]
    ppermute x0 -> x22, waiting for transfers between devices: none -> 42.6 us  [flip(): lax.ppermute(value, axis, [(i, i ^ bit) for i in range(lax.axis_size(axis...]
    all_gather x2 -> x0, waiting for transfers between devices: 33.2 us -> none  [the longest x1 28 us: local(): lax.all_gather(normed, 'gy', axis=1, tiled=True)]
    ppermute x0 -> x22, starting transfers between devices: none -> 24.7 us  [flip(): lax.ppermute(value, axis, [(i, i ^ bit) for i in range(lax.axis_size(axis...]
    all_gather x1 -> x0, blocking collectives: 19.4 us -> none  [local(): lax.all_gather(attn_context, 'gy', axis=1, tiled=True)]
    psum x1 -> x0, blocking collectives: 8.36 us -> none  [local(): summed = lax.psum(row_sums, 'gy')]
    all_to_all x3 -> x0, local copies, waits for them, and re-layouts: 3.17 us -> none  [the longest x1 1.84 us: local(): lax.all_to_all(wide_hidden, 'gx', split_axis=1, concat_axis=0, tiled=True)]
  transfers between devices with their start and end apart: 5 -> 22, of which waited for: 4 -> 12; matrix products, arithmetic and copies ran while one was open for 14% -> 32% of each run, Pallas kernels for 0% -> 0%
where the time goes in v2:
time: 117 us
  waiting for transfers between devices  42.6 us (36%)
  matrix products  40.1 us (34%)
  starting transfers between devices  24.7 us (21%)
  other arithmetic  5.27 us (5%)
  local copies, waits for them, and re-layouts  3.06 us (3%)
    ppermute x22, waiting for transfers between devices, flip(): lax.ppermute(value, axis, [(i, i ^ bit) for i in range(lax.axis_size(axis...  42.6 us
    dot_general x5, matrix products, dot(): return jnp.dot(left, right, preferred_element_type=jnp.float32)  40.1 us
    ppermute x22, starting transfers between devices, flip(): lax.ppermute(value, axis, [(i, i ^ bit) for i in range(lax.axis_size(axis...  24.7 us
  transfers between devices with their start and end apart: 22, of which 12 were waited for; matrix products, arithmetic and copies ran while one was open for 32% of the time, Pallas kernels for 0%

profile of v2, /device:TPU:0, one launch (start us, length us, event | category | flops | bytes accessed | tf_op | source)
XLA Modules:
  0.0 116.6 jit_solution(6905612401682469845)
XLA Ops:
  0.7 1.3 %fusion.19 = f32[32]{0:T(128)S(1)} fusion(bf16[32,4096]{1,0:T(8,128)(2,1)} %param.8), kind=kLoop, calls=%fused_computation.24 | loop fusion | flops 393184 | bytes 262272 | tf_op jit(solution)/shard_map/reduce_sum | solution.py:69
  1.9 3.1 %collective-permute-start = (f32[32]{0:T(128)S(1)}, f32[32]{0:T(128)S(1)}, u32[]{:S(2)}, u32[]{:S(2)}) collective-permute-start(f32[32]{0:T(128)S(1)} %fusion.19), channel_id=1, source_target_pairs={{0,1},{1,0},{2,3},{3,2},{4,5},{5,4},{6,7},{7,6},{8,9},{9,8},{10,11... | collective-permute-start | bytes 392 | tf_op jit(solution)/shard_map/ppermute | solution.py:18
  5.0 2.6 %collective-permute-start.6 = (bf16[32,2048]{1,0:T(8,128)(2,1)}, bf16[32,2048]{1,0:T(8,128)(2,1)S(1)}, u32[]{:S(2)}, u32[]{:S(2)}) collective-permute-start(bf16[32,2048]{1,0:T(8,128)(2,1)} %param.9), channel_id=1, source_target_pairs={{0,2},{1,3},{2,0},{3,1},{4,6},{5,7},{6,4},{7,5},{8,10},{9,11},{10,... | collective-permute-start | bytes 393224 | tf_op jit(solution)/shard_map/ppermute | solution.py:18
  7.6 0.9 slice.46
  8.6 0.4 collective-permute-start.10
  9.0 0.7 dynamic_slice.3
  9.7 2.6 %collective-permute-start.1 = (f32[32]{0:T(128)S(1)}, f32[32]{0:T(128)S(1)}, u32[]{:S(2)}, u32[]{:S(2)}) collective-permute-start(f32[32]{0:T(128)S(1)} %add.53), channel_id=1, source_target_pairs={{0,2},{1,3},{2,0},{3,1},{4,6},{5,7},{6,4},{7,5},{8,10},{9,11},{10,... | collective-permute-start | bytes 392 | tf_op jit(solution)/shard_map/ppermute | solution.py:18
  12.3 10.7 %collective-permute-done.1 = f32[32]{0:T(128)S(1)} collective-permute-done((f32[32]{0:T(128)S(1)}, f32[32]{0:T(128)S(1)}, u32[]{:S(2)}, u32[]{:S(2)}) %collective-permute-start.1) | collective-permute-done | bytes 160 | tf_op jit(solution)/shard_map/ppermute | solution.py:18
  22.9 1.1 fusion.21
  24.0 0.1 collective-permute-start.2
  24.1 0.9 broadcast_select_fusion.15
  25.1 1.6 %collective-permute-start.7 = (bf16[32,2048]{1,0:T(8,128)(2,1)S(1)}, bf16[32,2048]{1,0:T(8,128)(2,1)S(1)}, u32[]{:S(2)}, u32[]{:S(2)}) collective-permute-start(bf16[32,2048]{1,0:T(8,128)(2,1)S(1)} %get-tuple-element.41), channel_id=1, source_target_pairs={{0,8},{4,12},{8,0},{12,4},{1,9},{5,13},{9,1},{13,5},{2,10},{6,14},... | collective-permute-start | bytes 393224 | tf_op jit(solution)/shard_map/ppermute | solution.py:18
  26.7 0.5 collective-permute-start.11
  27.3 2.9 %collective-permute-start.14 = (bf16[32,3328]{1,0:T(8,128)(2,1)S(1)}, bf16[32,3328]{1,0:T(8,128)(2,1)S(1)}, u32[]{:S(2)}, u32[]{:S(2)}) collective-permute-start(bf16[32,3328]{1,0:T(8,128)(2,1)S(1)} %get-tuple-element.18), channel_id=1, source_target_pairs={{0,2},{1,3},{2,0},{3,1},{4,6},{5,7},{6,4},{7,5},{8,10},{9,11},{10,... | collective-permute-start | bytes 638984 | tf_op jit(solution)/shard_map/ppermute | solution.py:18
  30.2 1.3 %collective-permute-done.7 = bf16[32,2048]{1,0:T(8,128)(2,1)S(1)} collective-permute-done((bf16[32,2048]{1,0:T(8,128)(2,1)S(1)}, bf16[32,2048]{1,0:T(8,128)(2,1)S(1)}, u32[]{:S(2)}, u32[]{:S(2)}) %collective-permute-start.7) | collective-permute-done | bytes 131104 | tf_op jit(solution)/shard_map/ppermute | solution.py:18
  31.5 3.2 %collective-permute-start.8 = (bf16[64,2048]{1,0:T(8,128)(2,1)S(1)}, bf16[64,2048]{1,0:T(8,128)(2,1)S(1)}, u32[]{:S(2)}, u32[]{:S(2)}) collective-permute-start(bf16[64,2048]{1,0:T(8,128)(2,1)S(1)} %pad_maximum_fusion.5), channel_id=1, source_target_pairs={{0,1},{1,0},{2,3},{3,2},{4,5},{5,4},{6,7},{7,6},{8,9},{9,8},{10,11... | collective-permute-start | bytes 786440 | tf_op jit(solution)/shard_map/ppermute | solution.py:18
  34.7 7.8 %collective-permute-done.2 = bf16[32,4096]{1,0:T(8,128)(2,1)S(1)} collective-permute-done((bf16[32,4096]{1,0:T(8,128)(2,1)S(1)}, bf16[32,4096]{1,0:T(8,128)(2,1)S(1)}, u32[]{:S(2)}, u32[]{:S(2)}) %collective-permute-start.2) | collective-permute-done | bytes 262176 | tf_op jit(solution)/shard_map/ppermute | solution.py:18
  42.5 0.2 broadcast_select_fusion.9
  42.7 1.6 %collective-permute-start.3 = (bf16[32,4096]{1,0:T(8,128)(2,1)S(1)}, bf16[32,4096]{1,0:T(8,128)(2,1)S(1)}, u32[]{:S(2)}, u32[]{:S(2)}) collective-permute-start(bf16[32,4096]{1,0:T(8,128)(2,1)S(1)} %get-tuple-element.36), channel_id=1, source_target_pairs={{0,8},{4,12},{8,0},{12,4},{1,9},{5,13},{9,1},{13,5},{2,10},{6,14},... | collective-permute-start | bytes 786440 | tf_op jit(solution)/shard_map/ppermute | solution.py:18
  44.3 0.1 collective-permute-start.12
  44.4 2.6 %collective-permute-done.14 = bf16[32,3328]{1,0:T(8,128)(2,1)S(1)} collective-permute-done((bf16[32,3328]{1,0:T(8,128)(2,1)S(1)}, bf16[32,3328]{1,0:T(8,128)(2,1)S(1)}, u32[]{:S(2)}, u32[]{:S(2)}) %collective-permute-start.14) | collective-permute-done | bytes 213024 | tf_op jit(solution)/shard_map/ppermute | solution.py:18
  47.0 1.6 %collective-permute-start.15 = (bf16[32,3328]{1,0:T(8,128)(2,1)S(1)}, bf16[32,3328]{1,0:T(8,128)(2,1)S(1)}, u32[]{:S(2)}, u32[]{:S(2)}) collective-permute-start(bf16[32,3328]{1,0:T(8,128)(2,1)S(1)} %get-tuple-element.38), channel_id=1, source_target_pairs={{0,8},{4,12},{8,0},{12,4},{1,9},{5,13},{9,1},{13,5},{2,10},{6,14},... | collective-permute-start | bytes 638984 | tf_op jit(solution)/shard_map/ppermute | solution.py:18
  48.5 1.0 collective-permute-done.8
  49.5 0.1 broadcast_select_fusion.6
  49.7 2.2 %collective-permute-done.3 = bf16[32,4096]{1,0:T(8,128)(2,1)S(1)} collective-permute-done((bf16[32,4096]{1,0:T(8,128)(2,1)S(1)}, bf16[32,4096]{1,0:T(8,128)(2,1)S(1)}, u32[]{:S(2)}, u32[]{:S(2)}) %collective-permute-start.3) | collective-permute-done | bytes 262176 | tf_op jit(solution)/shard_map/ppermute | solution.py:18
  52.0 3.3 %collective-permute-done.15 = bf16[32,3328]{1,0:T(8,128)(2,1)S(1)} collective-permute-done((bf16[32,3328]{1,0:T(8,128)(2,1)S(1)}, bf16[32,3328]{1,0:T(8,128)(2,1)S(1)}, u32[]{:S(2)}, u32[]{:S(2)}) %collective-permute-start.15) | collective-permute-done | bytes 213024 | tf_op jit(solution)/shard_map/ppermute | solution.py:18
  55.5 3.1 %collective-permute-done.12 = bf16[64,3328]{1,0:T(8,128)(2,1)S(1)} collective-permute-done((bf16[64,3328]{1,0:T(8,128)(2,1)S(1)}, bf16[64,3328]{1,0:T(8,128)(2,1)S(1)}, u32[]{:S(2)}, u32[]{:S(2)}) %collective-permute-start.12) | collective-permute-done | bytes 426016 | tf_op jit(solution)/shard_map/ppermute | solution.py:18
  58.7 0.1 broadcast_select_fusion.4
  58.9 8.1 %fusion.23 = f32[128,4096]{1,0:T(8,128)S(1)} fusion(bf16[2048,4096]{1,0:T(8,128)(2,1)} %param.14, bf16[64,2048]{1,0:T(8,128)(2,1)S(1)} %collective-permute-done.9, bf16[64,2048]{1,0:T(8,128)(2,1)S(1)} %get-tuple-element.14), kind=kOutput, calls=%fused_computation.31 | convolution fusion | flops 2148532224 | bytes 19398656 | tf_op jit(solution)/shard_map/dot_general | solution.py:14
  67.0 12.4 %fusion.4 = f32[128,4096]{1,0:T(8,128)} fusion(f32[128,4096]{1,0:T(8,128)S(1)} %fusion.23, bf16[6656,4096]{1,0:T(8,128)(2,1)} %param.15, bf16[64,3328]{1,0:T(8,128)(2,1)S(1)} %collective-permute-done.13, bf16[64,3328]{1,0:T(8,128)(2,1)S(1)} %get-tuple-element.16), kind=kOutput, calls=%fused_computation.4 | convolution fusion | flops 3491889152 | bytes 32309248 | tf_op jit(solution)/shard_map/dot_general | solution.py:14
  79.5 0.6 collective-permute-start.17
  80.1 0.2 broadcast_select_fusion.1
  80.3 0.1 collective-permute-start.5
  80.4 1.1 collective-permute-done.17
  81.5 10.9 %fusion.7 = f32[128,4096]{1,0:T(8,128)S(1)} fusion(f32[128,4096]{1,0:T(8,128)S(1)} %copy-done.3, bf16[6656,4096]{1,0:T(8,128)(2,1)} %param.15, bf16[64,3328]{1,0:T(8,128)(2,1)S(1)} %collective-permute-done.17, bf16[64,3328]{1,0:T(8,128)(2,1)S(1)} %get-tuple-element.21), kind=kOutput, calls=%fused_computation.5 | convolution fusion | flops 3491889152 | bytes 32309248 | tf_op jit(solution)/shard_map/dot_general | solution.py:14
  92.4 0.4 collective-permute-start.18
  93.0 1.5 %collective-permute-done.18 = bf16[64,4096]{1,0:T(8,128)(2,1)S(1)} collective-permute-done((bf16[64,4096]{1,0:T(8,128)(2,1)S(1)}, bf16[64,4096]{1,0:T(8,128)(2,1)S(1)}, u32[]{:S(2)}, u32[]{:S(2)}) %collective-permute-start.18) | collective-permute-done | bytes 524320 | tf_op jit(solution)/shard_map/ppermute | solution.py:18
  94.4 0.1 slice_add_fusion
  94.5 8.2 %fusion.31 = f32[128,2048]{1,0:T(8,128)S(1)} fusion(bf16[128,4096]{1,0:T(8,128)(2,1)S(1)} %pad_maximum_fusion, bf16[4096,2048]{1,0:T(8,128)(2,1)} %param.12), kind=kOutput, calls=%fused_computation.61 | convolution fusion | flops 2147483648 | bytes 18874368 | tf_op jit(solution)/shard_map/dot_general | solution.py:14
  102.7 0.5 fusion.32
  103.2 0.4 collective-permute-start.19
  103.7 1.6 %collective-permute-start.21 = (bf16[32,4096]{1,0:T(8,128)(2,1)S(1)}, bf16[32,4096]{1,0:T(8,128)(2,1)S(1)}, u32[]{:S(2)}, u32[]{:S(2)}) collective-permute-start(bf16[32,4096]{1,0:T(8,128)(2,1)S(1)} %slice.99), channel_id=1, source_target_pairs={{0,8},{4,12},{8,0},{12,4},{1,9},{5,13},{9,1},{13,5},{2,10},{6,14},... | collective-permute-start | bytes 786440 | tf_op jit(solution)/shard_map/ppermute | solution.py:18
  105.4 1.2 %collective-permute-start.20 = (bf16[32,2304]{1,0:T(8,128)(2,1)S(1)}, bf16[32,2304]{1,0:T(8,128)(2,1)S(1)}, u32[]{:S(2)}, u32[]{:S(2)}) collective-permute-start(bf16[32,2304]{1,0:T(8,128)(2,1)S(1)} %slice.100), channel_id=1, source_target_pairs={{0,8},{4,12},{8,0},{12,4},{1,9},{5,13},{9,1},{13,5},{2,10},{6,14},... | collective-permute-start | bytes 442376 | tf_op jit(solution)/shard_map/ppermute | solution.py:18
  106.6 6.4 %collective-permute-done.21 = bf16[32,4096]{1,0:T(8,128)(2,1)S(1)} collective-permute-done((bf16[32,4096]{1,0:T(8,128)(2,1)S(1)}, bf16[32,4096]{1,0:T(8,128)(2,1)S(1)}, u32[]{:S(2)}, u32[]{:S(2)}) %collective-permute-start.21) | collective-permute-done | bytes 262176 | tf_op jit(solution)/shard_map/ppermute | solution.py:18
  112.9 0.8 fusion.22
  113.7 1.6 %collective-permute-done.20 = bf16[32,2304]{1,0:T(8,128)(2,1)S(1)} collective-permute-done((bf16[32,2304]{1,0:T(8,128)(2,1)S(1)}, bf16[32,2304]{1,0:T(8,128)(2,1)S(1)}, u32[]{:S(2)}, u32[]{:S(2)}) %collective-permute-start.20) | collective-permute-done | bytes 147488 | tf_op jit(solution)/shard_map/ppermute | solution.py:18
  115.3 0.7 slice.66
  116.0 0.6 slice.67
  (38 shorter events, 0.9 us)
Async XLA Ops:
  0.6 102.1 %copy-start = (bf16[4096,256]{1,0:T(8,128)(2,1)S(1)}, bf16[4096,256]{1,0:T(8,128)(2,1)}, u32[]{:S(2)}) copy-start(bf16[4096,256]{1,0:T(8,128)(2,1)} %param.13) | copy-start | bytes 6291460
  0.6 41.8 %copy-start.1 = (bf16[32,4096]{1,0:T(8,128)(2,1)S(1)}, bf16[32,4096]{1,0:T(8,128)(2,1)}, u32[]{:S(2)}) copy-start(bf16[32,4096]{1,0:T(8,128)(2,1)} %param.8) | copy-start | bytes 786436
  0.7 26.0 %copy-start.2 = (bf16[32,6656]{1,0:T(8,128)(2,1)S(1)}, bf16[32,6656]{1,0:T(8,128)(2,1)}, u32[]{:S(2)}) copy-start(bf16[32,6656]{1,0:T(8,128)(2,1)} %param.10) | copy-start | bytes 1277956
  1.9 7.7 %collective-permute-start = (f32[32]{0:T(128)S(1)}, f32[32]{0:T(128)S(1)}, u32[]{:S(2)}, u32[]{:S(2)}) collective-permute-start(f32[32]{0:T(128)S(1)} %fusion.19), channel_id=1, source_target_pairs={{0,1},{1,0},{2,3},{3,2},{4,5},{5,4},{6,7},{7,6},{8,9},{9,8},{10,11... | collective-permute-start | bytes 392 | tf_op jit(solution)/shard_map/ppermute | solution.py:18
  5.0 19.1 %collective-permute-start.6 = (bf16[32,2048]{1,0:T(8,128)(2,1)}, bf16[32,2048]{1,0:T(8,128)(2,1)S(1)}, u32[]{:S(2)}, u32[]{:S(2)}) collective-permute-start(bf16[32,2048]{1,0:T(8,128)(2,1)} %param.9), channel_id=1, source_target_pairs={{0,2},{1,3},{2,0},{3,1},{4,6},{5,7},{6,4},{7,5},{8,10},{9,11},{10,... | collective-permute-start | bytes 393224 | tf_op jit(solution)/shard_map/ppermute | solution.py:18
  8.6 18.1 %collective-permute-start.10 = (bf16[32,3328]{1,0:T(8,128)(2,1)S(1)}, bf16[32,3328]{1,0:T(8,128)(2,1)S(1)}, u32[]{:S(2)}, u32[]{:S(2)}) collective-permute-start(bf16[32,3328]{1,0:T(8,128)(2,1)S(1)} %slice.46), channel_id=1, source_target_pairs={{0,2},{1,3},{2,0},{3,1},{4,6},{5,7},{6,4},{7,5},{8,10},{9,11},{10,... | collective-permute-start | bytes 638984 | tf_op jit(solution)/shard_map/ppermute | solution.py:18
  9.7 13.2 %collective-permute-start.1 = (f32[32]{0:T(128)S(1)}, f32[32]{0:T(128)S(1)}, u32[]{:S(2)}, u32[]{:S(2)}) collective-permute-start(f32[32]{0:T(128)S(1)} %add.53), channel_id=1, source_target_pairs={{0,2},{1,3},{2,0},{3,1},{4,6},{5,7},{6,4},{7,5},{8,10},{9,11},{10,... | collective-permute-start | bytes 392 | tf_op jit(solution)/shard_map/ppermute | solution.py:18
  24.0 18.4 %collective-permute-start.2 = (bf16[32,4096]{1,0:T(8,128)(2,1)S(1)}, bf16[32,4096]{1,0:T(8,128)(2,1)S(1)}, u32[]{:S(2)}, u32[]{:S(2)}) collective-permute-start(bf16[32,4096]{1,0:T(8,128)(2,1)S(1)} %fusion.21), channel_id=1, source_target_pairs={{0,2},{1,3},{2,0},{3,1},{4,6},{5,7},{6,4},{7,5},{8,10},{9,11},{10,... | collective-permute-start | bytes 786440 | tf_op jit(solution)/shard_map/ppermute | solution.py:18
  25.1 6.4 %collective-permute-start.7 = (bf16[32,2048]{1,0:T(8,128)(2,1)S(1)}, bf16[32,2048]{1,0:T(8,128)(2,1)S(1)}, u32[]{:S(2)}, u32[]{:S(2)}) collective-permute-start(bf16[32,2048]{1,0:T(8,128)(2,1)S(1)} %get-tuple-element.41), channel_id=1, source_target_pairs={{0,8},{4,12},{8,0},{12,4},{1,9},{5,13},{9,1},{13,5},{2,10},{6,14},... | collective-permute-start | bytes 393224 | tf_op jit(solution)/shard_map/ppermute | solution.py:18
  26.7 17.5 %collective-permute-start.11 = (bf16[32,3328]{1,0:T(8,128)(2,1)S(1)}, bf16[32,3328]{1,0:T(8,128)(2,1)S(1)}, u32[]{:S(2)}, u32[]{:S(2)}) collective-permute-start(bf16[32,3328]{1,0:T(8,128)(2,1)S(1)} %get-tuple-element.32), channel_id=1, source_target_pairs={{0,8},{4,12},{8,0},{12,4},{1,9},{5,13},{9,1},{13,5},{2,10},{6,14},... | collective-permute-start | bytes 638984 | tf_op jit(solution)/shard_map/ppermute | solution.py:18
  27.3 19.7 %collective-permute-start.14 = (bf16[32,3328]{1,0:T(8,128)(2,1)S(1)}, bf16[32,3328]{1,0:T(8,128)(2,1)S(1)}, u32[]{:S(2)}, u32[]{:S(2)}) collective-permute-start(bf16[32,3328]{1,0:T(8,128)(2,1)S(1)} %get-tuple-element.18), channel_id=1, source_target_pairs={{0,2},{1,3},{2,0},{3,1},{4,6},{5,7},{6,4},{7,5},{8,10},{9,11},{10,... | collective-permute-start | bytes 638984 | tf_op jit(solution)/shard_map/ppermute | solution.py:18
  31.5 18.0 %collective-permute-start.8 = (bf16[64,2048]{1,0:T(8,128)(2,1)S(1)}, bf16[64,2048]{1,0:T(8,128)(2,1)S(1)}, u32[]{:S(2)}, u32[]{:S(2)}) collective-permute-start(bf16[64,2048]{1,0:T(8,128)(2,1)S(1)} %pad_maximum_fusion.5), channel_id=1, source_target_pairs={{0,1},{1,0},{2,3},{3,2},{4,5},{5,4},{6,7},{7,6},{8,9},{9,8},{10,11... | collective-permute-start | bytes 786440 | tf_op jit(solution)/shard_map/ppermute | solution.py:18
  42.7 9.3 %collective-permute-start.3 = (bf16[32,4096]{1,0:T(8,128)(2,1)S(1)}, bf16[32,4096]{1,0:T(8,128)(2,1)S(1)}, u32[]{:S(2)}, u32[]{:S(2)}) collective-permute-start(bf16[32,4096]{1,0:T(8,128)(2,1)S(1)} %get-tuple-element.36), channel_id=1, source_target_pairs={{0,8},{4,12},{8,0},{12,4},{1,9},{5,13},{9,1},{13,5},{2,10},{6,14},... | collective-permute-start | bytes 786440 | tf_op jit(solution)/shard_map/ppermute | solution.py:18
  44.3 14.4 %collective-permute-start.12 = (bf16[64,3328]{1,0:T(8,128)(2,1)S(1)}, bf16[64,3328]{1,0:T(8,128)(2,1)S(1)}, u32[]{:S(2)}, u32[]{:S(2)}) collective-permute-start(bf16[64,3328]{1,0:T(8,128)(2,1)S(1)} %pad_maximum_fusion.3), channel_id=1, source_target_pairs={{0,1},{1,0},{2,3},{3,2},{4,5},{5,4},{6,7},{7,6},{8,9},{9,8},{10,11... | collective-permute-start | bytes 1277960 | tf_op jit(solution)/shard_map/ppermute | solution.py:18
  47.0 8.4 %collective-permute-start.15 = (bf16[32,3328]{1,0:T(8,128)(2,1)S(1)}, bf16[32,3328]{1,0:T(8,128)(2,1)S(1)}, u32[]{:S(2)}, u32[]{:S(2)}) collective-permute-start(bf16[32,3328]{1,0:T(8,128)(2,1)S(1)} %get-tuple-element.38), channel_id=1, source_target_pairs={{0,8},{4,12},{8,0},{12,4},{1,9},{5,13},{9,1},{13,5},{2,10},{6,14},... | collective-permute-start | bytes 638984 | tf_op jit(solution)/shard_map/ppermute | solution.py:18
  49.6 5.9 %collective-permute-start.9 = (bf16[64,2048]{1,0:T(8,128)(2,1)S(1)}, bf16[64,2048]{1,0:T(8,128)(2,1)S(1)}, u32[]{:S(2)}, u32[]{:S(2)}) collective-permute-start(bf16[64,2048]{1,0:T(8,128)(2,1)S(1)} %get-tuple-element.33), channel_id=1, source_target_pairs={{0,4},{4,0},{8,12},{12,8},{1,5},{5,1},{9,13},{13,9},{2,6},{6,2},{1... | collective-permute-start | bytes 786440 | tf_op jit(solution)/shard_map/ppermute | solution.py:18
  52.0 28.1 %collective-permute-start.4 = (bf16[64,4096]{1,0:T(8,128)(2,1)S(1)}, bf16[64,4096]{1,0:T(8,128)(2,1)S(1)}, u32[]{:S(2)}, u32[]{:S(2)}) collective-permute-start(bf16[64,4096]{1,0:T(8,128)(2,1)S(1)} %pad_maximum_fusion.2), channel_id=1, source_target_pairs={{0,1},{1,0},{2,3},{3,2},{4,5},{5,4},{6,7},{7,6},{8,9},{9,8},{10,11... | collective-permute-start | bytes 1572872 | tf_op jit(solution)/shard_map/ppermute | solution.py:18
  55.4 24.0 %collective-permute-start.16 = (bf16[64,3328]{1,0:T(8,128)(2,1)S(1)}, bf16[64,3328]{1,0:T(8,128)(2,1)S(1)}, u32[]{:S(2)}, u32[]{:S(2)}) collective-permute-start(bf16[64,3328]{1,0:T(8,128)(2,1)S(1)} %pad_maximum_fusion.4), channel_id=1, source_target_pairs={{0,1},{1,0},{2,3},{3,2},{4,5},{5,4},{6,7},{7,6},{8,9},{9,8},{10,11... | collective-permute-start | bytes 1277960 | tf_op jit(solution)/shard_map/ppermute | solution.py:18
  58.8 8.2 %collective-permute-start.13 = (bf16[64,3328]{1,0:T(8,128)(2,1)S(1)}, bf16[64,3328]{1,0:T(8,128)(2,1)S(1)}, u32[]{:S(2)}, u32[]{:S(2)}) collective-permute-start(bf16[64,3328]{1,0:T(8,128)(2,1)S(1)} %get-tuple-element.29), channel_id=1, source_target_pairs={{0,4},{4,0},{8,12},{12,8},{1,5},{5,1},{9,13},{13,9},{2,6},{6,2},{1... | collective-permute-start | bytes 1277960 | tf_op jit(solution)/shard_map/ppermute | solution.py:18
  79.5 2.0 %copy-start.3 = (f32[128,4096]{1,0:T(8,128)S(1)}, f32[128,4096]{1,0:T(8,128)}, u32[]{:S(2)}) copy-start(f32[128,4096]{1,0:T(8,128)} %fusion.4) | copy-start | bytes 6291460
  79.5 2.0 %collective-permute-start.17 = (bf16[64,3328]{1,0:T(8,128)(2,1)S(1)}, bf16[64,3328]{1,0:T(8,128)(2,1)S(1)}, u32[]{:S(2)}, u32[]{:S(2)}) collective-permute-start(bf16[64,3328]{1,0:T(8,128)(2,1)S(1)} %get-tuple-element.27), channel_id=1, source_target_pairs={{0,4},{4,0},{8,12},{12,8},{1,5},{5,1},{9,13},{13,9},{2,6},{6,2},{1... | collective-permute-start | bytes 1277960 | tf_op jit(solution)/shard_map/ppermute | solution.py:18
  80.3 12.6 %collective-permute-start.5 = (bf16[64,4096]{1,0:T(8,128)(2,1)S(1)}, bf16[64,4096]{1,0:T(8,128)(2,1)S(1)}, u32[]{:S(2)}, u32[]{:S(2)}) collective-permute-start(bf16[64,4096]{1,0:T(8,128)(2,1)S(1)} %get-tuple-element.26), channel_id=1, source_target_pairs={{0,4},{4,0},{8,12},{12,8},{1,5},{5,1},{9,13},{13,9},{2,6},{6,2},{1... | collective-permute-start | bytes 1572872 | tf_op jit(solution)/shard_map/ppermute | solution.py:18
  92.4 2.0 %collective-permute-start.18 = (bf16[64,4096]{1,0:T(8,128)(2,1)S(1)}, bf16[64,4096]{1,0:T(8,128)(2,1)S(1)}, u32[]{:S(2)}, u32[]{:S(2)}) collective-permute-start(bf16[64,4096]{1,0:T(8,128)(2,1)S(1)} %slice.98), channel_id=1, source_target_pairs={{0,4},{4,0},{8,12},{12,8},{1,5},{5,1},{9,13},{13,9},{2,6},{6,2},{1... | collective-permute-start | bytes 1572872 | tf_op jit(solution)/shard_map/ppermute | solution.py:18
  103.2 2.0 %collective-permute-start.19 = (bf16[64,2304]{1,0:T(8,128)(2,1)S(1)}, bf16[64,2304]{1,0:T(8,128)(2,1)S(1)}, u32[]{:S(2)}, u32[]{:S(2)}) collective-permute-start(bf16[64,2304]{1,0:T(8,128)(2,1)S(1)} %fusion.18), channel_id=1, source_target_pairs={{0,4},{4,0},{8,12},{12,8},{1,5},{5,1},{9,13},{13,9},{2,6},{6,2},{1... | collective-permute-start | bytes 884744 | tf_op jit(solution)/shard_map/ppermute | solution.py:18
  103.7 9.2 %collective-permute-start.21 = (bf16[32,4096]{1,0:T(8,128)(2,1)S(1)}, bf16[32,4096]{1,0:T(8,128)(2,1)S(1)}, u32[]{:S(2)}, u32[]{:S(2)}) collective-permute-start(bf16[32,4096]{1,0:T(8,128)(2,1)S(1)} %slice.99), channel_id=1, source_target_pairs={{0,8},{4,12},{8,0},{12,4},{1,9},{5,13},{9,1},{13,5},{2,10},{6,14},... | collective-permute-start | bytes 786440 | tf_op jit(solution)/shard_map/ppermute | solution.py:18
  105.4 9.9 %collective-permute-start.20 = (bf16[32,2304]{1,0:T(8,128)(2,1)S(1)}, bf16[32,2304]{1,0:T(8,128)(2,1)S(1)}, u32[]{:S(2)}, u32[]{:S(2)}) collective-permute-start(bf16[32,2304]{1,0:T(8,128)(2,1)S(1)} %slice.100), channel_id=1, source_target_pairs={{0,8},{4,12},{8,0},{12,4},{1,9},{5,13},{9,1},{13,5},{2,10},{6,14},... | collective-permute-start | bytes 442376 | tf_op jit(solution)/shard_map/ppermute | solution.py:18

commit v3 on v2

--- a/solution.py
+++ b/solution.py
@@ -55,57 +55,62 @@
         pair = partial[: 2 * rows] + flip(give.astype(jnp.bfloat16), "gx", 1).astype(jnp.float32)
         return pair, pair[:rows] + flip(pair[rows:].astype(jnp.bfloat16), "gx", 2).astype(jnp.float32)
 
-    def sum_over_gy(value):
-        if not square:
-            return lax.psum(value, "gy")
-        value = value + flip(value, "gy", 1)
-        return value + flip(value, "gy", 2)
-
     def local(layer_input, attn_context, ffn_hidden, norm_gain, w_query, w_keyval, w_out, w_down):
         rows, feat_width = layer_input.shape
         model_width = norm_gain.shape[0]
 
         input_float = layer_input.astype(jnp.float32)
-        row_sums = sum_over_gy(jnp.sum(input_float * input_float, axis=1))
-        scale = lax.rsqrt(row_sums / model_width + norm_epsilon)
         gain = lax.dynamic_slice_in_dim(norm_gain, lax.axis_index("gy") * feat_width, feat_width)
-        normed = (input_float * scale[:, None] * gain).astype(jnp.bfloat16)
+        own_sums = jnp.sum(input_float * input_float, axis=1)
+
+        def normalise(row_sums):
+            scale = lax.rsqrt(row_sums / model_width + norm_epsilon)
+            return (input_float * scale[:, None] * gain).astype(jnp.bfloat16)
 
         if square:
             half = ffn_hidden.shape[1] // 2
             first, second = ffn_hidden[:, :half], ffn_hidden[:, half:]
             context, first = over_z(attn_context), over_z(first)
+            sums = own_sums + flip(own_sums, "gy", 1)
             second = over_z(after(second, context[1]))
+            sums = sums + flip(after(sums, context[1]), "gy", 2)
             context = over_x(context)
-            normed = over_z(normed)
+            normed = normalise(sums)
+            ready_norm = normed
+            normed = over_z(after(normed, first[1]))
             first = over_x(first)
-            context = over_near_z(context)
-            context = over_cores(context)
+            context = over_cores(over_near_z(context))
+            arrived = first[1]
             first = over_near_z(first)
-            second = over_x(second)
-            ready = jnp.concatenate(after(context, normed[1]))
-            block_part = dot(ready, w_out)
-            first = over_cores(first)
-            normed = over_x(normed)
+            block_part = dot(jnp.concatenate(after(context, arrived, ready_norm)), w_out)
+            second = over_x(after(second, block_part))
+            normed = over_x(after(normed, block_part))
+            arrived = second[1]
             second = over_near_z(second)
-            ready = jnp.concatenate(after(first, block_part))
-            block_part += dot(ready, w_down[:half])
+            first = over_cores(after(first, arrived))
+            block_part += dot(jnp.concatenate(after(first, arrived)), w_down[:half])
+            normed = over_near_z(after(normed, block_part))
             second = over_cores(after(second, block_part))
-            normed = over_near_z(normed)
-            ready = jnp.concatenate(after(second, block_part))
-            block_part += dot(ready, w_down[half:])
-            normed = jnp.concatenate(over_cores(normed))
-            normed = after(normed, block_part)
+            block_part += dot(jnp.concatenate(second), w_down[half:])
+            normed = jnp.concatenate(over_cores(after(normed, block_part)))
         else:
-            context, hidden, normed = gather_plain(attn_context), gather_plain(ffn_hidden), gather_plain(normed)
+            normed = gather_plain(normalise(lax.psum(own_sums, "gy")))
+            context, hidden = gather_plain(attn_context), gather_plain(ffn_hidden)
             block_part = dot(context, w_out) + dot(hidden, w_down)
         paired, block_sum = sum_over_gx(block_part, rows)
         normed = after(normed, paired)
 
-        query_part, keyval_part = dot(normed, w_query), dot(normed, w_keyval)
-        heads = sum_over_gx(jnp.concatenate([query_part, keyval_part], axis=1), rows)[1].astype(jnp.bfloat16)
-        split = w_query.shape[1]
-        return (heads[:, :split], heads[:, split:], (input_float + block_sum).astype(jnp.bfloat16))
+        pieces = 2 if square else 1
+        width = w_query.shape[1] // pieces
+        heads = []
+        for i in range(pieces):
+            columns = dot(normed, w_query[:, i * width : (i + 1) * width])
+            if i == 0:
+                columns = jnp.concatenate([columns, dot(normed, w_keyval)], axis=1)
+                normed = after(normed, columns, block_sum)
+            heads.append(sum_over_gx(columns, rows)[1].astype(jnp.bfloat16))
+        queries = jnp.concatenate([heads[0][:, :width], *heads[1:]], axis=1)
+        return (queries, heads[0][:, width:], (input_float + block_sum).astype(jnp.bfloat16))
 
     return jax.shard_map(
         local,

time: 117 us -> 104 us (0.89)
  waiting for transfers between devices: 42.6 us -> 24.9 us
  starting transfers between devices: 24.7 us -> 30.5 us
    ppermute x22 -> x24, waiting for transfers between devices: 42.6 us -> 24.9 us  [flip(): lax.ppermute(value, axis, [(i, i ^ bit) for i in range(lax.axis_size(axis...]
    ppermute x22 -> x24, starting transfers between devices: 24.7 us -> 30.5 us  [flip(): lax.ppermute(value, axis, [(i, i ^ bit) for i in range(lax.axis_size(axis...]
    dot_general x5 -> x6, matrix products: 40.1 us -> 39.6 us  [dot(): return jnp.dot(left, right, preferred_element_type=jnp.float32)]
  transfers between devices with their start and end apart: 22 -> 24, of which waited for: 12 -> 13; matrix products, arithmetic and copies ran while one was open for 32% -> 45% of each run, Pallas kernels for 0% -> 0%
where the time goes in v3:
time: 104 us
  matrix products  39.6 us (38%)
  starting transfers between devices  30.5 us (29%)
  waiting for transfers between devices  24.9 us (24%)
  other arithmetic  5.38 us (5%)
  local copies, waits for them, and re-layouts  2.46 us (2%)
    dot_general x6, matrix products, dot(): return jnp.dot(left, right, preferred_element_type=jnp.float32)  39.6 us
    ppermute x24, starting transfers between devices, flip(): lax.ppermute(value, axis, [(i, i ^ bit) for i in range(lax.axis_size(axis...  30.5 us
    ppermute x24, waiting for transfers between devices, flip(): lax.ppermute(value, axis, [(i, i ^ bit) for i in range(lax.axis_size(axis...  24.9 us
  transfers between devices with their start and end apart: 24, of which 13 were waited for; matrix products, arithmetic and copies ran while one was open for 45% of the time, Pallas kernels for 0%

profile of v3, /device:TPU:0, one launch (start us, length us, event | category | flops | bytes accessed | tf_op | source)
XLA Modules:
  0.0 103.9 jit_solution(16310672043591002338)
XLA Ops:
  0.7 4.1 %collective-permute-start.1 = (bf16[32,2048]{1,0:T(8,128)(2,1)}, bf16[32,2048]{1,0:T(8,128)(2,1)S(1)}, u32[]{:S(2)}, u32[]{:S(2)}) collective-permute-start(bf16[32,2048]{1,0:T(8,128)(2,1)} %param.9), channel_id=1, source_target_pairs={{0,2},{1,3},{2,0},{3,1},{4,6},{5,7},{6,4},{7,5},{8,10},{9,11},{10,... | collective-permute-start | bytes 393224 | tf_op jit(solution)/shard_map/ppermute | solution.py:18
  4.8 1.1 %fusion.20 = f32[32]{0:T(128)S(1)} fusion(bf16[32,4096]{1,0:T(8,128)(2,1)} %param.8), kind=kLoop, calls=%fused_computation.27 | loop fusion | flops 393184 | bytes 262272 | tf_op jit(solution)/shard_map/reduce_sum | solution.py:64
  5.9 1.6 %collective-permute-start = (f32[32]{0:T(128)S(1)}, f32[32]{0:T(128)S(1)}, u32[]{:S(2)}, u32[]{:S(2)}) collective-permute-start(f32[32]{0:T(128)S(1)} %fusion.20), channel_id=1, source_target_pairs={{0,1},{1,0},{2,3},{3,2},{4,5},{5,4},{6,7},{7,6},{8,9},{9,8},{10,11... | collective-permute-start | bytes 392 | tf_op jit(solution)/shard_map/ppermute | solution.py:18
  7.5 0.9 slice.66
  8.5 0.4 collective-permute-start.3
  8.9 0.7 dynamic_slice.3
  9.6 1.7 %collective-permute-done.1 = bf16[32,2048]{1,0:T(8,128)(2,1)S(1)} collective-permute-done((bf16[32,2048]{1,0:T(8,128)(2,1)}, bf16[32,2048]{1,0:T(8,128)(2,1)S(1)}, u32[]{:S(2)}, u32[]{:S(2)}) %collective-permute-start.1) | collective-permute-done | bytes 131104 | tf_op jit(solution)/shard_map/ppermute | solution.py:18
  11.3 1.0 collective-permute-start.2
  12.2 0.9 broadcast_select_fusion.15
  13.2 5.2 %collective-permute-start.5 = (bf16[32,2048]{1,0:T(8,128)(2,1)S(1)}, bf16[32,2048]{1,0:T(8,128)(2,1)S(1)}, u32[]{:S(2)}, u32[]{:S(2)}) collective-permute-start(bf16[32,2048]{1,0:T(8,128)(2,1)S(1)} %get-tuple-element.63), channel_id=1, source_target_pairs={{0,8},{4,12},{8,0},{12,4},{1,9},{5,13},{9,1},{13,5},{2,10},{6,14},... | collective-permute-start | bytes 393224 | tf_op jit(solution)/shard_map/ppermute | solution.py:18
  18.4 2.1 %collective-permute-done.2 = f32[32]{0:T(128)S(1)} collective-permute-done((f32[32]{0:T(128)S(1)}, f32[32]{0:T(128)S(1)}, u32[]{:S(2)}, u32[]{:S(2)}) %collective-permute-start.2) | collective-permute-done | bytes 160 | tf_op jit(solution)/shard_map/ppermute | solution.py:18
  20.5 1.1 %fusion.22 = bf16[32,4096]{1,0:T(8,128)(2,1)S(1)} fusion(bf16[32,4096]{1,0:T(8,128)(2,1)} %param.8, f32[4096]{0:T(1024)S(1)} %dynamic_slice.3, f32[32]{0:T(128)S(1)} %add_rsqrt_fusion), kind=kLoop, calls=%fused_computation.29 | loop fusion | flops 524288 | bytes 540800 | tf_op jit(solution)/shard_map/convert_element_type | solution.py:68
  21.6 0.9 collective-permute-start.4
  22.5 3.7 %collective-permute-start.6 = (bf16[64,2048]{1,0:T(8,128)(2,1)S(1)}, bf16[64,2048]{1,0:T(8,128)(2,1)S(1)}, u32[]{:S(2)}, u32[]{:S(2)}) collective-permute-start(bf16[64,2048]{1,0:T(8,128)(2,1)S(1)} %pad_maximum_fusion.4), channel_id=1, source_target_pairs={{0,1},{1,0},{2,3},{3,2},{4,5},{5,4},{6,7},{7,6},{8,9},{9,8},{10,11... | collective-permute-start | bytes 786440 | tf_op jit(solution)/shard_map/ppermute | solution.py:18
  26.2 1.6 %collective-permute-start.8 = (bf16[32,3328]{1,0:T(8,128)(2,1)S(1)}, bf16[32,3328]{1,0:T(8,128)(2,1)S(1)}, u32[]{:S(2)}, u32[]{:S(2)}) collective-permute-start(bf16[32,3328]{1,0:T(8,128)(2,1)S(1)} %get-tuple-element.54), channel_id=1, source_target_pairs={{0,8},{4,12},{8,0},{12,4},{1,9},{5,13},{9,1},{13,5},{2,10},{6,14},... | collective-permute-start | bytes 638984 | tf_op jit(solution)/shard_map/ppermute | solution.py:18
  27.8 0.3 collective-permute-start.11
  28.1 8.0 %collective-permute-done.6 = bf16[64,2048]{1,0:T(8,128)(2,1)S(1)} collective-permute-done((bf16[64,2048]{1,0:T(8,128)(2,1)S(1)}, bf16[64,2048]{1,0:T(8,128)(2,1)S(1)}, u32[]{:S(2)}, u32[]{:S(2)}) %collective-permute-start.6) | collective-permute-done | bytes 262176 | tf_op jit(solution)/shard_map/ppermute | solution.py:18
  36.1 0.1 broadcast_select_fusion.6
  36.3 1.3 %collective-permute-start.10 = (bf16[64,3328]{1,0:T(8,128)(2,1)S(1)}, bf16[64,3328]{1,0:T(8,128)(2,1)S(1)}, u32[]{:S(2)}, u32[]{:S(2)}) collective-permute-start(bf16[64,3328]{1,0:T(8,128)(2,1)S(1)} %pad_maximum_fusion.2), channel_id=1, source_target_pairs={{0,1},{1,0},{2,3},{3,2},{4,5},{5,4},{6,7},{7,6},{8,9},{9,8},{10,11... | collective-permute-start | bytes 1277960 | tf_op jit(solution)/shard_map/ppermute | solution.py:18
  37.7 0.1 collective-permute-done.7
  37.8 8.1 %fusion.24 = f32[128,4096]{1,0:T(8,128)S(1)} fusion(bf16[2048,4096]{1,0:T(8,128)(2,1)} %param.14, bf16[64,2048]{1,0:T(8,128)(2,1)S(1)} %collective-permute-done.7, bf16[64,2048]{1,0:T(8,128)(2,1)S(1)} %get-tuple-element.26), kind=kOutput, calls=%fused_computation.33 | convolution fusion | flops 2148532224 | bytes 19398656 | tf_op jit(solution)/shard_map/dot_general | solution.py:14
  46.0 2.5 %collective-permute-start.12 = (bf16[32,3328]{1,0:T(8,128)(2,1)S(1)}, bf16[32,3328]{1,0:T(8,128)(2,1)S(1)}, u32[]{:S(2)}, u32[]{:S(2)}) collective-permute-start(bf16[32,3328]{1,0:T(8,128)(2,1)S(1)} %get-tuple-element.60), channel_id=1, source_target_pairs={{0,8},{4,12},{8,0},{12,4},{1,9},{5,13},{9,1},{13,5},{2,10},{6,14},... | collective-permute-start | bytes 638984 | tf_op jit(solution)/shard_map/ppermute | solution.py:18
  48.6 3.6 %collective-permute-done.10 = bf16[64,3328]{1,0:T(8,128)(2,1)S(1)} collective-permute-done((bf16[64,3328]{1,0:T(8,128)(2,1)S(1)}, bf16[64,3328]{1,0:T(8,128)(2,1)S(1)}, u32[]{:S(2)}, u32[]{:S(2)}) %collective-permute-start.10) | collective-permute-done | bytes 426016 | tf_op jit(solution)/shard_map/ppermute | solution.py:18
  52.2 2.3 %collective-permute-done.12 = bf16[32,3328]{1,0:T(8,128)(2,1)S(1)} collective-permute-done((bf16[32,3328]{1,0:T(8,128)(2,1)S(1)}, bf16[32,3328]{1,0:T(8,128)(2,1)S(1)}, u32[]{:S(2)}, u32[]{:S(2)}) %collective-permute-start.12) | collective-permute-done | bytes 213024 | tf_op jit(solution)/shard_map/ppermute | solution.py:18
  54.7 1.0 collective-permute-start.15
  55.7 0.8 collective-permute-done.13
  56.4 10.9 %fusion.8 = f32[128,4096]{1,0:T(8,128)S(1)} fusion(f32[128,4096]{1,0:T(8,128)S(1)} %fusion.24, bf16[6656,4096]{1,0:T(8,128)(2,1)} %param.15, bf16[64,3328]{1,0:T(8,128)(2,1)S(1)} %collective-permute-done.13, bf16[64,3328]{1,0:T(8,128)(2,1)S(1)} %get-tuple-element.35), kind=kOutput, calls=%fused_computation.8 | convolution fusion | flops 3491889152 | bytes 32309248 | tf_op jit(solution)/shard_map/dot_general | solution.py:14
  67.4 0.2 collective-permute-start.16
  67.6 1.0 collective-permute-start.14
  68.6 0.7 collective-permute-done.16
  69.2 10.9 %fusion.11 = f32[128,4096]{1,0:T(8,128)S(1)} fusion(f32[128,4096]{1,0:T(8,128)S(1)} %fusion.8, bf16[6656,4096]{1,0:T(8,128)(2,1)} %param.15, bf16[64,3328]{1,0:T(8,128)(2,1)S(1)} %collective-permute-done.16, bf16[64,3328]{1,0:T(8,128)(2,1)S(1)} %get-tuple-element.49), kind=kOutput, calls=%fused_computation.9 | convolution fusion | flops 3491889152 | bytes 32309248 | tf_op jit(solution)/shard_map/dot_general | solution.py:14
  80.2 0.2 collective-permute-start.18
  80.4 1.5 %collective-permute-done.14 = bf16[64,4096]{1,0:T(8,128)(2,1)S(1)} collective-permute-done((bf16[64,4096]{1,0:T(8,128)(2,1)S(1)}, bf16[64,4096]{1,0:T(8,128)(2,1)S(1)}, u32[]{:S(2)}, u32[]{:S(2)}) %collective-permute-start.14) | collective-permute-done | bytes 524320 | tf_op jit(solution)/shard_map/ppermute | solution.py:18
  82.1 0.1 collective-permute-done.18
  82.2 0.1 slice_add_fusion
  82.4 2.1 %collective-permute-start.21 = (bf16[32,4096]{1,0:T(8,128)(2,1)S(1)}, bf16[32,4096]{1,0:T(8,128)(2,1)S(1)}, u32[]{:S(2)}, u32[]{:S(2)}) collective-permute-start(bf16[32,4096]{1,0:T(8,128)(2,1)S(1)} %slice.147), channel_id=1, source_target_pairs={{0,8},{4,12},{8,0},{12,4},{1,9},{5,13},{9,1},{13,5},{2,10},{6,14},... | collective-permute-start | bytes 786440 | tf_op jit(solution)/shard_map/ppermute | solution.py:18
  84.6 4.6 %fusion.6 = f32[128,1024]{1,0:T(8,128)S(1)} fusion(bf16[128,4096]{1,0:T(8,128)(2,1)S(1)} %pad_maximum_fusion.1, bf16[4096,2048]{1,0:T(8,128)(2,1)} %param.12), kind=kOutput, calls=%fused_computation.6 | convolution fusion | flops 1073741824 | bytes 9961472 | tf_op jit(solution)/shard_map/dot_general | solution.py:14
  89.2 0.4 fusion.37
  89.7 0.1 collective-permute-start.19
  89.9 1.4 %collective-permute-done.21 = bf16[32,4096]{1,0:T(8,128)(2,1)S(1)} collective-permute-done((bf16[32,4096]{1,0:T(8,128)(2,1)S(1)}, bf16[32,4096]{1,0:T(8,128)(2,1)S(1)}, u32[]{:S(2)}, u32[]{:S(2)}) %collective-permute-start.21) | collective-permute-done | bytes 262176 | tf_op jit(solution)/shard_map/ppermute | solution.py:18
  91.3 0.8 fusion.23
  92.1 4.6 %fusion.4 = f32[128,1024]{1,0:T(8,128)S(1)} fusion(bf16[128,4096]{1,0:T(8,128)(2,1)S(1)} %pad_maximum_fusion.1, bf16[4096,2048]{1,0:T(8,128)(2,1)} %param.12), kind=kOutput, calls=%fused_computation.4 | convolution fusion | flops 1073741824 | bytes 9961472 | tf_op jit(solution)/shard_map/dot_general | solution.py:14
  96.9 1.8 %collective-permute-start.20 = (bf16[32,1280]{1,0:T(8,128)(2,1)S(1)}, bf16[32,1280]{1,0:T(8,128)(2,1)S(1)}, u32[]{:S(2)}, u32[]{:S(2)}) collective-permute-start(bf16[32,1280]{1,0:T(8,128)(2,1)S(1)} %slice.149), channel_id=1, source_target_pairs={{0,8},{4,12},{8,0},{12,4},{1,9},{5,13},{9,1},{13,5},{2,10},{6,14},... | collective-permute-start | bytes 245768 | tf_op jit(solution)/shard_map/ppermute | solution.py:18
  98.8 1.3 %collective-permute-start.23 = (bf16[32,1024]{1,0:T(8,128)(2,1)S(1)}, bf16[32,1024]{1,0:T(8,128)(2,1)S(1)}, u32[]{:S(2)}, u32[]{:S(2)}) collective-permute-start(bf16[32,1024]{1,0:T(8,128)(2,1)S(1)} %slice.150), channel_id=1, source_target_pairs={{0,8},{4,12},{8,0},{12,4},{1,9},{5,13},{9,1},{13,5},{2,10},{6,14},... | collective-permute-start | bytes 196616 | tf_op jit(solution)/shard_map/ppermute | solution.py:18
  100.0 1.9 %collective-permute-done.20 = bf16[32,1280]{1,0:T(8,128)(2,1)S(1)} collective-permute-done((bf16[32,1280]{1,0:T(8,128)(2,1)S(1)}, bf16[32,1280]{1,0:T(8,128)(2,1)S(1)}, u32[]{:S(2)}, u32[]{:S(2)}) %collective-permute-start.20) | collective-permute-done | bytes 81952 | tf_op jit(solution)/shard_map/ppermute | solution.py:18
  102.0 0.6 slice.101
  102.6 0.6 collective-permute-done.23
  103.2 0.7 pad_maximum_fusion.5
  (47 shorter events, 1.2 us)
Async XLA Ops:
  0.6 88.6 %copy-start = (bf16[4096,256]{1,0:T(8,128)(2,1)S(1)}, bf16[4096,256]{1,0:T(8,128)(2,1)}, u32[]{:S(2)}) copy-start(bf16[4096,256]{1,0:T(8,128)(2,1)} %param.13) | copy-start | bytes 6291460
  0.6 25.5 %copy-start.2 = (bf16[32,6656]{1,0:T(8,128)(2,1)S(1)}, bf16[32,6656]{1,0:T(8,128)(2,1)}, u32[]{:S(2)}) copy-start(bf16[32,6656]{1,0:T(8,128)(2,1)} %param.10) | copy-start | bytes 1277956
  0.7 10.6 %collective-permute-start.1 = (bf16[32,2048]{1,0:T(8,128)(2,1)}, bf16[32,2048]{1,0:T(8,128)(2,1)S(1)}, u32[]{:S(2)}, u32[]{:S(2)}) collective-permute-start(bf16[32,2048]{1,0:T(8,128)(2,1)} %param.9), channel_id=1, source_target_pairs={{0,2},{1,3},{2,0},{3,1},{4,6},{5,7},{6,4},{7,5},{8,10},{9,11},{10,... | collective-permute-start | bytes 393224 | tf_op jit(solution)/shard_map/ppermute | solution.py:18
  5.9 3.7 %collective-permute-start = (f32[32]{0:T(128)S(1)}, f32[32]{0:T(128)S(1)}, u32[]{:S(2)}, u32[]{:S(2)}) collective-permute-start(f32[32]{0:T(128)S(1)} %fusion.20), channel_id=1, source_target_pairs={{0,1},{1,0},{2,3},{3,2},{4,5},{5,4},{6,7},{7,6},{8,9},{9,8},{10,11... | collective-permute-start | bytes 392 | tf_op jit(solution)/shard_map/ppermute | solution.py:18
  8.5 13.1 %collective-permute-start.3 = (bf16[32,3328]{1,0:T(8,128)(2,1)S(1)}, bf16[32,3328]{1,0:T(8,128)(2,1)S(1)}, u32[]{:S(2)}, u32[]{:S(2)}) collective-permute-start(bf16[32,3328]{1,0:T(8,128)(2,1)S(1)} %slice.66), channel_id=1, source_target_pairs={{0,2},{1,3},{2,0},{3,1},{4,6},{5,7},{6,4},{7,5},{8,10},{9,11},{10,... | collective-permute-start | bytes 638984 | tf_op jit(solution)/shard_map/ppermute | solution.py:18
  11.3 9.2 %collective-permute-start.2 = (f32[32]{0:T(128)S(1)}, f32[32]{0:T(128)S(1)}, u32[]{:S(2)}, u32[]{:S(2)}) collective-permute-start(f32[32]{0:T(128)S(1)} %add.59), channel_id=1, source_target_pairs={{0,2},{1,3},{2,0},{3,1},{4,6},{5,7},{6,4},{7,5},{8,10},{9,11},{10,... | collective-permute-start | bytes 392 | tf_op jit(solution)/shard_map/ppermute | solution.py:18
  13.2 9.3 %collective-permute-start.5 = (bf16[32,2048]{1,0:T(8,128)(2,1)S(1)}, bf16[32,2048]{1,0:T(8,128)(2,1)S(1)}, u32[]{:S(2)}, u32[]{:S(2)}) collective-permute-start(bf16[32,2048]{1,0:T(8,128)(2,1)S(1)} %get-tuple-element.63), channel_id=1, source_target_pairs={{0,8},{4,12},{8,0},{12,4},{1,9},{5,13},{9,1},{13,5},{2,10},{6,14},... | collective-permute-start | bytes 393224 | tf_op jit(solution)/shard_map/ppermute | solution.py:18
  21.6 24.4 %collective-permute-start.4 = (bf16[32,4096]{1,0:T(8,128)(2,1)S(1)}, bf16[32,4096]{1,0:T(8,128)(2,1)S(1)}, u32[]{:S(2)}, u32[]{:S(2)}) collective-permute-start(bf16[32,4096]{1,0:T(8,128)(2,1)S(1)} %fusion.22), channel_id=1, source_target_pairs={{0,2},{1,3},{2,0},{3,1},{4,6},{5,7},{6,4},{7,5},{8,10},{9,11},{10,... | collective-permute-start | bytes 786440 | tf_op jit(solution)/shard_map/ppermute | solution.py:18
  22.5 13.6 %collective-permute-start.6 = (bf16[64,2048]{1,0:T(8,128)(2,1)S(1)}, bf16[64,2048]{1,0:T(8,128)(2,1)S(1)}, u32[]{:S(2)}, u32[]{:S(2)}) collective-permute-start(bf16[64,2048]{1,0:T(8,128)(2,1)S(1)} %pad_maximum_fusion.4), channel_id=1, source_target_pairs={{0,1},{1,0},{2,3},{3,2},{4,5},{5,4},{6,7},{7,6},{8,9},{9,8},{10,11... | collective-permute-start | bytes 786440 | tf_op jit(solution)/shard_map/ppermute | solution.py:18
  26.2 10.0 %collective-permute-start.8 = (bf16[32,3328]{1,0:T(8,128)(2,1)S(1)}, bf16[32,3328]{1,0:T(8,128)(2,1)S(1)}, u32[]{:S(2)}, u32[]{:S(2)}) collective-permute-start(bf16[32,3328]{1,0:T(8,128)(2,1)S(1)} %get-tuple-element.54), channel_id=1, source_target_pairs={{0,8},{4,12},{8,0},{12,4},{1,9},{5,13},{9,1},{13,5},{2,10},{6,14},... | collective-permute-start | bytes 638984 | tf_op jit(solution)/shard_map/ppermute | solution.py:18
  27.8 18.2 %collective-permute-start.11 = (bf16[32,3328]{1,0:T(8,128)(2,1)S(1)}, bf16[32,3328]{1,0:T(8,128)(2,1)S(1)}, u32[]{:S(2)}, u32[]{:S(2)}) collective-permute-start(bf16[32,3328]{1,0:T(8,128)(2,1)S(1)} %get-tuple-element.32), channel_id=1, source_target_pairs={{0,2},{1,3},{2,0},{3,1},{4,6},{5,7},{6,4},{7,5},{8,10},{9,11},{10,... | collective-permute-start | bytes 638984 | tf_op jit(solution)/shard_map/ppermute | solution.py:18
  36.2 1.6 %collective-permute-start.7 = (bf16[64,2048]{1,0:T(8,128)(2,1)S(1)}, bf16[64,2048]{1,0:T(8,128)(2,1)S(1)}, u32[]{:S(2)}, u32[]{:S(2)}) collective-permute-start(bf16[64,2048]{1,0:T(8,128)(2,1)S(1)} %get-tuple-element.57), channel_id=1, source_target_pairs={{0,4},{4,0},{8,12},{12,8},{1,5},{5,1},{9,13},{13,9},{2,6},{6,2},{1... | collective-permute-start | bytes 786440 | tf_op jit(solution)/shard_map/ppermute | solution.py:18
  36.3 15.9 %collective-permute-start.10 = (bf16[64,3328]{1,0:T(8,128)(2,1)S(1)}, bf16[64,3328]{1,0:T(8,128)(2,1)S(1)}, u32[]{:S(2)}, u32[]{:S(2)}) collective-permute-start(bf16[64,3328]{1,0:T(8,128)(2,1)S(1)} %pad_maximum_fusion.2), channel_id=1, source_target_pairs={{0,1},{1,0},{2,3},{3,2},{4,5},{5,4},{6,7},{7,6},{8,9},{9,8},{10,11... | collective-permute-start | bytes 1277960 | tf_op jit(solution)/shard_map/ppermute | solution.py:18
  46.0 8.5 %collective-permute-start.12 = (bf16[32,3328]{1,0:T(8,128)(2,1)S(1)}, bf16[32,3328]{1,0:T(8,128)(2,1)S(1)}, u32[]{:S(2)}, u32[]{:S(2)}) collective-permute-start(bf16[32,3328]{1,0:T(8,128)(2,1)S(1)} %get-tuple-element.60), channel_id=1, source_target_pairs={{0,8},{4,12},{8,0},{12,4},{1,9},{5,13},{9,1},{13,5},{2,10},{6,14},... | collective-permute-start | bytes 638984 | tf_op jit(solution)/shard_map/ppermute | solution.py:18
  48.5 18.8 %collective-permute-start.9 = (bf16[32,4096]{1,0:T(8,128)(2,1)S(1)}, bf16[32,4096]{1,0:T(8,128)(2,1)S(1)}, u32[]{:S(2)}, u32[]{:S(2)}) collective-permute-start(bf16[32,4096]{1,0:T(8,128)(2,1)S(1)} %get-tuple-element.55), channel_id=1, source_target_pairs={{0,8},{4,12},{8,0},{12,4},{1,9},{5,13},{9,1},{13,5},{2,10},{6,14},... | collective-permute-start | bytes 786440 | tf_op jit(solution)/shard_map/ppermute | solution.py:18
  54.6 1.8 %collective-permute-start.13 = (bf16[64,3328]{1,0:T(8,128)(2,1)S(1)}, bf16[64,3328]{1,0:T(8,128)(2,1)S(1)}, u32[]{:S(2)}, u32[]{:S(2)}) collective-permute-start(bf16[64,3328]{1,0:T(8,128)(2,1)S(1)} %get-tuple-element.51), channel_id=1, source_target_pairs={{0,4},{4,0},{8,12},{12,8},{1,5},{5,1},{9,13},{13,9},{2,6},{6,2},{1... | collective-permute-start | bytes 1277960 | tf_op jit(solution)/shard_map/ppermute | solution.py:18
  54.7 12.6 %collective-permute-start.15 = (bf16[64,3328]{1,0:T(8,128)(2,1)S(1)}, bf16[64,3328]{1,0:T(8,128)(2,1)S(1)}, u32[]{:S(2)}, u32[]{:S(2)}) collective-permute-start(bf16[64,3328]{1,0:T(8,128)(2,1)S(1)} %pad_maximum_fusion.3), channel_id=1, source_target_pairs={{0,1},{1,0},{2,3},{3,2},{4,5},{5,4},{6,7},{7,6},{8,9},{9,8},{10,11... | collective-permute-start | bytes 1277960 | tf_op jit(solution)/shard_map/ppermute | solution.py:18
  67.4 1.8 %collective-permute-start.16 = (bf16[64,3328]{1,0:T(8,128)(2,1)S(1)}, bf16[64,3328]{1,0:T(8,128)(2,1)S(1)}, u32[]{:S(2)}, u32[]{:S(2)}) collective-permute-start(bf16[64,3328]{1,0:T(8,128)(2,1)S(1)} %get-tuple-element.50), channel_id=1, source_target_pairs={{0,4},{4,0},{8,12},{12,8},{1,5},{5,1},{9,13},{13,9},{2,6},{6,2},{1... | collective-permute-start | bytes 1277960 | tf_op jit(solution)/shard_map/ppermute | solution.py:18
  67.6 14.3 %collective-permute-start.14 = (bf16[64,4096]{1,0:T(8,128)(2,1)S(1)}, bf16[64,4096]{1,0:T(8,128)(2,1)S(1)}, u32[]{:S(2)}, u32[]{:S(2)}) collective-permute-start(bf16[64,4096]{1,0:T(8,128)(2,1)S(1)} %constant_dynamic-update-slice_fusion), channel_id=1, source_target_pairs={{0,1},{1,0},{2,3},{3,2},{4,5},{5,4},{6,7},{7,6},{8,9},{9,8},{10,11... | collective-permute-start | bytes 1572872 | tf_op jit(solution)/shard_map/ppermute | solution.py:18
  80.2 2.0 %collective-permute-start.18 = (bf16[64,4096]{1,0:T(8,128)(2,1)S(1)}, bf16[64,4096]{1,0:T(8,128)(2,1)S(1)}, u32[]{:S(2)}, u32[]{:S(2)}) collective-permute-start(bf16[64,4096]{1,0:T(8,128)(2,1)S(1)} %slice.146), channel_id=1, source_target_pairs={{0,4},{4,0},{8,12},{12,8},{1,5},{5,1},{9,13},{13,9},{2,6},{6,2},{1... | collective-permute-start | bytes 1572872 | tf_op jit(solution)/shard_map/ppermute | solution.py:18
  82.0 2.5 %collective-permute-start.17 = (bf16[64,4096]{1,0:T(8,128)(2,1)S(1)}, bf16[64,4096]{1,0:T(8,128)(2,1)S(1)}, u32[]{:S(2)}, u32[]{:S(2)}) collective-permute-start(bf16[64,4096]{1,0:T(8,128)(2,1)S(1)} %get-tuple-element.48), channel_id=1, source_target_pairs={{0,4},{4,0},{8,12},{12,8},{1,5},{5,1},{9,13},{13,9},{2,6},{6,2},{1... | collective-permute-start | bytes 1572872 | tf_op jit(solution)/shard_map/ppermute | solution.py:18
  82.4 8.9 %collective-permute-start.21 = (bf16[32,4096]{1,0:T(8,128)(2,1)S(1)}, bf16[32,4096]{1,0:T(8,128)(2,1)S(1)}, u32[]{:S(2)}, u32[]{:S(2)}) collective-permute-start(bf16[32,4096]{1,0:T(8,128)(2,1)S(1)} %slice.147), channel_id=1, source_target_pairs={{0,8},{4,12},{8,0},{12,4},{1,9},{5,13},{9,1},{13,5},{2,10},{6,14},... | collective-permute-start | bytes 786440 | tf_op jit(solution)/shard_map/ppermute | solution.py:18
  89.2 2.1 %copy-start.1 = (bf16[32,4096]{1,0:T(8,128)(2,1)S(1)}, bf16[32,4096]{1,0:T(8,128)(2,1)}, u32[]{:S(2)}) copy-start(bf16[32,4096]{1,0:T(8,128)(2,1)} %param.8) | copy-start | bytes 786436
  89.7 7.1 %collective-permute-start.19 = (bf16[64,1280]{1,0:T(8,128)(2,1)S(1)}, bf16[64,1280]{1,0:T(8,128)(2,1)S(1)}, u32[]{:S(2)}, u32[]{:S(2)}) collective-permute-start(bf16[64,1280]{1,0:T(8,128)(2,1)S(1)} %fusion.31), channel_id=1, source_target_pairs={{0,4},{4,0},{8,12},{12,8},{1,5},{5,1},{9,13},{13,9},{2,6},{6,2},{1... | collective-permute-start | bytes 491528 | tf_op jit(solution)/shard_map/ppermute | solution.py:18
  96.7 2.0 %collective-permute-start.22 = (bf16[64,1024]{1,0:T(8,128)(2,1)S(1)}, bf16[64,1024]{1,0:T(8,128)(2,1)S(1)}, u32[]{:S(2)}, u32[]{:S(2)}) collective-permute-start(bf16[64,1024]{1,0:T(8,128)(2,1)S(1)} %slice.148), channel_id=1, source_target_pairs={{0,4},{4,0},{8,12},{12,8},{1,5},{5,1},{9,13},{13,9},{2,6},{6,2},{1... | collective-permute-start | bytes 393224 | tf_op jit(solution)/shard_map/ppermute | solution.py:18
  96.9 5.1 %collective-permute-start.20 = (bf16[32,1280]{1,0:T(8,128)(2,1)S(1)}, bf16[32,1280]{1,0:T(8,128)(2,1)S(1)}, u32[]{:S(2)}, u32[]{:S(2)}) collective-permute-start(bf16[32,1280]{1,0:T(8,128)(2,1)S(1)} %slice.149), channel_id=1, source_target_pairs={{0,8},{4,12},{8,0},{12,4},{1,9},{5,13},{9,1},{13,5},{2,10},{6,14},... | collective-permute-start | bytes 245768 | tf_op jit(solution)/shard_map/ppermute | solution.py:18
  98.8 4.4 %collective-permute-start.23 = (bf16[32,1024]{1,0:T(8,128)(2,1)S(1)}, bf16[32,1024]{1,0:T(8,128)(2,1)S(1)}, u32[]{:S(2)}, u32[]{:S(2)}) collective-permute-start(bf16[32,1024]{1,0:T(8,128)(2,1)S(1)} %slice.150), channel_id=1, source_target_pairs={{0,8},{4,12},{8,0},{12,4},{1,9},{5,13},{9,1},{13,5},{2,10},{6,14},... | collective-permute-start | bytes 196616 | tf_op jit(solution)/shard_map/ppermute | solution.py:18

commit v4 on v3

--- a/solution.py
+++ b/solution.py
@@ -77,17 +77,18 @@
             context = over_x(context)
             normed = normalise(sums)
             ready_norm = normed
-            normed = over_z(after(normed, first[1]))
+            normed = over_z(after(normed, second[1]))
             first = over_x(first)
-            context = over_cores(over_near_z(context))
+            context = over_near_z(context)
             arrived = first[1]
             first = over_near_z(first)
-            block_part = dot(jnp.concatenate(after(context, arrived, ready_norm)), w_out)
-            second = over_x(after(second, block_part))
+            context = over_cores(context)
+            block_part = dot(jnp.concatenate(after(context, arrived, ready_norm, second[1])), w_out)
+            second = over_x(second)
             normed = over_x(after(normed, block_part))
             arrived = second[1]
             second = over_near_z(second)
-            first = over_cores(after(first, arrived))
+            first = over_cores(after(first, arrived, block_part))
             block_part += dot(jnp.concatenate(after(first, arrived)), w_down[:half])
             normed = over_near_z(after(normed, block_part))
             second = over_cores(after(second, block_part))

time: 104 us -> 102 us (0.981)
  starting transfers between devices: 30.5 us -> 29.3 us
    ppermute x24, starting transfers between devices: 30.5 us -> 29.3 us  [flip(): lax.ppermute(value, axis, [(i, i ^ bit) for i in range(lax.axis_size(axis...]
  transfers between devices with their start and end apart: 24 -> 24, of which waited for: 13 -> 12; matrix products, arithmetic and copies ran while one was open for 45% -> 46% of each run, Pallas kernels for 0% -> 0%
where the time goes in v4:
time: 102 us
  matrix products  39.6 us (39%)
  starting transfers between devices  29.3 us (29%)
  waiting for transfers between devices  24.2 us (24%)
  other arithmetic  5.37 us (5%)
  local copies, waits for them, and re-layouts  2.46 us (2%)
    dot_general x6, matrix products, dot(): return jnp.dot(left, right, preferred_element_type=jnp.float32)  39.6 us
    ppermute x24, starting transfers between devices, flip(): lax.ppermute(value, axis, [(i, i ^ bit) for i in range(lax.axis_size(axis...  29.3 us
    ppermute x24, waiting for transfers between devices, flip(): lax.ppermute(value, axis, [(i, i ^ bit) for i in range(lax.axis_size(axis...  24.2 us
  transfers between devices with their start and end apart: 24, of which 12 were waited for; matrix products, arithmetic and copies ran while one was open for 46% of the time, Pallas kernels for 0%

profile of v4, /device:TPU:0, one launch (start us, length us, event | category | flops | bytes accessed | tf_op | source)
XLA Modules:
  0.0 101.9 jit_solution(16027155587682702357)
XLA Ops:
  0.7 4.1 %collective-permute-start.1 = (bf16[32,2048]{1,0:T(8,128)(2,1)}, bf16[32,2048]{1,0:T(8,128)(2,1)S(1)}, u32[]{:S(2)}, u32[]{:S(2)}) collective-permute-start(bf16[32,2048]{1,0:T(8,128)(2,1)} %param.9), channel_id=1, source_target_pairs={{0,2},{1,3},{2,0},{3,1},{4,6},{5,7},{6,4},{7,5},{8,10},{9,11},{10,... | collective-permute-start | bytes 393224 | tf_op jit(solution)/shard_map/ppermute | solution.py:18
  4.8 1.1 %fusion.20 = f32[32]{0:T(128)S(1)} fusion(bf16[32,4096]{1,0:T(8,128)(2,1)} %param.8), kind=kLoop, calls=%fused_computation.27 | loop fusion | flops 393184 | bytes 262272 | tf_op jit(solution)/shard_map/reduce_sum | solution.py:64
  5.9 1.6 %collective-permute-start = (f32[32]{0:T(128)S(1)}, f32[32]{0:T(128)S(1)}, u32[]{:S(2)}, u32[]{:S(2)}) collective-permute-start(f32[32]{0:T(128)S(1)} %fusion.20), channel_id=1, source_target_pairs={{0,1},{1,0},{2,3},{3,2},{4,5},{5,4},{6,7},{7,6},{8,9},{9,8},{10,11... | collective-permute-start | bytes 392 | tf_op jit(solution)/shard_map/ppermute | solution.py:18
  7.5 0.9 slice.67
  8.5 0.4 collective-permute-start.8
  8.9 0.7 dynamic_slice.3
  9.6 1.7 %collective-permute-done.1 = bf16[32,2048]{1,0:T(8,128)(2,1)S(1)} collective-permute-done((bf16[32,2048]{1,0:T(8,128)(2,1)}, bf16[32,2048]{1,0:T(8,128)(2,1)S(1)}, u32[]{:S(2)}, u32[]{:S(2)}) %collective-permute-start.1) | collective-permute-done | bytes 131104 | tf_op jit(solution)/shard_map/ppermute | solution.py:18
  11.3 1.0 collective-permute-start.2
  12.2 0.9 broadcast_select_fusion.15
  13.2 5.2 %collective-permute-start.5 = (bf16[32,2048]{1,0:T(8,128)(2,1)S(1)}, bf16[32,2048]{1,0:T(8,128)(2,1)S(1)}, u32[]{:S(2)}, u32[]{:S(2)}) collective-permute-start(bf16[32,2048]{1,0:T(8,128)(2,1)S(1)} %get-tuple-element.59), channel_id=1, source_target_pairs={{0,8},{4,12},{8,0},{12,4},{1,9},{5,13},{9,1},{13,5},{2,10},{6,14},... | collective-permute-start | bytes 393224 | tf_op jit(solution)/shard_map/ppermute | solution.py:18
  18.4 2.1 %collective-permute-done.2 = f32[32]{0:T(128)S(1)} collective-permute-done((f32[32]{0:T(128)S(1)}, f32[32]{0:T(128)S(1)}, u32[]{:S(2)}, u32[]{:S(2)}) %collective-permute-start.2) | collective-permute-done | bytes 160 | tf_op jit(solution)/shard_map/ppermute | solution.py:18
  20.5 1.1 %fusion.22 = bf16[32,4096]{1,0:T(8,128)(2,1)S(1)} fusion(bf16[32,4096]{1,0:T(8,128)(2,1)} %param.8, f32[4096]{0:T(1024)S(1)} %dynamic_slice.3, f32[32]{0:T(128)S(1)} %add_rsqrt_fusion), kind=kLoop, calls=%fused_computation.29 | loop fusion | flops 524288 | bytes 540800 | tf_op jit(solution)/shard_map/convert_element_type | solution.py:68
  21.6 0.9 collective-permute-start.3
  22.5 0.8 collective-permute-start.9
  23.3 4.1 %collective-permute-start.6 = (bf16[64,2048]{1,0:T(8,128)(2,1)S(1)}, bf16[64,2048]{1,0:T(8,128)(2,1)S(1)}, u32[]{:S(2)}, u32[]{:S(2)}) collective-permute-start(bf16[64,2048]{1,0:T(8,128)(2,1)S(1)} %pad_maximum_fusion.4), channel_id=1, source_target_pairs={{0,1},{1,0},{2,3},{3,2},{4,5},{5,4},{6,7},{7,6},{8,9},{9,8},{10,11... | collective-permute-start | bytes 786440 | tf_op jit(solution)/shard_map/ppermute | solution.py:18
  27.4 7.1 %collective-permute-done.3 = bf16[32,3328]{1,0:T(8,128)(2,1)S(1)} collective-permute-done((bf16[32,3328]{1,0:T(8,128)(2,1)S(1)}, bf16[32,3328]{1,0:T(8,128)(2,1)S(1)}, u32[]{:S(2)}, u32[]{:S(2)}) %collective-permute-start.3) | collective-permute-done | bytes 213024 | tf_op jit(solution)/shard_map/ppermute | solution.py:18
  34.5 1.8 %collective-permute-start.11 = (bf16[64,3328]{1,0:T(8,128)(2,1)S(1)}, bf16[64,3328]{1,0:T(8,128)(2,1)S(1)}, u32[]{:S(2)}, u32[]{:S(2)}) collective-permute-start(bf16[64,3328]{1,0:T(8,128)(2,1)S(1)} %pad_maximum_fusion.2), channel_id=1, source_target_pairs={{0,1},{1,0},{2,3},{3,2},{4,5},{5,4},{6,7},{7,6},{8,9},{9,8},{10,11... | collective-permute-start | bytes 1277960 | tf_op jit(solution)/shard_map/ppermute | solution.py:18
  36.4 1.6 %collective-permute-start.12 = (bf16[32,3328]{1,0:T(8,128)(2,1)S(1)}, bf16[32,3328]{1,0:T(8,128)(2,1)S(1)}, u32[]{:S(2)}, u32[]{:S(2)}) collective-permute-start(bf16[32,3328]{1,0:T(8,128)(2,1)S(1)} %get-tuple-element.56), channel_id=1, source_target_pairs={{0,8},{4,12},{8,0},{12,4},{1,9},{5,13},{9,1},{13,5},{2,10},{6,14},... | collective-permute-start | bytes 638984 | tf_op jit(solution)/shard_map/ppermute | solution.py:18
  38.0 0.1 broadcast_select_fusion.6
  38.1 4.9 %collective-permute-done.12 = bf16[32,3328]{1,0:T(8,128)(2,1)S(1)} collective-permute-done((bf16[32,3328]{1,0:T(8,128)(2,1)S(1)}, bf16[32,3328]{1,0:T(8,128)(2,1)S(1)}, u32[]{:S(2)}, u32[]{:S(2)}) %collective-permute-start.12) | collective-permute-done | bytes 213024 | tf_op jit(solution)/shard_map/ppermute | solution.py:18
  43.0 0.4 collective-permute-start.15
  43.4 8.1 %fusion.24 = f32[128,4096]{1,0:T(8,128)S(1)} fusion(bf16[2048,4096]{1,0:T(8,128)(2,1)} %param.14, bf16[64,2048]{1,0:T(8,128)(2,1)S(1)} %collective-permute-done.7, bf16[64,2048]{1,0:T(8,128)(2,1)S(1)} %get-tuple-element.25), kind=kOutput, calls=%fused_computation.33 | convolution fusion | flops 2148532224 | bytes 19398656 | tf_op jit(solution)/shard_map/dot_general | solution.py:14
  51.5 1.3 %collective-permute-done.11 = bf16[64,3328]{1,0:T(8,128)(2,1)S(1)} collective-permute-done((bf16[64,3328]{1,0:T(8,128)(2,1)S(1)}, bf16[64,3328]{1,0:T(8,128)(2,1)S(1)}, u32[]{:S(2)}, u32[]{:S(2)}) %collective-permute-start.11) | collective-permute-done | bytes 426016 | tf_op jit(solution)/shard_map/ppermute | solution.py:18
  53.0 1.6 %collective-permute-start.10 = (bf16[32,4096]{1,0:T(8,128)(2,1)S(1)}, bf16[32,4096]{1,0:T(8,128)(2,1)S(1)}, u32[]{:S(2)}, u32[]{:S(2)}) collective-permute-start(bf16[32,4096]{1,0:T(8,128)(2,1)S(1)} %get-tuple-element.51), channel_id=1, source_target_pairs={{0,8},{4,12},{8,0},{12,4},{1,9},{5,13},{9,1},{13,5},{2,10},{6,14},... | collective-permute-start | bytes 786440 | tf_op jit(solution)/shard_map/ppermute | solution.py:18
  54.6 0.1 collective-permute-done.13
  54.7 10.8 %fusion.8 = f32[128,4096]{1,0:T(8,128)S(1)} fusion(f32[128,4096]{1,0:T(8,128)S(1)} %fusion.24, bf16[6656,4096]{1,0:T(8,128)(2,1)} %param.15, bf16[64,3328]{1,0:T(8,128)(2,1)S(1)} %collective-permute-done.13, bf16[64,3328]{1,0:T(8,128)(2,1)S(1)} %get-tuple-element.31), kind=kOutput, calls=%fused_computation.8 | convolution fusion | flops 3491889152 | bytes 32309248 | tf_op jit(solution)/shard_map/dot_general | solution.py:14
  65.7 0.2 collective-permute-start.16
  65.9 0.5 collective-permute-start.14
  66.5 1.1 %collective-permute-done.16 = bf16[64,3328]{1,0:T(8,128)(2,1)S(1)} collective-permute-done((bf16[64,3328]{1,0:T(8,128)(2,1)S(1)}, bf16[64,3328]{1,0:T(8,128)(2,1)S(1)}, u32[]{:S(2)}, u32[]{:S(2)}) %collective-permute-start.16) | collective-permute-done | bytes 426016 | tf_op jit(solution)/shard_map/ppermute | solution.py:18
  67.5 10.9 %fusion.11 = f32[128,4096]{1,0:T(8,128)S(1)} fusion(f32[128,4096]{1,0:T(8,128)S(1)} %fusion.8, bf16[6656,4096]{1,0:T(8,128)(2,1)} %param.15, bf16[64,3328]{1,0:T(8,128)(2,1)S(1)} %collective-permute-done.16, bf16[64,3328]{1,0:T(8,128)(2,1)S(1)} %get-tuple-element.45), kind=kOutput, calls=%fused_computation.9 | convolution fusion | flops 3491889152 | bytes 32309248 | tf_op jit(solution)/shard_map/dot_general | solution.py:14
  78.5 0.2 collective-permute-start.18
  78.7 1.5 %collective-permute-done.14 = bf16[64,4096]{1,0:T(8,128)(2,1)S(1)} collective-permute-done((bf16[64,4096]{1,0:T(8,128)(2,1)S(1)}, bf16[64,4096]{1,0:T(8,128)(2,1)S(1)}, u32[]{:S(2)}, u32[]{:S(2)}) %collective-permute-start.14) | collective-permute-done | bytes 524320 | tf_op jit(solution)/shard_map/ppermute | solution.py:18
  80.3 0.1 collective-permute-done.18
  80.5 0.1 slice_add_fusion
  80.6 1.6 %collective-permute-start.21 = (bf16[32,4096]{1,0:T(8,128)(2,1)S(1)}, bf16[32,4096]{1,0:T(8,128)(2,1)S(1)}, u32[]{:S(2)}, u32[]{:S(2)}) collective-permute-start(bf16[32,4096]{1,0:T(8,128)(2,1)S(1)} %slice.147), channel_id=1, source_target_pairs={{0,8},{4,12},{8,0},{12,4},{1,9},{5,13},{9,1},{13,5},{2,10},{6,14},... | collective-permute-start | bytes 786440 | tf_op jit(solution)/shard_map/ppermute | solution.py:18
  82.2 0.1 pad_maximum_fusion.1
  82.3 4.6 %fusion.6 = f32[128,1024]{1,0:T(8,128)S(1)} fusion(bf16[128,4096]{1,0:T(8,128)(2,1)S(1)} %pad_maximum_fusion.1, bf16[4096,2048]{1,0:T(8,128)(2,1)} %param.12), kind=kOutput, calls=%fused_computation.6 | convolution fusion | flops 1073741824 | bytes 9961472 | tf_op jit(solution)/shard_map/dot_general | solution.py:14
  87.0 0.4 fusion.37
  87.5 0.2 collective-permute-start.19
  87.7 1.6 %collective-permute-done.21 = bf16[32,4096]{1,0:T(8,128)(2,1)S(1)} collective-permute-done((bf16[32,4096]{1,0:T(8,128)(2,1)S(1)}, bf16[32,4096]{1,0:T(8,128)(2,1)S(1)}, u32[]{:S(2)}, u32[]{:S(2)}) %collective-permute-start.21) | collective-permute-done | bytes 262176 | tf_op jit(solution)/shard_map/ppermute | solution.py:18
  89.3 0.8 fusion.23
  90.1 4.6 %fusion.4 = f32[128,1024]{1,0:T(8,128)S(1)} fusion(bf16[128,4096]{1,0:T(8,128)(2,1)S(1)} %pad_maximum_fusion.1, bf16[4096,2048]{1,0:T(8,128)(2,1)} %param.12), kind=kOutput, calls=%fused_computation.4 | convolution fusion | flops 1073741824 | bytes 9961472 | tf_op jit(solution)/shard_map/dot_general | solution.py:14
  94.9 1.6 %collective-permute-start.20 = (bf16[32,1280]{1,0:T(8,128)(2,1)S(1)}, bf16[32,1280]{1,0:T(8,128)(2,1)S(1)}, u32[]{:S(2)}, u32[]{:S(2)}) collective-permute-start(bf16[32,1280]{1,0:T(8,128)(2,1)S(1)} %slice.149), channel_id=1, source_target_pairs={{0,8},{4,12},{8,0},{12,4},{1,9},{5,13},{9,1},{13,5},{2,10},{6,14},... | collective-permute-start | bytes 245768 | tf_op jit(solution)/shard_map/ppermute | solution.py:18
  96.5 1.3 %collective-permute-start.23 = (bf16[32,1024]{1,0:T(8,128)(2,1)S(1)}, bf16[32,1024]{1,0:T(8,128)(2,1)S(1)}, u32[]{:S(2)}, u32[]{:S(2)}) collective-permute-start(bf16[32,1024]{1,0:T(8,128)(2,1)S(1)} %slice.150), channel_id=1, source_target_pairs={{0,8},{4,12},{8,0},{12,4},{1,9},{5,13},{9,1},{13,5},{2,10},{6,14},... | collective-permute-start | bytes 196616 | tf_op jit(solution)/shard_map/ppermute | solution.py:18
  97.8 2.4 %collective-permute-done.20 = bf16[32,1280]{1,0:T(8,128)(2,1)S(1)} collective-permute-done((bf16[32,1280]{1,0:T(8,128)(2,1)S(1)}, bf16[32,1280]{1,0:T(8,128)(2,1)S(1)}, u32[]{:S(2)}, u32[]{:S(2)}) %collective-permute-start.20) | collective-permute-done | bytes 81952 | tf_op jit(solution)/shard_map/ppermute | solution.py:18
  100.2 0.6 slice.101
  100.8 0.4 collective-permute-done.23
  101.2 0.7 pad_maximum_fusion.5
  (47 shorter events, 1.0 us)
Async XLA Ops:
  0.6 86.4 %copy-start = (bf16[4096,256]{1,0:T(8,128)(2,1)S(1)}, bf16[4096,256]{1,0:T(8,128)(2,1)}, u32[]{:S(2)}) copy-start(bf16[4096,256]{1,0:T(8,128)(2,1)} %param.13) | copy-start | bytes 6291460
  0.6 20.9 %copy-start.2 = (bf16[32,6656]{1,0:T(8,128)(2,1)S(1)}, bf16[32,6656]{1,0:T(8,128)(2,1)}, u32[]{:S(2)}) copy-start(bf16[32,6656]{1,0:T(8,128)(2,1)} %param.10) | copy-start | bytes 1277956
  0.7 10.6 %collective-permute-start.1 = (bf16[32,2048]{1,0:T(8,128)(2,1)}, bf16[32,2048]{1,0:T(8,128)(2,1)S(1)}, u32[]{:S(2)}, u32[]{:S(2)}) collective-permute-start(bf16[32,2048]{1,0:T(8,128)(2,1)} %param.9), channel_id=1, source_target_pairs={{0,2},{1,3},{2,0},{3,1},{4,6},{5,7},{6,4},{7,5},{8,10},{9,11},{10,... | collective-permute-start | bytes 393224 | tf_op jit(solution)/shard_map/ppermute | solution.py:18
  5.9 3.7 %collective-permute-start = (f32[32]{0:T(128)S(1)}, f32[32]{0:T(128)S(1)}, u32[]{:S(2)}, u32[]{:S(2)}) collective-permute-start(f32[32]{0:T(128)S(1)} %fusion.20), channel_id=1, source_target_pairs={{0,1},{1,0},{2,3},{3,2},{4,5},{5,4},{6,7},{7,6},{8,9},{9,8},{10,11... | collective-permute-start | bytes 392 | tf_op jit(solution)/shard_map/ppermute | solution.py:18
  8.5 13.1 %collective-permute-start.8 = (bf16[32,3328]{1,0:T(8,128)(2,1)S(1)}, bf16[32,3328]{1,0:T(8,128)(2,1)S(1)}, u32[]{:S(2)}, u32[]{:S(2)}) collective-permute-start(bf16[32,3328]{1,0:T(8,128)(2,1)S(1)} %slice.67), channel_id=1, source_target_pairs={{0,2},{1,3},{2,0},{3,1},{4,6},{5,7},{6,4},{7,5},{8,10},{9,11},{10,... | collective-permute-start | bytes 638984 | tf_op jit(solution)/shard_map/ppermute | solution.py:18
  11.3 9.2 %collective-permute-start.2 = (f32[32]{0:T(128)S(1)}, f32[32]{0:T(128)S(1)}, u32[]{:S(2)}, u32[]{:S(2)}) collective-permute-start(f32[32]{0:T(128)S(1)} %add.59), channel_id=1, source_target_pairs={{0,2},{1,3},{2,0},{3,1},{4,6},{5,7},{6,4},{7,5},{8,10},{9,11},{10,... | collective-permute-start | bytes 392 | tf_op jit(solution)/shard_map/ppermute | solution.py:18
  13.2 10.1 %collective-permute-start.5 = (bf16[32,2048]{1,0:T(8,128)(2,1)S(1)}, bf16[32,2048]{1,0:T(8,128)(2,1)S(1)}, u32[]{:S(2)}, u32[]{:S(2)}) collective-permute-start(bf16[32,2048]{1,0:T(8,128)(2,1)S(1)} %get-tuple-element.59), channel_id=1, source_target_pairs={{0,8},{4,12},{8,0},{12,4},{1,9},{5,13},{9,1},{13,5},{2,10},{6,14},... | collective-permute-start | bytes 393224 | tf_op jit(solution)/shard_map/ppermute | solution.py:18
  21.6 12.8 %collective-permute-start.3 = (bf16[32,3328]{1,0:T(8,128)(2,1)S(1)}, bf16[32,3328]{1,0:T(8,128)(2,1)S(1)}, u32[]{:S(2)}, u32[]{:S(2)}) collective-permute-start(bf16[32,3328]{1,0:T(8,128)(2,1)S(1)} %get-tuple-element.23), channel_id=1, source_target_pairs={{0,2},{1,3},{2,0},{3,1},{4,6},{5,7},{6,4},{7,5},{8,10},{9,11},{10,... | collective-permute-start | bytes 638984 | tf_op jit(solution)/shard_map/ppermute | solution.py:18
  22.5 12.0 %collective-permute-start.9 = (bf16[32,3328]{1,0:T(8,128)(2,1)S(1)}, bf16[32,3328]{1,0:T(8,128)(2,1)S(1)}, u32[]{:S(2)}, u32[]{:S(2)}) collective-permute-start(bf16[32,3328]{1,0:T(8,128)(2,1)S(1)} %get-tuple-element.50), channel_id=1, source_target_pairs={{0,8},{4,12},{8,0},{12,4},{1,9},{5,13},{9,1},{13,5},{2,10},{6,14},... | collective-permute-start | bytes 638984 | tf_op jit(solution)/shard_map/ppermute | solution.py:18
  23.3 14.6 %collective-permute-start.6 = (bf16[64,2048]{1,0:T(8,128)(2,1)S(1)}, bf16[64,2048]{1,0:T(8,128)(2,1)S(1)}, u32[]{:S(2)}, u32[]{:S(2)}) collective-permute-start(bf16[64,2048]{1,0:T(8,128)(2,1)S(1)} %pad_maximum_fusion.4), channel_id=1, source_target_pairs={{0,1},{1,0},{2,3},{3,2},{4,5},{5,4},{6,7},{7,6},{8,9},{9,8},{10,11... | collective-permute-start | bytes 786440 | tf_op jit(solution)/shard_map/ppermute | solution.py:18
  34.5 17.1 %collective-permute-start.4 = (bf16[32,4096]{1,0:T(8,128)(2,1)S(1)}, bf16[32,4096]{1,0:T(8,128)(2,1)S(1)}, u32[]{:S(2)}, u32[]{:S(2)}) collective-permute-start(bf16[32,4096]{1,0:T(8,128)(2,1)S(1)} %fusion.22), channel_id=1, source_target_pairs={{0,2},{1,3},{2,0},{3,1},{4,6},{5,7},{6,4},{7,5},{8,10},{9,11},{10,... | collective-permute-start | bytes 786440 | tf_op jit(solution)/shard_map/ppermute | solution.py:18
  34.5 18.3 %collective-permute-start.11 = (bf16[64,3328]{1,0:T(8,128)(2,1)S(1)}, bf16[64,3328]{1,0:T(8,128)(2,1)S(1)}, u32[]{:S(2)}, u32[]{:S(2)}) collective-permute-start(bf16[64,3328]{1,0:T(8,128)(2,1)S(1)} %pad_maximum_fusion.2), channel_id=1, source_target_pairs={{0,1},{1,0},{2,3},{3,2},{4,5},{5,4},{6,7},{7,6},{8,9},{9,8},{10,11... | collective-permute-start | bytes 1277960 | tf_op jit(solution)/shard_map/ppermute | solution.py:18
  36.4 6.6 %collective-permute-start.12 = (bf16[32,3328]{1,0:T(8,128)(2,1)S(1)}, bf16[32,3328]{1,0:T(8,128)(2,1)S(1)}, u32[]{:S(2)}, u32[]{:S(2)}) collective-permute-start(bf16[32,3328]{1,0:T(8,128)(2,1)S(1)} %get-tuple-element.56), channel_id=1, source_target_pairs={{0,8},{4,12},{8,0},{12,4},{1,9},{5,13},{9,1},{13,5},{2,10},{6,14},... | collective-permute-start | bytes 638984 | tf_op jit(solution)/shard_map/ppermute | solution.py:18
  38.1 5.3 %collective-permute-start.7 = (bf16[64,2048]{1,0:T(8,128)(2,1)S(1)}, bf16[64,2048]{1,0:T(8,128)(2,1)S(1)}, u32[]{:S(2)}, u32[]{:S(2)}) collective-permute-start(bf16[64,2048]{1,0:T(8,128)(2,1)S(1)} %get-tuple-element.53), channel_id=1, source_target_pairs={{0,4},{4,0},{8,12},{12,8},{1,5},{5,1},{9,13},{13,9},{2,6},{6,2},{1... | collective-permute-start | bytes 786440 | tf_op jit(solution)/shard_map/ppermute | solution.py:18
  43.0 22.6 %collective-permute-start.15 = (bf16[64,3328]{1,0:T(8,128)(2,1)S(1)}, bf16[64,3328]{1,0:T(8,128)(2,1)S(1)}, u32[]{:S(2)}, u32[]{:S(2)}) collective-permute-start(bf16[64,3328]{1,0:T(8,128)(2,1)S(1)} %pad_maximum_fusion.3), channel_id=1, source_target_pairs={{0,1},{1,0},{2,3},{3,2},{4,5},{5,4},{6,7},{7,6},{8,9},{9,8},{10,11... | collective-permute-start | bytes 1277960 | tf_op jit(solution)/shard_map/ppermute | solution.py:18
  52.9 1.8 %collective-permute-start.13 = (bf16[64,3328]{1,0:T(8,128)(2,1)S(1)}, bf16[64,3328]{1,0:T(8,128)(2,1)S(1)}, u32[]{:S(2)}, u32[]{:S(2)}) collective-permute-start(bf16[64,3328]{1,0:T(8,128)(2,1)S(1)} %get-tuple-element.47), channel_id=1, source_target_pairs={{0,4},{4,0},{8,12},{12,8},{1,5},{5,1},{9,13},{13,9},{2,6},{6,2},{1... | collective-permute-start | bytes 1277960 | tf_op jit(solution)/shard_map/ppermute | solution.py:18
  53.0 12.5 %collective-permute-start.10 = (bf16[32,4096]{1,0:T(8,128)(2,1)S(1)}, bf16[32,4096]{1,0:T(8,128)(2,1)S(1)}, u32[]{:S(2)}, u32[]{:S(2)}) collective-permute-start(bf16[32,4096]{1,0:T(8,128)(2,1)S(1)} %get-tuple-element.51), channel_id=1, source_target_pairs={{0,8},{4,12},{8,0},{12,4},{1,9},{5,13},{9,1},{13,5},{2,10},{6,14},... | collective-permute-start | bytes 786440 | tf_op jit(solution)/shard_map/ppermute | solution.py:18
  65.7 1.8 %collective-permute-start.16 = (bf16[64,3328]{1,0:T(8,128)(2,1)S(1)}, bf16[64,3328]{1,0:T(8,128)(2,1)S(1)}, u32[]{:S(2)}, u32[]{:S(2)}) collective-permute-start(bf16[64,3328]{1,0:T(8,128)(2,1)S(1)} %get-tuple-element.46), channel_id=1, source_target_pairs={{0,4},{4,0},{8,12},{12,8},{1,5},{5,1},{9,13},{13,9},{2,6},{6,2},{1... | collective-permute-start | bytes 1277960 | tf_op jit(solution)/shard_map/ppermute | solution.py:18
  65.9 14.3 %collective-permute-start.14 = (bf16[64,4096]{1,0:T(8,128)(2,1)S(1)}, bf16[64,4096]{1,0:T(8,128)(2,1)S(1)}, u32[]{:S(2)}, u32[]{:S(2)}) collective-permute-start(bf16[64,4096]{1,0:T(8,128)(2,1)S(1)} %constant_dynamic-update-slice_fusion), channel_id=1, source_target_pairs={{0,1},{1,0},{2,3},{3,2},{4,5},{5,4},{6,7},{7,6},{8,9},{9,8},{10,11... | collective-permute-start | bytes 1572872 | tf_op jit(solution)/shard_map/ppermute | solution.py:18
  78.5 2.0 %collective-permute-start.18 = (bf16[64,4096]{1,0:T(8,128)(2,1)S(1)}, bf16[64,4096]{1,0:T(8,128)(2,1)S(1)}, u32[]{:S(2)}, u32[]{:S(2)}) collective-permute-start(bf16[64,4096]{1,0:T(8,128)(2,1)S(1)} %slice.146), channel_id=1, source_target_pairs={{0,4},{4,0},{8,12},{12,8},{1,5},{5,1},{9,13},{13,9},{2,6},{6,2},{1... | collective-permute-start | bytes 1572872 | tf_op jit(solution)/shard_map/ppermute | solution.py:18
  80.3 2.0 %collective-permute-start.17 = (bf16[64,4096]{1,0:T(8,128)(2,1)S(1)}, bf16[64,4096]{1,0:T(8,128)(2,1)S(1)}, u32[]{:S(2)}, u32[]{:S(2)}) collective-permute-start(bf16[64,4096]{1,0:T(8,128)(2,1)S(1)} %get-tuple-element.44), channel_id=1, source_target_pairs={{0,4},{4,0},{8,12},{12,8},{1,5},{5,1},{9,13},{13,9},{2,6},{6,2},{1... | collective-permute-start | bytes 1572872 | tf_op jit(solution)/shard_map/ppermute | solution.py:18
  80.6 8.6 %collective-permute-start.21 = (bf16[32,4096]{1,0:T(8,128)(2,1)S(1)}, bf16[32,4096]{1,0:T(8,128)(2,1)S(1)}, u32[]{:S(2)}, u32[]{:S(2)}) collective-permute-start(bf16[32,4096]{1,0:T(8,128)(2,1)S(1)} %slice.147), channel_id=1, source_target_pairs={{0,8},{4,12},{8,0},{12,4},{1,9},{5,13},{9,1},{13,5},{2,10},{6,14},... | collective-permute-start | bytes 786440 | tf_op jit(solution)/shard_map/ppermute | solution.py:18
  87.0 2.3 %copy-start.1 = (bf16[32,4096]{1,0:T(8,128)(2,1)S(1)}, bf16[32,4096]{1,0:T(8,128)(2,1)}, u32[]{:S(2)}) copy-start(bf16[32,4096]{1,0:T(8,128)(2,1)} %param.8) | copy-start | bytes 786436
  87.5 7.3 %collective-permute-start.19 = (bf16[64,1280]{1,0:T(8,128)(2,1)S(1)}, bf16[64,1280]{1,0:T(8,128)(2,1)S(1)}, u32[]{:S(2)}, u32[]{:S(2)}) collective-permute-start(bf16[64,1280]{1,0:T(8,128)(2,1)S(1)} %fusion.31), channel_id=1, source_target_pairs={{0,4},{4,0},{8,12},{12,8},{1,5},{5,1},{9,13},{13,9},{2,6},{6,2},{1... | collective-permute-start | bytes 491528 | tf_op jit(solution)/shard_map/ppermute | solution.py:18
  94.7 1.8 %collective-permute-start.22 = (bf16[64,1024]{1,0:T(8,128)(2,1)S(1)}, bf16[64,1024]{1,0:T(8,128)(2,1)S(1)}, u32[]{:S(2)}, u32[]{:S(2)}) collective-permute-start(bf16[64,1024]{1,0:T(8,128)(2,1)S(1)} %slice.148), channel_id=1, source_target_pairs={{0,4},{4,0},{8,12},{12,8},{1,5},{5,1},{9,13},{13,9},{2,6},{6,2},{1... | collective-permute-start | bytes 393224 | tf_op jit(solution)/shard_map/ppermute | solution.py:18
  94.9 5.3 %collective-permute-start.20 = (bf16[32,1280]{1,0:T(8,128)(2,1)S(1)}, bf16[32,1280]{1,0:T(8,128)(2,1)S(1)}, u32[]{:S(2)}, u32[]{:S(2)}) collective-permute-start(bf16[32,1280]{1,0:T(8,128)(2,1)S(1)} %slice.149), channel_id=1, source_target_pairs={{0,8},{4,12},{8,0},{12,4},{1,9},{5,13},{9,1},{13,5},{2,10},{6,14},... | collective-permute-start | bytes 245768 | tf_op jit(solution)/shard_map/ppermute | solution.py:18
  96.5 4.7 %collective-permute-start.23 = (bf16[32,1024]{1,0:T(8,128)(2,1)S(1)}, bf16[32,1024]{1,0:T(8,128)(2,1)S(1)}, u32[]{:S(2)}, u32[]{:S(2)}) collective-permute-start(bf16[32,1024]{1,0:T(8,128)(2,1)S(1)} %slice.150), channel_id=1, source_target_pairs={{0,8},{4,12},{8,0},{12,4},{1,9},{5,13},{9,1},{13,5},{2,10},{6,14},... | collective-permute-start | bytes 196616 | tf_op jit(solution)/shard_map/ppermute | solution.py:18

commit v5 on v4

--- a/solution.py
+++ b/solution.py
@@ -89,7 +89,7 @@
             arrived = second[1]
             second = over_near_z(second)
             first = over_cores(after(first, arrived, block_part))
-            block_part += dot(jnp.concatenate(after(first, arrived)), w_down[:half])
+            block_part += dot(jnp.concatenate(first), w_down[:half])
             normed = over_near_z(after(normed, block_part))
             second = over_cores(after(second, block_part))
             block_part += dot(jnp.concatenate(second), w_down[half:])

time: 102 us -> 102 us (level)
  no operation moved by 1% of the time
where the time goes in v5:
time: 102 us
  matrix products  39.6 us (39%)
  starting transfers between devices  29.3 us (29%)
  waiting for transfers between devices  24.2 us (24%)
  other arithmetic  5.37 us (5%)
  local copies, waits for them, and re-layouts  2.46 us (2%)
    dot_general x6, matrix products, dot(): return jnp.dot(left, right, preferred_element_type=jnp.float32)  39.6 us
    ppermute x24, starting transfers between devices, flip(): lax.ppermute(value, axis, [(i, i ^ bit) for i in range(lax.axis_size(axis...  29.3 us
    ppermute x24, waiting for transfers between devices, flip(): lax.ppermute(value, axis, [(i, i ^ bit) for i in range(lax.axis_size(axis...  24.2 us
  transfers between devices with their start and end apart: 24, of which 12 were waited for; matrix products, arithmetic and copies ran while one was open for 46% of the time, Pallas kernels for 0%

profile of v5, /device:TPU:0, one launch (start us, length us, event | category | flops | bytes accessed | tf_op | source)
XLA Modules:
  0.0 101.9 jit_solution(8711665636212709766)
XLA Ops:
  0.7 4.1 %collective-permute-start.1 = (bf16[32,2048]{1,0:T(8,128)(2,1)}, bf16[32,2048]{1,0:T(8,128)(2,1)S(1)}, u32[]{:S(2)}, u32[]{:S(2)}) collective-permute-start(bf16[32,2048]{1,0:T(8,128)(2,1)} %param.9), channel_id=1, source_target_pairs={{0,2},{1,3},{2,0},{3,1},{4,6},{5,7},{6,4},{7,5},{8,10},{9,11},{10,... | collective-permute-start | bytes 393224 | tf_op jit(solution)/shard_map/ppermute | solution.py:18
  4.8 1.1 %fusion.20 = f32[32]{0:T(128)S(1)} fusion(bf16[32,4096]{1,0:T(8,128)(2,1)} %param.8), kind=kLoop, calls=%fused_computation.27 | loop fusion | flops 393184 | bytes 262272 | tf_op jit(solution)/shard_map/reduce_sum | solution.py:64
  5.9 1.6 %collective-permute-start = (f32[32]{0:T(128)S(1)}, f32[32]{0:T(128)S(1)}, u32[]{:S(2)}, u32[]{:S(2)}) collective-permute-start(f32[32]{0:T(128)S(1)} %fusion.20), channel_id=1, source_target_pairs={{0,1},{1,0},{2,3},{3,2},{4,5},{5,4},{6,7},{7,6},{8,9},{9,8},{10,11... | collective-permute-start | bytes 392 | tf_op jit(solution)/shard_map/ppermute | solution.py:18
  7.5 0.9 slice.67
  8.5 0.4 collective-permute-start.8
  8.9 0.7 dynamic_slice.3
  9.6 1.7 %collective-permute-done.1 = bf16[32,2048]{1,0:T(8,128)(2,1)S(1)} collective-permute-done((bf16[32,2048]{1,0:T(8,128)(2,1)}, bf16[32,2048]{1,0:T(8,128)(2,1)S(1)}, u32[]{:S(2)}, u32[]{:S(2)}) %collective-permute-start.1) | collective-permute-done | bytes 131104 | tf_op jit(solution)/shard_map/ppermute | solution.py:18
  11.3 1.0 collective-permute-start.2
  12.2 0.9 broadcast_select_fusion.15
  13.2 5.2 %collective-permute-start.5 = (bf16[32,2048]{1,0:T(8,128)(2,1)S(1)}, bf16[32,2048]{1,0:T(8,128)(2,1)S(1)}, u32[]{:S(2)}, u32[]{:S(2)}) collective-permute-start(bf16[32,2048]{1,0:T(8,128)(2,1)S(1)} %get-tuple-element.55), channel_id=1, source_target_pairs={{0,8},{4,12},{8,0},{12,4},{1,9},{5,13},{9,1},{13,5},{2,10},{6,14},... | collective-permute-start | bytes 393224 | tf_op jit(solution)/shard_map/ppermute | solution.py:18
  18.4 2.1 %collective-permute-done.2 = f32[32]{0:T(128)S(1)} collective-permute-done((f32[32]{0:T(128)S(1)}, f32[32]{0:T(128)S(1)}, u32[]{:S(2)}, u32[]{:S(2)}) %collective-permute-start.2) | collective-permute-done | bytes 160 | tf_op jit(solution)/shard_map/ppermute | solution.py:18
  20.5 1.1 %fusion.22 = bf16[32,4096]{1,0:T(8,128)(2,1)S(1)} fusion(bf16[32,4096]{1,0:T(8,128)(2,1)} %param.8, f32[4096]{0:T(1024)S(1)} %dynamic_slice.3, f32[32]{0:T(128)S(1)} %add_rsqrt_fusion), kind=kLoop, calls=%fused_computation.29 | loop fusion | flops 524288 | bytes 540800 | tf_op jit(solution)/shard_map/convert_element_type | solution.py:68
  21.6 0.9 collective-permute-start.3
  22.5 0.8 collective-permute-start.9
  23.3 4.1 %collective-permute-start.6 = (bf16[64,2048]{1,0:T(8,128)(2,1)S(1)}, bf16[64,2048]{1,0:T(8,128)(2,1)S(1)}, u32[]{:S(2)}, u32[]{:S(2)}) collective-permute-start(bf16[64,2048]{1,0:T(8,128)(2,1)S(1)} %pad_maximum_fusion.4), channel_id=1, source_target_pairs={{0,1},{1,0},{2,3},{3,2},{4,5},{5,4},{6,7},{7,6},{8,9},{9,8},{10,11... | collective-permute-start | bytes 786440 | tf_op jit(solution)/shard_map/ppermute | solution.py:18
  27.4 7.1 %collective-permute-done.3 = bf16[32,3328]{1,0:T(8,128)(2,1)S(1)} collective-permute-done((bf16[32,3328]{1,0:T(8,128)(2,1)S(1)}, bf16[32,3328]{1,0:T(8,128)(2,1)S(1)}, u32[]{:S(2)}, u32[]{:S(2)}) %collective-permute-start.3) | collective-permute-done | bytes 213024 | tf_op jit(solution)/shard_map/ppermute | solution.py:18
  34.5 1.8 %collective-permute-start.11 = (bf16[64,3328]{1,0:T(8,128)(2,1)S(1)}, bf16[64,3328]{1,0:T(8,128)(2,1)S(1)}, u32[]{:S(2)}, u32[]{:S(2)}) collective-permute-start(bf16[64,3328]{1,0:T(8,128)(2,1)S(1)} %pad_maximum_fusion.2), channel_id=1, source_target_pairs={{0,1},{1,0},{2,3},{3,2},{4,5},{5,4},{6,7},{7,6},{8,9},{9,8},{10,11... | collective-permute-start | bytes 1277960 | tf_op jit(solution)/shard_map/ppermute | solution.py:18
  36.4 1.6 %collective-permute-start.12 = (bf16[32,3328]{1,0:T(8,128)(2,1)S(1)}, bf16[32,3328]{1,0:T(8,128)(2,1)S(1)}, u32[]{:S(2)}, u32[]{:S(2)}) collective-permute-start(bf16[32,3328]{1,0:T(8,128)(2,1)S(1)} %get-tuple-element.52), channel_id=1, source_target_pairs={{0,8},{4,12},{8,0},{12,4},{1,9},{5,13},{9,1},{13,5},{2,10},{6,14},... | collective-permute-start | bytes 638984 | tf_op jit(solution)/shard_map/ppermute | solution.py:18
  38.0 0.1 broadcast_select_fusion.6
  38.1 4.9 %collective-permute-done.12 = bf16[32,3328]{1,0:T(8,128)(2,1)S(1)} collective-permute-done((bf16[32,3328]{1,0:T(8,128)(2,1)S(1)}, bf16[32,3328]{1,0:T(8,128)(2,1)S(1)}, u32[]{:S(2)}, u32[]{:S(2)}) %collective-permute-start.12) | collective-permute-done | bytes 213024 | tf_op jit(solution)/shard_map/ppermute | solution.py:18
  43.0 0.4 collective-permute-start.15
  43.4 8.1 %fusion.24 = f32[128,4096]{1,0:T(8,128)S(1)} fusion(bf16[2048,4096]{1,0:T(8,128)(2,1)} %param.14, bf16[64,2048]{1,0:T(8,128)(2,1)S(1)} %collective-permute-done.7, bf16[64,2048]{1,0:T(8,128)(2,1)S(1)} %get-tuple-element.23), kind=kOutput, calls=%fused_computation.33 | convolution fusion | flops 2148532224 | bytes 19398656 | tf_op jit(solution)/shard_map/dot_general | solution.py:14
  51.5 1.3 %collective-permute-done.11 = bf16[64,3328]{1,0:T(8,128)(2,1)S(1)} collective-permute-done((bf16[64,3328]{1,0:T(8,128)(2,1)S(1)}, bf16[64,3328]{1,0:T(8,128)(2,1)S(1)}, u32[]{:S(2)}, u32[]{:S(2)}) %collective-permute-start.11) | collective-permute-done | bytes 426016 | tf_op jit(solution)/shard_map/ppermute | solution.py:18
  53.0 1.6 %collective-permute-start.10 = (bf16[32,4096]{1,0:T(8,128)(2,1)S(1)}, bf16[32,4096]{1,0:T(8,128)(2,1)S(1)}, u32[]{:S(2)}, u32[]{:S(2)}) collective-permute-start(bf16[32,4096]{1,0:T(8,128)(2,1)S(1)} %get-tuple-element.47), channel_id=1, source_target_pairs={{0,8},{4,12},{8,0},{12,4},{1,9},{5,13},{9,1},{13,5},{2,10},{6,14},... | collective-permute-start | bytes 786440 | tf_op jit(solution)/shard_map/ppermute | solution.py:18
  54.6 0.1 collective-permute-done.13
  54.7 10.8 %fusion.8 = f32[128,4096]{1,0:T(8,128)S(1)} fusion(f32[128,4096]{1,0:T(8,128)S(1)} %fusion.24, bf16[6656,4096]{1,0:T(8,128)(2,1)} %param.15, bf16[64,3328]{1,0:T(8,128)(2,1)S(1)} %collective-permute-done.13, bf16[64,3328]{1,0:T(8,128)(2,1)S(1)} %get-tuple-element.43), kind=kOutput, calls=%fused_computation.8 | convolution fusion | flops 3491889152 | bytes 32309248 | tf_op jit(solution)/shard_map/dot_general | solution.py:14
  65.7 0.2 collective-permute-start.16
  65.9 0.5 collective-permute-start.14
  66.5 1.1 %collective-permute-done.16 = bf16[64,3328]{1,0:T(8,128)(2,1)S(1)} collective-permute-done((bf16[64,3328]{1,0:T(8,128)(2,1)S(1)}, bf16[64,3328]{1,0:T(8,128)(2,1)S(1)}, u32[]{:S(2)}, u32[]{:S(2)}) %collective-permute-start.16) | collective-permute-done | bytes 426016 | tf_op jit(solution)/shard_map/ppermute | solution.py:18
  67.5 10.9 %fusion.11 = f32[128,4096]{1,0:T(8,128)S(1)} fusion(f32[128,4096]{1,0:T(8,128)S(1)} %fusion.8, bf16[6656,4096]{1,0:T(8,128)(2,1)} %param.15, bf16[64,3328]{1,0:T(8,128)(2,1)S(1)} %collective-permute-done.16, bf16[64,3328]{1,0:T(8,128)(2,1)S(1)} %get-tuple-element.41), kind=kOutput, calls=%fused_computation.9 | convolution fusion | flops 3491889152 | bytes 32309248 | tf_op jit(solution)/shard_map/dot_general | solution.py:14
  78.5 0.2 collective-permute-start.18
  78.7 1.5 %collective-permute-done.14 = bf16[64,4096]{1,0:T(8,128)(2,1)S(1)} collective-permute-done((bf16[64,4096]{1,0:T(8,128)(2,1)S(1)}, bf16[64,4096]{1,0:T(8,128)(2,1)S(1)}, u32[]{:S(2)}, u32[]{:S(2)}) %collective-permute-start.14) | collective-permute-done | bytes 524320 | tf_op jit(solution)/shard_map/ppermute | solution.py:18
  80.3 0.1 collective-permute-done.18
  80.5 0.1 slice_add_fusion
  80.6 1.6 %collective-permute-start.21 = (bf16[32,4096]{1,0:T(8,128)(2,1)S(1)}, bf16[32,4096]{1,0:T(8,128)(2,1)S(1)}, u32[]{:S(2)}, u32[]{:S(2)}) collective-permute-start(bf16[32,4096]{1,0:T(8,128)(2,1)S(1)} %slice.147), channel_id=1, source_target_pairs={{0,8},{4,12},{8,0},{12,4},{1,9},{5,13},{9,1},{13,5},{2,10},{6,14},... | collective-permute-start | bytes 786440 | tf_op jit(solution)/shard_map/ppermute | solution.py:18
  82.2 0.1 pad_maximum_fusion.1
  82.3 4.6 %fusion.6 = f32[128,1024]{1,0:T(8,128)S(1)} fusion(bf16[128,4096]{1,0:T(8,128)(2,1)S(1)} %pad_maximum_fusion.1, bf16[4096,2048]{1,0:T(8,128)(2,1)} %param.12), kind=kOutput, calls=%fused_computation.6 | convolution fusion | flops 1073741824 | bytes 9961472 | tf_op jit(solution)/shard_map/dot_general | solution.py:14
  87.0 0.4 fusion.37
  87.5 0.2 collective-permute-start.19
  87.7 1.6 %collective-permute-done.21 = bf16[32,4096]{1,0:T(8,128)(2,1)S(1)} collective-permute-done((bf16[32,4096]{1,0:T(8,128)(2,1)S(1)}, bf16[32,4096]{1,0:T(8,128)(2,1)S(1)}, u32[]{:S(2)}, u32[]{:S(2)}) %collective-permute-start.21) | collective-permute-done | bytes 262176 | tf_op jit(solution)/shard_map/ppermute | solution.py:18
  89.3 0.8 fusion.23
  90.1 4.6 %fusion.4 = f32[128,1024]{1,0:T(8,128)S(1)} fusion(bf16[128,4096]{1,0:T(8,128)(2,1)S(1)} %pad_maximum_fusion.1, bf16[4096,2048]{1,0:T(8,128)(2,1)} %param.12), kind=kOutput, calls=%fused_computation.4 | convolution fusion | flops 1073741824 | bytes 9961472 | tf_op jit(solution)/shard_map/dot_general | solution.py:14
  94.9 1.6 %collective-permute-start.20 = (bf16[32,1280]{1,0:T(8,128)(2,1)S(1)}, bf16[32,1280]{1,0:T(8,128)(2,1)S(1)}, u32[]{:S(2)}, u32[]{:S(2)}) collective-permute-start(bf16[32,1280]{1,0:T(8,128)(2,1)S(1)} %slice.149), channel_id=1, source_target_pairs={{0,8},{4,12},{8,0},{12,4},{1,9},{5,13},{9,1},{13,5},{2,10},{6,14},... | collective-permute-start | bytes 245768 | tf_op jit(solution)/shard_map/ppermute | solution.py:18
  96.5 1.3 %collective-permute-start.23 = (bf16[32,1024]{1,0:T(8,128)(2,1)S(1)}, bf16[32,1024]{1,0:T(8,128)(2,1)S(1)}, u32[]{:S(2)}, u32[]{:S(2)}) collective-permute-start(bf16[32,1024]{1,0:T(8,128)(2,1)S(1)} %slice.150), channel_id=1, source_target_pairs={{0,8},{4,12},{8,0},{12,4},{1,9},{5,13},{9,1},{13,5},{2,10},{6,14},... | collective-permute-start | bytes 196616 | tf_op jit(solution)/shard_map/ppermute | solution.py:18
  97.8 2.4 %collective-permute-done.20 = bf16[32,1280]{1,0:T(8,128)(2,1)S(1)} collective-permute-done((bf16[32,1280]{1,0:T(8,128)(2,1)S(1)}, bf16[32,1280]{1,0:T(8,128)(2,1)S(1)}, u32[]{:S(2)}, u32[]{:S(2)}) %collective-permute-start.20) | collective-permute-done | bytes 81952 | tf_op jit(solution)/shard_map/ppermute | solution.py:18
  100.2 0.6 slice.101
  100.8 0.4 collective-permute-done.23
  101.2 0.7 pad_maximum_fusion.5
  (47 shorter events, 1.0 us)
Async XLA Ops:
  0.6 86.4 %copy-start = (bf16[4096,256]{1,0:T(8,128)(2,1)S(1)}, bf16[4096,256]{1,0:T(8,128)(2,1)}, u32[]{:S(2)}) copy-start(bf16[4096,256]{1,0:T(8,128)(2,1)} %param.13) | copy-start | bytes 6291460
  0.6 20.9 %copy-start.2 = (bf16[32,6656]{1,0:T(8,128)(2,1)S(1)}, bf16[32,6656]{1,0:T(8,128)(2,1)}, u32[]{:S(2)}) copy-start(bf16[32,6656]{1,0:T(8,128)(2,1)} %param.10) | copy-start | bytes 1277956
  0.7 10.6 %collective-permute-start.1 = (bf16[32,2048]{1,0:T(8,128)(2,1)}, bf16[32,2048]{1,0:T(8,128)(2,1)S(1)}, u32[]{:S(2)}, u32[]{:S(2)}) collective-permute-start(bf16[32,2048]{1,0:T(8,128)(2,1)} %param.9), channel_id=1, source_target_pairs={{0,2},{1,3},{2,0},{3,1},{4,6},{5,7},{6,4},{7,5},{8,10},{9,11},{10,... | collective-permute-start | bytes 393224 | tf_op jit(solution)/shard_map/ppermute | solution.py:18
  5.9 3.7 %collective-permute-start = (f32[32]{0:T(128)S(1)}, f32[32]{0:T(128)S(1)}, u32[]{:S(2)}, u32[]{:S(2)}) collective-permute-start(f32[32]{0:T(128)S(1)} %fusion.20), channel_id=1, source_target_pairs={{0,1},{1,0},{2,3},{3,2},{4,5},{5,4},{6,7},{7,6},{8,9},{9,8},{10,11... | collective-permute-start | bytes 392 | tf_op jit(solution)/shard_map/ppermute | solution.py:18
  8.5 13.1 %collective-permute-start.8 = (bf16[32,3328]{1,0:T(8,128)(2,1)S(1)}, bf16[32,3328]{1,0:T(8,128)(2,1)S(1)}, u32[]{:S(2)}, u32[]{:S(2)}) collective-permute-start(bf16[32,3328]{1,0:T(8,128)(2,1)S(1)} %slice.67), channel_id=1, source_target_pairs={{0,2},{1,3},{2,0},{3,1},{4,6},{5,7},{6,4},{7,5},{8,10},{9,11},{10,... | collective-permute-start | bytes 638984 | tf_op jit(solution)/shard_map/ppermute | solution.py:18
  11.3 9.2 %collective-permute-start.2 = (f32[32]{0:T(128)S(1)}, f32[32]{0:T(128)S(1)}, u32[]{:S(2)}, u32[]{:S(2)}) collective-permute-start(f32[32]{0:T(128)S(1)} %add.59), channel_id=1, source_target_pairs={{0,2},{1,3},{2,0},{3,1},{4,6},{5,7},{6,4},{7,5},{8,10},{9,11},{10,... | collective-permute-start | bytes 392 | tf_op jit(solution)/shard_map/ppermute | solution.py:18
  13.2 10.1 %collective-permute-start.5 = (bf16[32,2048]{1,0:T(8,128)(2,1)S(1)}, bf16[32,2048]{1,0:T(8,128)(2,1)S(1)}, u32[]{:S(2)}, u32[]{:S(2)}) collective-permute-start(bf16[32,2048]{1,0:T(8,128)(2,1)S(1)} %get-tuple-element.55), channel_id=1, source_target_pairs={{0,8},{4,12},{8,0},{12,4},{1,9},{5,13},{9,1},{13,5},{2,10},{6,14},... | collective-permute-start | bytes 393224 | tf_op jit(solution)/shard_map/ppermute | solution.py:18
  21.6 12.8 %collective-permute-start.3 = (bf16[32,3328]{1,0:T(8,128)(2,1)S(1)}, bf16[32,3328]{1,0:T(8,128)(2,1)S(1)}, u32[]{:S(2)}, u32[]{:S(2)}) collective-permute-start(bf16[32,3328]{1,0:T(8,128)(2,1)S(1)} %get-tuple-element.21), channel_id=1, source_target_pairs={{0,2},{1,3},{2,0},{3,1},{4,6},{5,7},{6,4},{7,5},{8,10},{9,11},{10,... | collective-permute-start | bytes 638984 | tf_op jit(solution)/shard_map/ppermute | solution.py:18
  22.5 12.0 %collective-permute-start.9 = (bf16[32,3328]{1,0:T(8,128)(2,1)S(1)}, bf16[32,3328]{1,0:T(8,128)(2,1)S(1)}, u32[]{:S(2)}, u32[]{:S(2)}) collective-permute-start(bf16[32,3328]{1,0:T(8,128)(2,1)S(1)} %get-tuple-element.46), channel_id=1, source_target_pairs={{0,8},{4,12},{8,0},{12,4},{1,9},{5,13},{9,1},{13,5},{2,10},{6,14},... | collective-permute-start | bytes 638984 | tf_op jit(solution)/shard_map/ppermute | solution.py:18
  23.3 14.6 %collective-permute-start.6 = (bf16[64,2048]{1,0:T(8,128)(2,1)S(1)}, bf16[64,2048]{1,0:T(8,128)(2,1)S(1)}, u32[]{:S(2)}, u32[]{:S(2)}) collective-permute-start(bf16[64,2048]{1,0:T(8,128)(2,1)S(1)} %pad_maximum_fusion.4), channel_id=1, source_target_pairs={{0,1},{1,0},{2,3},{3,2},{4,5},{5,4},{6,7},{7,6},{8,9},{9,8},{10,11... | collective-permute-start | bytes 786440 | tf_op jit(solution)/shard_map/ppermute | solution.py:18
  34.5 17.1 %collective-permute-start.4 = (bf16[32,4096]{1,0:T(8,128)(2,1)S(1)}, bf16[32,4096]{1,0:T(8,128)(2,1)S(1)}, u32[]{:S(2)}, u32[]{:S(2)}) collective-permute-start(bf16[32,4096]{1,0:T(8,128)(2,1)S(1)} %fusion.22), channel_id=1, source_target_pairs={{0,2},{1,3},{2,0},{3,1},{4,6},{5,7},{6,4},{7,5},{8,10},{9,11},{10,... | collective-permute-start | bytes 786440 | tf_op jit(solution)/shard_map/ppermute | solution.py:18
  34.5 18.3 %collective-permute-start.11 = (bf16[64,3328]{1,0:T(8,128)(2,1)S(1)}, bf16[64,3328]{1,0:T(8,128)(2,1)S(1)}, u32[]{:S(2)}, u32[]{:S(2)}) collective-permute-start(bf16[64,3328]{1,0:T(8,128)(2,1)S(1)} %pad_maximum_fusion.2), channel_id=1, source_target_pairs={{0,1},{1,0},{2,3},{3,2},{4,5},{5,4},{6,7},{7,6},{8,9},{9,8},{10,11... | collective-permute-start | bytes 1277960 | tf_op jit(solution)/shard_map/ppermute | solution.py:18
  36.4 6.6 %collective-permute-start.12 = (bf16[32,3328]{1,0:T(8,128)(2,1)S(1)}, bf16[32,3328]{1,0:T(8,128)(2,1)S(1)}, u32[]{:S(2)}, u32[]{:S(2)}) collective-permute-start(bf16[32,3328]{1,0:T(8,128)(2,1)S(1)} %get-tuple-element.52), channel_id=1, source_target_pairs={{0,8},{4,12},{8,0},{12,4},{1,9},{5,13},{9,1},{13,5},{2,10},{6,14},... | collective-permute-start | bytes 638984 | tf_op jit(solution)/shard_map/ppermute | solution.py:18
  38.1 5.3 %collective-permute-start.7 = (bf16[64,2048]{1,0:T(8,128)(2,1)S(1)}, bf16[64,2048]{1,0:T(8,128)(2,1)S(1)}, u32[]{:S(2)}, u32[]{:S(2)}) collective-permute-start(bf16[64,2048]{1,0:T(8,128)(2,1)S(1)} %get-tuple-element.49), channel_id=1, source_target_pairs={{0,4},{4,0},{8,12},{12,8},{1,5},{5,1},{9,13},{13,9},{2,6},{6,2},{1... | collective-permute-start | bytes 786440 | tf_op jit(solution)/shard_map/ppermute | solution.py:18
  43.0 22.6 %collective-permute-start.15 = (bf16[64,3328]{1,0:T(8,128)(2,1)S(1)}, bf16[64,3328]{1,0:T(8,128)(2,1)S(1)}, u32[]{:S(2)}, u32[]{:S(2)}) collective-permute-start(bf16[64,3328]{1,0:T(8,128)(2,1)S(1)} %pad_maximum_fusion.3), channel_id=1, source_target_pairs={{0,1},{1,0},{2,3},{3,2},{4,5},{5,4},{6,7},{7,6},{8,9},{9,8},{10,11... | collective-permute-start | bytes 1277960 | tf_op jit(solution)/shard_map/ppermute | solution.py:18
  52.9 1.8 %collective-permute-start.13 = (bf16[64,3328]{1,0:T(8,128)(2,1)S(1)}, bf16[64,3328]{1,0:T(8,128)(2,1)S(1)}, u32[]{:S(2)}, u32[]{:S(2)}) collective-permute-start(bf16[64,3328]{1,0:T(8,128)(2,1)S(1)} %get-tuple-element.44), channel_id=1, source_target_pairs={{0,4},{4,0},{8,12},{12,8},{1,5},{5,1},{9,13},{13,9},{2,6},{6,2},{1... | collective-permute-start | bytes 1277960 | tf_op jit(solution)/shard_map/ppermute | solution.py:18
  53.0 12.5 %collective-permute-start.10 = (bf16[32,4096]{1,0:T(8,128)(2,1)S(1)}, bf16[32,4096]{1,0:T(8,128)(2,1)S(1)}, u32[]{:S(2)}, u32[]{:S(2)}) collective-permute-start(bf16[32,4096]{1,0:T(8,128)(2,1)S(1)} %get-tuple-element.47), channel_id=1, source_target_pairs={{0,8},{4,12},{8,0},{12,4},{1,9},{5,13},{9,1},{13,5},{2,10},{6,14},... | collective-permute-start | bytes 786440 | tf_op jit(solution)/shard_map/ppermute | solution.py:18
  65.7 1.8 %collective-permute-start.16 = (bf16[64,3328]{1,0:T(8,128)(2,1)S(1)}, bf16[64,3328]{1,0:T(8,128)(2,1)S(1)}, u32[]{:S(2)}, u32[]{:S(2)}) collective-permute-start(bf16[64,3328]{1,0:T(8,128)(2,1)S(1)} %get-tuple-element.42), channel_id=1, source_target_pairs={{0,4},{4,0},{8,12},{12,8},{1,5},{5,1},{9,13},{13,9},{2,6},{6,2},{1... | collective-permute-start | bytes 1277960 | tf_op jit(solution)/shard_map/ppermute | solution.py:18
  65.9 14.3 %collective-permute-start.14 = (bf16[64,4096]{1,0:T(8,128)(2,1)S(1)}, bf16[64,4096]{1,0:T(8,128)(2,1)S(1)}, u32[]{:S(2)}, u32[]{:S(2)}) collective-permute-start(bf16[64,4096]{1,0:T(8,128)(2,1)S(1)} %constant_dynamic-update-slice_fusion), channel_id=1, source_target_pairs={{0,1},{1,0},{2,3},{3,2},{4,5},{5,4},{6,7},{7,6},{8,9},{9,8},{10,11... | collective-permute-start | bytes 1572872 | tf_op jit(solution)/shard_map/ppermute | solution.py:18
  78.5 2.0 %collective-permute-start.18 = (bf16[64,4096]{1,0:T(8,128)(2,1)S(1)}, bf16[64,4096]{1,0:T(8,128)(2,1)S(1)}, u32[]{:S(2)}, u32[]{:S(2)}) collective-permute-start(bf16[64,4096]{1,0:T(8,128)(2,1)S(1)} %slice.146), channel_id=1, source_target_pairs={{0,4},{4,0},{8,12},{12,8},{1,5},{5,1},{9,13},{13,9},{2,6},{6,2},{1... | collective-permute-start | bytes 1572872 | tf_op jit(solution)/shard_map/ppermute | solution.py:18
  80.3 2.0 %collective-permute-start.17 = (bf16[64,4096]{1,0:T(8,128)(2,1)S(1)}, bf16[64,4096]{1,0:T(8,128)(2,1)S(1)}, u32[]{:S(2)}, u32[]{:S(2)}) collective-permute-start(bf16[64,4096]{1,0:T(8,128)(2,1)S(1)} %get-tuple-element.40), channel_id=1, source_target_pairs={{0,4},{4,0},{8,12},{12,8},{1,5},{5,1},{9,13},{13,9},{2,6},{6,2},{1... | collective-permute-start | bytes 1572872 | tf_op jit(solution)/shard_map/ppermute | solution.py:18
  80.6 8.6 %collective-permute-start.21 = (bf16[32,4096]{1,0:T(8,128)(2,1)S(1)}, bf16[32,4096]{1,0:T(8,128)(2,1)S(1)}, u32[]{:S(2)}, u32[]{:S(2)}) collective-permute-start(bf16[32,4096]{1,0:T(8,128)(2,1)S(1)} %slice.147), channel_id=1, source_target_pairs={{0,8},{4,12},{8,0},{12,4},{1,9},{5,13},{9,1},{13,5},{2,10},{6,14},... | collective-permute-start | bytes 786440 | tf_op jit(solution)/shard_map/ppermute | solution.py:18
  87.0 2.3 %copy-start.1 = (bf16[32,4096]{1,0:T(8,128)(2,1)S(1)}, bf16[32,4096]{1,0:T(8,128)(2,1)}, u32[]{:S(2)}) copy-start(bf16[32,4096]{1,0:T(8,128)(2,1)} %param.8) | copy-start | bytes 786436
  87.5 7.3 %collective-permute-start.19 = (bf16[64,1280]{1,0:T(8,128)(2,1)S(1)}, bf16[64,1280]{1,0:T(8,128)(2,1)S(1)}, u32[]{:S(2)}, u32[]{:S(2)}) collective-permute-start(bf16[64,1280]{1,0:T(8,128)(2,1)S(1)} %fusion.31), channel_id=1, source_target_pairs={{0,4},{4,0},{8,12},{12,8},{1,5},{5,1},{9,13},{13,9},{2,6},{6,2},{1... | collective-permute-start | bytes 491528 | tf_op jit(solution)/shard_map/ppermute | solution.py:18
  94.7 1.8 %collective-permute-start.22 = (bf16[64,1024]{1,0:T(8,128)(2,1)S(1)}, bf16[64,1024]{1,0:T(8,128)(2,1)S(1)}, u32[]{:S(2)}, u32[]{:S(2)}) collective-permute-start(bf16[64,1024]{1,0:T(8,128)(2,1)S(1)} %slice.148), channel_id=1, source_target_pairs={{0,4},{4,0},{8,12},{12,8},{1,5},{5,1},{9,13},{13,9},{2,6},{6,2},{1... | collective-permute-start | bytes 393224 | tf_op jit(solution)/shard_map/ppermute | solution.py:18
  94.9 5.3 %collective-permute-start.20 = (bf16[32,1280]{1,0:T(8,128)(2,1)S(1)}, bf16[32,1280]{1,0:T(8,128)(2,1)S(1)}, u32[]{:S(2)}, u32[]{:S(2)}) collective-permute-start(bf16[32,1280]{1,0:T(8,128)(2,1)S(1)} %slice.149), channel_id=1, source_target_pairs={{0,8},{4,12},{8,0},{12,4},{1,9},{5,13},{9,1},{13,5},{2,10},{6,14},... | collective-permute-start | bytes 245768 | tf_op jit(solution)/shard_map/ppermute | solution.py:18
  96.5 4.7 %collective-permute-start.23 = (bf16[32,1024]{1,0:T(8,128)(2,1)S(1)}, bf16[32,1024]{1,0:T(8,128)(2,1)S(1)}, u32[]{:S(2)}, u32[]{:S(2)}) collective-permute-start(bf16[32,1024]{1,0:T(8,128)(2,1)S(1)} %slice.150), channel_id=1, source_target_pairs={{0,8},{4,12},{8,0},{12,4},{1,9},{5,13},{9,1},{13,5},{2,10},{6,14},... | collective-permute-start | bytes 196616 | tf_op jit(solution)/shard_map/ppermute | solution.py:18

commit v6 on v4

--- a/solution.py
+++ b/solution.py
@@ -109,9 +109,9 @@
             if i == 0:
                 columns = jnp.concatenate([columns, dot(normed, w_keyval)], axis=1)
                 normed = after(normed, columns, block_sum)
-            heads.append(sum_over_gx(columns, rows)[1].astype(jnp.bfloat16))
-        queries = jnp.concatenate([heads[0][:, :width], *heads[1:]], axis=1)
-        return (queries, heads[0][:, width:], (input_float + block_sum).astype(jnp.bfloat16))
+            heads.append(sum_over_gx(columns, rows)[1])
+        queries = jnp.concatenate([heads[0][:, :width], *heads[1:]], axis=1).astype(jnp.bfloat16)
+        return (queries, heads[0][:, width:].astype(jnp.bfloat16), (input_float + block_sum).astype(jnp.bfloat16))
 
     return jax.shard_map(
         local,

time: 102 us -> 102 us (level)
  no operation moved by 1% of the time
where the time goes in v6:
time: 102 us
  matrix products  39.6 us (39%)
  starting transfers between devices  29.3 us (29%)
  waiting for transfers between devices  24.2 us (24%)
  other arithmetic  5.37 us (5%)
  local copies, waits for them, and re-layouts  2.46 us (2%)
    dot_general x6, matrix products, dot(): return jnp.dot(left, right, preferred_element_type=jnp.float32)  39.6 us
    ppermute x24, starting transfers between devices, flip(): lax.ppermute(value, axis, [(i, i ^ bit) for i in range(lax.axis_size(axis...  29.3 us
    ppermute x24, waiting for transfers between devices, flip(): lax.ppermute(value, axis, [(i, i ^ bit) for i in range(lax.axis_size(axis...  24.2 us
  transfers between devices with their start and end apart: 24, of which 12 were waited for; matrix products, arithmetic and copies ran while one was open for 46% of the time, Pallas kernels for 0%

profile of v6, /device:TPU:0, one launch (start us, length us, event | category | flops | bytes accessed | tf_op | source)
XLA Modules:
  0.0 101.9 jit_solution(16027155587682702357)
XLA Ops:
  0.7 4.1 %collective-permute-start.1 = (bf16[32,2048]{1,0:T(8,128)(2,1)}, bf16[32,2048]{1,0:T(8,128)(2,1)S(1)}, u32[]{:S(2)}, u32[]{:S(2)}) collective-permute-start(bf16[32,2048]{1,0:T(8,128)(2,1)} %param.9), channel_id=1, source_target_pairs={{0,2},{1,3},{2,0},{3,1},{4,6},{5,7},{6,4},{7,5},{8,10},{9,11},{10,... | collective-permute-start | bytes 393224 | tf_op jit(solution)/shard_map/ppermute | solution.py:18
  4.8 1.1 %fusion.20 = f32[32]{0:T(128)S(1)} fusion(bf16[32,4096]{1,0:T(8,128)(2,1)} %param.8), kind=kLoop, calls=%fused_computation.27 | loop fusion | flops 393184 | bytes 262272 | tf_op jit(solution)/shard_map/reduce_sum | solution.py:64
  5.9 1.6 %collective-permute-start = (f32[32]{0:T(128)S(1)}, f32[32]{0:T(128)S(1)}, u32[]{:S(2)}, u32[]{:S(2)}) collective-permute-start(f32[32]{0:T(128)S(1)} %fusion.20), channel_id=1, source_target_pairs={{0,1},{1,0},{2,3},{3,2},{4,5},{5,4},{6,7},{7,6},{8,9},{9,8},{10,11... | collective-permute-start | bytes 392 | tf_op jit(solution)/shard_map/ppermute | solution.py:18
  7.5 0.9 slice.69
  8.5 0.4 collective-permute-start.8
  8.9 0.7 dynamic_slice.3
  9.6 1.7 %collective-permute-done.1 = bf16[32,2048]{1,0:T(8,128)(2,1)S(1)} collective-permute-done((bf16[32,2048]{1,0:T(8,128)(2,1)}, bf16[32,2048]{1,0:T(8,128)(2,1)S(1)}, u32[]{:S(2)}, u32[]{:S(2)}) %collective-permute-start.1) | collective-permute-done | bytes 131104 | tf_op jit(solution)/shard_map/ppermute | solution.py:18
  11.3 1.0 collective-permute-start.2
  12.2 0.9 broadcast_select_fusion.15
  13.2 5.2 %collective-permute-start.5 = (bf16[32,2048]{1,0:T(8,128)(2,1)S(1)}, bf16[32,2048]{1,0:T(8,128)(2,1)S(1)}, u32[]{:S(2)}, u32[]{:S(2)}) collective-permute-start(bf16[32,2048]{1,0:T(8,128)(2,1)S(1)} %get-tuple-element.59), channel_id=1, source_target_pairs={{0,8},{4,12},{8,0},{12,4},{1,9},{5,13},{9,1},{13,5},{2,10},{6,14},... | collective-permute-start | bytes 393224 | tf_op jit(solution)/shard_map/ppermute | solution.py:18
  18.4 2.1 %collective-permute-done.2 = f32[32]{0:T(128)S(1)} collective-permute-done((f32[32]{0:T(128)S(1)}, f32[32]{0:T(128)S(1)}, u32[]{:S(2)}, u32[]{:S(2)}) %collective-permute-start.2) | collective-permute-done | bytes 160 | tf_op jit(solution)/shard_map/ppermute | solution.py:18
  20.5 1.1 %fusion.22 = bf16[32,4096]{1,0:T(8,128)(2,1)S(1)} fusion(bf16[32,4096]{1,0:T(8,128)(2,1)} %param.8, f32[4096]{0:T(1024)S(1)} %dynamic_slice.3, f32[32]{0:T(128)S(1)} %add_rsqrt_fusion), kind=kLoop, calls=%fused_computation.29 | loop fusion | flops 524288 | bytes 540800 | tf_op jit(solution)/shard_map/convert_element_type | solution.py:68
  21.6 0.9 collective-permute-start.3
  22.5 0.8 collective-permute-start.9
  23.3 4.1 %collective-permute-start.6 = (bf16[64,2048]{1,0:T(8,128)(2,1)S(1)}, bf16[64,2048]{1,0:T(8,128)(2,1)S(1)}, u32[]{:S(2)}, u32[]{:S(2)}) collective-permute-start(bf16[64,2048]{1,0:T(8,128)(2,1)S(1)} %pad_maximum_fusion.4), channel_id=1, source_target_pairs={{0,1},{1,0},{2,3},{3,2},{4,5},{5,4},{6,7},{7,6},{8,9},{9,8},{10,11... | collective-permute-start | bytes 786440 | tf_op jit(solution)/shard_map/ppermute | solution.py:18
  27.4 7.1 %collective-permute-done.3 = bf16[32,3328]{1,0:T(8,128)(2,1)S(1)} collective-permute-done((bf16[32,3328]{1,0:T(8,128)(2,1)S(1)}, bf16[32,3328]{1,0:T(8,128)(2,1)S(1)}, u32[]{:S(2)}, u32[]{:S(2)}) %collective-permute-start.3) | collective-permute-done | bytes 213024 | tf_op jit(solution)/shard_map/ppermute | solution.py:18
  34.5 1.8 %collective-permute-start.11 = (bf16[64,3328]{1,0:T(8,128)(2,1)S(1)}, bf16[64,3328]{1,0:T(8,128)(2,1)S(1)}, u32[]{:S(2)}, u32[]{:S(2)}) collective-permute-start(bf16[64,3328]{1,0:T(8,128)(2,1)S(1)} %pad_maximum_fusion.2), channel_id=1, source_target_pairs={{0,1},{1,0},{2,3},{3,2},{4,5},{5,4},{6,7},{7,6},{8,9},{9,8},{10,11... | collective-permute-start | bytes 1277960 | tf_op jit(solution)/shard_map/ppermute | solution.py:18
  36.4 1.6 %collective-permute-start.12 = (bf16[32,3328]{1,0:T(8,128)(2,1)S(1)}, bf16[32,3328]{1,0:T(8,128)(2,1)S(1)}, u32[]{:S(2)}, u32[]{:S(2)}) collective-permute-start(bf16[32,3328]{1,0:T(8,128)(2,1)S(1)} %get-tuple-element.56), channel_id=1, source_target_pairs={{0,8},{4,12},{8,0},{12,4},{1,9},{5,13},{9,1},{13,5},{2,10},{6,14},... | collective-permute-start | bytes 638984 | tf_op jit(solution)/shard_map/ppermute | solution.py:18
  38.0 0.1 broadcast_select_fusion.6
  38.1 4.9 %collective-permute-done.12 = bf16[32,3328]{1,0:T(8,128)(2,1)S(1)} collective-permute-done((bf16[32,3328]{1,0:T(8,128)(2,1)S(1)}, bf16[32,3328]{1,0:T(8,128)(2,1)S(1)}, u32[]{:S(2)}, u32[]{:S(2)}) %collective-permute-start.12) | collective-permute-done | bytes 213024 | tf_op jit(solution)/shard_map/ppermute | solution.py:18
  43.0 0.4 collective-permute-start.15
  43.4 8.1 %fusion.24 = f32[128,4096]{1,0:T(8,128)S(1)} fusion(bf16[2048,4096]{1,0:T(8,128)(2,1)} %param.14, bf16[64,2048]{1,0:T(8,128)(2,1)S(1)} %collective-permute-done.7, bf16[64,2048]{1,0:T(8,128)(2,1)S(1)} %get-tuple-element.25), kind=kOutput, calls=%fused_computation.33 | convolution fusion | flops 2148532224 | bytes 19398656 | tf_op jit(solution)/shard_map/dot_general | solution.py:14
  51.5 1.3 %collective-permute-done.11 = bf16[64,3328]{1,0:T(8,128)(2,1)S(1)} collective-permute-done((bf16[64,3328]{1,0:T(8,128)(2,1)S(1)}, bf16[64,3328]{1,0:T(8,128)(2,1)S(1)}, u32[]{:S(2)}, u32[]{:S(2)}) %collective-permute-start.11) | collective-permute-done | bytes 426016 | tf_op jit(solution)/shard_map/ppermute | solution.py:18
  53.0 1.6 %collective-permute-start.10 = (bf16[32,4096]{1,0:T(8,128)(2,1)S(1)}, bf16[32,4096]{1,0:T(8,128)(2,1)S(1)}, u32[]{:S(2)}, u32[]{:S(2)}) collective-permute-start(bf16[32,4096]{1,0:T(8,128)(2,1)S(1)} %get-tuple-element.51), channel_id=1, source_target_pairs={{0,8},{4,12},{8,0},{12,4},{1,9},{5,13},{9,1},{13,5},{2,10},{6,14},... | collective-permute-start | bytes 786440 | tf_op jit(solution)/shard_map/ppermute | solution.py:18
  54.6 0.1 collective-permute-done.13
  54.7 10.8 %fusion.8 = f32[128,4096]{1,0:T(8,128)S(1)} fusion(f32[128,4096]{1,0:T(8,128)S(1)} %fusion.24, bf16[6656,4096]{1,0:T(8,128)(2,1)} %param.15, bf16[64,3328]{1,0:T(8,128)(2,1)S(1)} %collective-permute-done.13, bf16[64,3328]{1,0:T(8,128)(2,1)S(1)} %get-tuple-element.31), kind=kOutput, calls=%fused_computation.8 | convolution fusion | flops 3491889152 | bytes 32309248 | tf_op jit(solution)/shard_map/dot_general | solution.py:14
  65.7 0.2 collective-permute-start.16
  65.9 0.5 collective-permute-start.14
  66.5 1.1 %collective-permute-done.16 = bf16[64,3328]{1,0:T(8,128)(2,1)S(1)} collective-permute-done((bf16[64,3328]{1,0:T(8,128)(2,1)S(1)}, bf16[64,3328]{1,0:T(8,128)(2,1)S(1)}, u32[]{:S(2)}, u32[]{:S(2)}) %collective-permute-start.16) | collective-permute-done | bytes 426016 | tf_op jit(solution)/shard_map/ppermute | solution.py:18
  67.5 10.9 %fusion.11 = f32[128,4096]{1,0:T(8,128)S(1)} fusion(f32[128,4096]{1,0:T(8,128)S(1)} %fusion.8, bf16[6656,4096]{1,0:T(8,128)(2,1)} %param.15, bf16[64,3328]{1,0:T(8,128)(2,1)S(1)} %collective-permute-done.16, bf16[64,3328]{1,0:T(8,128)(2,1)S(1)} %get-tuple-element.45), kind=kOutput, calls=%fused_computation.9 | convolution fusion | flops 3491889152 | bytes 32309248 | tf_op jit(solution)/shard_map/dot_general | solution.py:14
  78.5 0.2 collective-permute-start.18
  78.7 1.5 %collective-permute-done.14 = bf16[64,4096]{1,0:T(8,128)(2,1)S(1)} collective-permute-done((bf16[64,4096]{1,0:T(8,128)(2,1)S(1)}, bf16[64,4096]{1,0:T(8,128)(2,1)S(1)}, u32[]{:S(2)}, u32[]{:S(2)}) %collective-permute-start.14) | collective-permute-done | bytes 524320 | tf_op jit(solution)/shard_map/ppermute | solution.py:18
  80.3 0.1 collective-permute-done.18
  80.5 0.1 slice_add_fusion
  80.6 1.6 %collective-permute-start.21 = (bf16[32,4096]{1,0:T(8,128)(2,1)S(1)}, bf16[32,4096]{1,0:T(8,128)(2,1)S(1)}, u32[]{:S(2)}, u32[]{:S(2)}) collective-permute-start(bf16[32,4096]{1,0:T(8,128)(2,1)S(1)} %slice.149), channel_id=1, source_target_pairs={{0,8},{4,12},{8,0},{12,4},{1,9},{5,13},{9,1},{13,5},{2,10},{6,14},... | collective-permute-start | bytes 786440 | tf_op jit(solution)/shard_map/ppermute | solution.py:18
  82.2 0.1 pad_maximum_fusion.1
  82.3 4.6 %fusion.6 = f32[128,1024]{1,0:T(8,128)S(1)} fusion(bf16[128,4096]{1,0:T(8,128)(2,1)S(1)} %pad_maximum_fusion.1, bf16[4096,2048]{1,0:T(8,128)(2,1)} %param.12), kind=kOutput, calls=%fused_computation.6 | convolution fusion | flops 1073741824 | bytes 9961472 | tf_op jit(solution)/shard_map/dot_general | solution.py:14
  87.0 0.4 fusion.37
  87.5 0.2 collective-permute-start.19
  87.7 1.6 %collective-permute-done.21 = bf16[32,4096]{1,0:T(8,128)(2,1)S(1)} collective-permute-done((bf16[32,4096]{1,0:T(8,128)(2,1)S(1)}, bf16[32,4096]{1,0:T(8,128)(2,1)S(1)}, u32[]{:S(2)}, u32[]{:S(2)}) %collective-permute-start.21) | collective-permute-done | bytes 262176 | tf_op jit(solution)/shard_map/ppermute | solution.py:18
  89.3 0.8 fusion.23
  90.1 4.6 %fusion.4 = f32[128,1024]{1,0:T(8,128)S(1)} fusion(bf16[128,4096]{1,0:T(8,128)(2,1)S(1)} %pad_maximum_fusion.1, bf16[4096,2048]{1,0:T(8,128)(2,1)} %param.12), kind=kOutput, calls=%fused_computation.4 | convolution fusion | flops 1073741824 | bytes 9961472 | tf_op jit(solution)/shard_map/dot_general | solution.py:14
  94.9 1.6 %collective-permute-start.20 = (bf16[32,1280]{1,0:T(8,128)(2,1)S(1)}, bf16[32,1280]{1,0:T(8,128)(2,1)S(1)}, u32[]{:S(2)}, u32[]{:S(2)}) collective-permute-start(bf16[32,1280]{1,0:T(8,128)(2,1)S(1)} %slice.151), channel_id=1, source_target_pairs={{0,8},{4,12},{8,0},{12,4},{1,9},{5,13},{9,1},{13,5},{2,10},{6,14},... | collective-permute-start | bytes 245768 | tf_op jit(solution)/shard_map/ppermute | solution.py:18
  96.5 1.3 %collective-permute-start.23 = (bf16[32,1024]{1,0:T(8,128)(2,1)S(1)}, bf16[32,1024]{1,0:T(8,128)(2,1)S(1)}, u32[]{:S(2)}, u32[]{:S(2)}) collective-permute-start(bf16[32,1024]{1,0:T(8,128)(2,1)S(1)} %slice.152), channel_id=1, source_target_pairs={{0,8},{4,12},{8,0},{12,4},{1,9},{5,13},{9,1},{13,5},{2,10},{6,14},... | collective-permute-start | bytes 196616 | tf_op jit(solution)/shard_map/ppermute | solution.py:18
  97.8 2.4 %collective-permute-done.20 = bf16[32,1280]{1,0:T(8,128)(2,1)S(1)} collective-permute-done((bf16[32,1280]{1,0:T(8,128)(2,1)S(1)}, bf16[32,1280]{1,0:T(8,128)(2,1)S(1)}, u32[]{:S(2)}, u32[]{:S(2)}) %collective-permute-start.20) | collective-permute-done | bytes 81952 | tf_op jit(solution)/shard_map/ppermute | solution.py:18
  100.2 0.6 slice.103
  100.8 0.4 collective-permute-done.23
  101.2 0.7 pad_maximum_fusion.5
  (47 shorter events, 1.0 us)
Async XLA Ops:
  0.6 86.4 %copy-start = (bf16[4096,256]{1,0:T(8,128)(2,1)S(1)}, bf16[4096,256]{1,0:T(8,128)(2,1)}, u32[]{:S(2)}) copy-start(bf16[4096,256]{1,0:T(8,128)(2,1)} %param.13) | copy-start | bytes 6291460
  0.6 20.9 %copy-start.2 = (bf16[32,6656]{1,0:T(8,128)(2,1)S(1)}, bf16[32,6656]{1,0:T(8,128)(2,1)}, u32[]{:S(2)}) copy-start(bf16[32,6656]{1,0:T(8,128)(2,1)} %param.10) | copy-start | bytes 1277956
  0.7 10.6 %collective-permute-start.1 = (bf16[32,2048]{1,0:T(8,128)(2,1)}, bf16[32,2048]{1,0:T(8,128)(2,1)S(1)}, u32[]{:S(2)}, u32[]{:S(2)}) collective-permute-start(bf16[32,2048]{1,0:T(8,128)(2,1)} %param.9), channel_id=1, source_target_pairs={{0,2},{1,3},{2,0},{3,1},{4,6},{5,7},{6,4},{7,5},{8,10},{9,11},{10,... | collective-permute-start | bytes 393224 | tf_op jit(solution)/shard_map/ppermute | solution.py:18
  5.9 3.7 %collective-permute-start = (f32[32]{0:T(128)S(1)}, f32[32]{0:T(128)S(1)}, u32[]{:S(2)}, u32[]{:S(2)}) collective-permute-start(f32[32]{0:T(128)S(1)} %fusion.20), channel_id=1, source_target_pairs={{0,1},{1,0},{2,3},{3,2},{4,5},{5,4},{6,7},{7,6},{8,9},{9,8},{10,11... | collective-permute-start | bytes 392 | tf_op jit(solution)/shard_map/ppermute | solution.py:18
  8.5 13.1 %collective-permute-start.8 = (bf16[32,3328]{1,0:T(8,128)(2,1)S(1)}, bf16[32,3328]{1,0:T(8,128)(2,1)S(1)}, u32[]{:S(2)}, u32[]{:S(2)}) collective-permute-start(bf16[32,3328]{1,0:T(8,128)(2,1)S(1)} %slice.69), channel_id=1, source_target_pairs={{0,2},{1,3},{2,0},{3,1},{4,6},{5,7},{6,4},{7,5},{8,10},{9,11},{10,... | collective-permute-start | bytes 638984 | tf_op jit(solution)/shard_map/ppermute | solution.py:18
  11.3 9.2 %collective-permute-start.2 = (f32[32]{0:T(128)S(1)}, f32[32]{0:T(128)S(1)}, u32[]{:S(2)}, u32[]{:S(2)}) collective-permute-start(f32[32]{0:T(128)S(1)} %add.59), channel_id=1, source_target_pairs={{0,2},{1,3},{2,0},{3,1},{4,6},{5,7},{6,4},{7,5},{8,10},{9,11},{10,... | collective-permute-start | bytes 392 | tf_op jit(solution)/shard_map/ppermute | solution.py:18
  13.2 10.1 %collective-permute-start.5 = (bf16[32,2048]{1,0:T(8,128)(2,1)S(1)}, bf16[32,2048]{1,0:T(8,128)(2,1)S(1)}, u32[]{:S(2)}, u32[]{:S(2)}) collective-permute-start(bf16[32,2048]{1,0:T(8,128)(2,1)S(1)} %get-tuple-element.59), channel_id=1, source_target_pairs={{0,8},{4,12},{8,0},{12,4},{1,9},{5,13},{9,1},{13,5},{2,10},{6,14},... | collective-permute-start | bytes 393224 | tf_op jit(solution)/shard_map/ppermute | solution.py:18
  21.6 12.8 %collective-permute-start.3 = (bf16[32,3328]{1,0:T(8,128)(2,1)S(1)}, bf16[32,3328]{1,0:T(8,128)(2,1)S(1)}, u32[]{:S(2)}, u32[]{:S(2)}) collective-permute-start(bf16[32,3328]{1,0:T(8,128)(2,1)S(1)} %get-tuple-element.23), channel_id=1, source_target_pairs={{0,2},{1,3},{2,0},{3,1},{4,6},{5,7},{6,4},{7,5},{8,10},{9,11},{10,... | collective-permute-start | bytes 638984 | tf_op jit(solution)/shard_map/ppermute | solution.py:18
  22.5 12.0 %collective-permute-start.9 = (bf16[32,3328]{1,0:T(8,128)(2,1)S(1)}, bf16[32,3328]{1,0:T(8,128)(2,1)S(1)}, u32[]{:S(2)}, u32[]{:S(2)}) collective-permute-start(bf16[32,3328]{1,0:T(8,128)(2,1)S(1)} %get-tuple-element.50), channel_id=1, source_target_pairs={{0,8},{4,12},{8,0},{12,4},{1,9},{5,13},{9,1},{13,5},{2,10},{6,14},... | collective-permute-start | bytes 638984 | tf_op jit(solution)/shard_map/ppermute | solution.py:18
  23.3 14.6 %collective-permute-start.6 = (bf16[64,2048]{1,0:T(8,128)(2,1)S(1)}, bf16[64,2048]{1,0:T(8,128)(2,1)S(1)}, u32[]{:S(2)}, u32[]{:S(2)}) collective-permute-start(bf16[64,2048]{1,0:T(8,128)(2,1)S(1)} %pad_maximum_fusion.4), channel_id=1, source_target_pairs={{0,1},{1,0},{2,3},{3,2},{4,5},{5,4},{6,7},{7,6},{8,9},{9,8},{10,11... | collective-permute-start | bytes 786440 | tf_op jit(solution)/shard_map/ppermute | solution.py:18
  34.5 17.1 %collective-permute-start.4 = (bf16[32,4096]{1,0:T(8,128)(2,1)S(1)}, bf16[32,4096]{1,0:T(8,128)(2,1)S(1)}, u32[]{:S(2)}, u32[]{:S(2)}) collective-permute-start(bf16[32,4096]{1,0:T(8,128)(2,1)S(1)} %fusion.22), channel_id=1, source_target_pairs={{0,2},{1,3},{2,0},{3,1},{4,6},{5,7},{6,4},{7,5},{8,10},{9,11},{10,... | collective-permute-start | bytes 786440 | tf_op jit(solution)/shard_map/ppermute | solution.py:18
  34.5 18.3 %collective-permute-start.11 = (bf16[64,3328]{1,0:T(8,128)(2,1)S(1)}, bf16[64,3328]{1,0:T(8,128)(2,1)S(1)}, u32[]{:S(2)}, u32[]{:S(2)}) collective-permute-start(bf16[64,3328]{1,0:T(8,128)(2,1)S(1)} %pad_maximum_fusion.2), channel_id=1, source_target_pairs={{0,1},{1,0},{2,3},{3,2},{4,5},{5,4},{6,7},{7,6},{8,9},{9,8},{10,11... | collective-permute-start | bytes 1277960 | tf_op jit(solution)/shard_map/ppermute | solution.py:18
  36.4 6.6 %collective-permute-start.12 = (bf16[32,3328]{1,0:T(8,128)(2,1)S(1)}, bf16[32,3328]{1,0:T(8,128)(2,1)S(1)}, u32[]{:S(2)}, u32[]{:S(2)}) collective-permute-start(bf16[32,3328]{1,0:T(8,128)(2,1)S(1)} %get-tuple-element.56), channel_id=1, source_target_pairs={{0,8},{4,12},{8,0},{12,4},{1,9},{5,13},{9,1},{13,5},{2,10},{6,14},... | collective-permute-start | bytes 638984 | tf_op jit(solution)/shard_map/ppermute | solution.py:18
  38.1 5.3 %collective-permute-start.7 = (bf16[64,2048]{1,0:T(8,128)(2,1)S(1)}, bf16[64,2048]{1,0:T(8,128)(2,1)S(1)}, u32[]{:S(2)}, u32[]{:S(2)}) collective-permute-start(bf16[64,2048]{1,0:T(8,128)(2,1)S(1)} %get-tuple-element.53), channel_id=1, source_target_pairs={{0,4},{4,0},{8,12},{12,8},{1,5},{5,1},{9,13},{13,9},{2,6},{6,2},{1... | collective-permute-start | bytes 786440 | tf_op jit(solution)/shard_map/ppermute | solution.py:18
  43.0 22.6 %collective-permute-start.15 = (bf16[64,3328]{1,0:T(8,128)(2,1)S(1)}, bf16[64,3328]{1,0:T(8,128)(2,1)S(1)}, u32[]{:S(2)}, u32[]{:S(2)}) collective-permute-start(bf16[64,3328]{1,0:T(8,128)(2,1)S(1)} %pad_maximum_fusion.3), channel_id=1, source_target_pairs={{0,1},{1,0},{2,3},{3,2},{4,5},{5,4},{6,7},{7,6},{8,9},{9,8},{10,11... | collective-permute-start | bytes 1277960 | tf_op jit(solution)/shard_map/ppermute | solution.py:18
  52.9 1.8 %collective-permute-start.13 = (bf16[64,3328]{1,0:T(8,128)(2,1)S(1)}, bf16[64,3328]{1,0:T(8,128)(2,1)S(1)}, u32[]{:S(2)}, u32[]{:S(2)}) collective-permute-start(bf16[64,3328]{1,0:T(8,128)(2,1)S(1)} %get-tuple-element.47), channel_id=1, source_target_pairs={{0,4},{4,0},{8,12},{12,8},{1,5},{5,1},{9,13},{13,9},{2,6},{6,2},{1... | collective-permute-start | bytes 1277960 | tf_op jit(solution)/shard_map/ppermute | solution.py:18
  53.0 12.5 %collective-permute-start.10 = (bf16[32,4096]{1,0:T(8,128)(2,1)S(1)}, bf16[32,4096]{1,0:T(8,128)(2,1)S(1)}, u32[]{:S(2)}, u32[]{:S(2)}) collective-permute-start(bf16[32,4096]{1,0:T(8,128)(2,1)S(1)} %get-tuple-element.51), channel_id=1, source_target_pairs={{0,8},{4,12},{8,0},{12,4},{1,9},{5,13},{9,1},{13,5},{2,10},{6,14},... | collective-permute-start | bytes 786440 | tf_op jit(solution)/shard_map/ppermute | solution.py:18
  65.7 1.8 %collective-permute-start.16 = (bf16[64,3328]{1,0:T(8,128)(2,1)S(1)}, bf16[64,3328]{1,0:T(8,128)(2,1)S(1)}, u32[]{:S(2)}, u32[]{:S(2)}) collective-permute-start(bf16[64,3328]{1,0:T(8,128)(2,1)S(1)} %get-tuple-element.46), channel_id=1, source_target_pairs={{0,4},{4,0},{8,12},{12,8},{1,5},{5,1},{9,13},{13,9},{2,6},{6,2},{1... | collective-permute-start | bytes 1277960 | tf_op jit(solution)/shard_map/ppermute | solution.py:18
  65.9 14.3 %collective-permute-start.14 = (bf16[64,4096]{1,0:T(8,128)(2,1)S(1)}, bf16[64,4096]{1,0:T(8,128)(2,1)S(1)}, u32[]{:S(2)}, u32[]{:S(2)}) collective-permute-start(bf16[64,4096]{1,0:T(8,128)(2,1)S(1)} %constant_dynamic-update-slice_fusion), channel_id=1, source_target_pairs={{0,1},{1,0},{2,3},{3,2},{4,5},{5,4},{6,7},{7,6},{8,9},{9,8},{10,11... | collective-permute-start | bytes 1572872 | tf_op jit(solution)/shard_map/ppermute | solution.py:18
  78.5 2.0 %collective-permute-start.18 = (bf16[64,4096]{1,0:T(8,128)(2,1)S(1)}, bf16[64,4096]{1,0:T(8,128)(2,1)S(1)}, u32[]{:S(2)}, u32[]{:S(2)}) collective-permute-start(bf16[64,4096]{1,0:T(8,128)(2,1)S(1)} %slice.148), channel_id=1, source_target_pairs={{0,4},{4,0},{8,12},{12,8},{1,5},{5,1},{9,13},{13,9},{2,6},{6,2},{1... | collective-permute-start | bytes 1572872 | tf_op jit(solution)/shard_map/ppermute | solution.py:18
  80.3 2.0 %collective-permute-start.17 = (bf16[64,4096]{1,0:T(8,128)(2,1)S(1)}, bf16[64,4096]{1,0:T(8,128)(2,1)S(1)}, u32[]{:S(2)}, u32[]{:S(2)}) collective-permute-start(bf16[64,4096]{1,0:T(8,128)(2,1)S(1)} %get-tuple-element.44), channel_id=1, source_target_pairs={{0,4},{4,0},{8,12},{12,8},{1,5},{5,1},{9,13},{13,9},{2,6},{6,2},{1... | collective-permute-start | bytes 1572872 | tf_op jit(solution)/shard_map/ppermute | solution.py:18
  80.6 8.6 %collective-permute-start.21 = (bf16[32,4096]{1,0:T(8,128)(2,1)S(1)}, bf16[32,4096]{1,0:T(8,128)(2,1)S(1)}, u32[]{:S(2)}, u32[]{:S(2)}) collective-permute-start(bf16[32,4096]{1,0:T(8,128)(2,1)S(1)} %slice.149), channel_id=1, source_target_pairs={{0,8},{4,12},{8,0},{12,4},{1,9},{5,13},{9,1},{13,5},{2,10},{6,14},... | collective-permute-start | bytes 786440 | tf_op jit(solution)/shard_map/ppermute | solution.py:18
  87.0 2.3 %copy-start.1 = (bf16[32,4096]{1,0:T(8,128)(2,1)S(1)}, bf16[32,4096]{1,0:T(8,128)(2,1)}, u32[]{:S(2)}) copy-start(bf16[32,4096]{1,0:T(8,128)(2,1)} %param.8) | copy-start | bytes 786436
  87.5 7.3 %collective-permute-start.19 = (bf16[64,1280]{1,0:T(8,128)(2,1)S(1)}, bf16[64,1280]{1,0:T(8,128)(2,1)S(1)}, u32[]{:S(2)}, u32[]{:S(2)}) collective-permute-start(bf16[64,1280]{1,0:T(8,128)(2,1)S(1)} %fusion.31), channel_id=1, source_target_pairs={{0,4},{4,0},{8,12},{12,8},{1,5},{5,1},{9,13},{13,9},{2,6},{6,2},{1... | collective-permute-start | bytes 491528 | tf_op jit(solution)/shard_map/ppermute | solution.py:18
  94.7 1.8 %collective-permute-start.22 = (bf16[64,1024]{1,0:T(8,128)(2,1)S(1)}, bf16[64,1024]{1,0:T(8,128)(2,1)S(1)}, u32[]{:S(2)}, u32[]{:S(2)}) collective-permute-start(bf16[64,1024]{1,0:T(8,128)(2,1)S(1)} %slice.150), channel_id=1, source_target_pairs={{0,4},{4,0},{8,12},{12,8},{1,5},{5,1},{9,13},{13,9},{2,6},{6,2},{1... | collective-permute-start | bytes 393224 | tf_op jit(solution)/shard_map/ppermute | solution.py:18
  94.9 5.3 %collective-permute-start.20 = (bf16[32,1280]{1,0:T(8,128)(2,1)S(1)}, bf16[32,1280]{1,0:T(8,128)(2,1)S(1)}, u32[]{:S(2)}, u32[]{:S(2)}) collective-permute-start(bf16[32,1280]{1,0:T(8,128)(2,1)S(1)} %slice.151), channel_id=1, source_target_pairs={{0,8},{4,12},{8,0},{12,4},{1,9},{5,13},{9,1},{13,5},{2,10},{6,14},... | collective-permute-start | bytes 245768 | tf_op jit(solution)/shard_map/ppermute | solution.py:18
  96.5 4.7 %collective-permute-start.23 = (bf16[32,1024]{1,0:T(8,128)(2,1)S(1)}, bf16[32,1024]{1,0:T(8,128)(2,1)S(1)}, u32[]{:S(2)}, u32[]{:S(2)}) collective-permute-start(bf16[32,1024]{1,0:T(8,128)(2,1)S(1)} %slice.152), channel_id=1, source_target_pairs={{0,8},{4,12},{8,0},{12,4},{1,9},{5,13},{9,1},{13,5},{2,10},{6,14},... | collective-permute-start | bytes 196616 | tf_op jit(solution)/shard_map/ppermute | solution.py:18
